TPU v7x, 512 devices: a whole 4x4x16 slice. The times are simulated.
512 devices in a mesh: dp: 32 (over z, core), shard: 16 (over x, y).
Axes of the slice: x: 4, y: 4, z: 16, core: 2. Of those that a mesh axis runs over, the one named last changes fastest.
Arguments:
- activations: bfloat16 [5120, 64, 640], P(('dp', 'shard')), may hold values from -40 to 40
- cotangent: bfloat16 [3584, 64, 640], P(('dp', 'shard')), may hold values from -24 to 24
- window_len: int32 [32, 16, 10], P(None, 'shard'), may hold values from 0 to 64, as said below
- move_dest: int32 [32, 16, 10], P(None, 'shard'), may hold values from 0 to 31, as said below
- move_slot: int32 [32, 16, 10], P(None, 'shard'), may hold values from -1 to 6, as said below
- w_qkv: bfloat16 [640, 1920], P('shard'), may hold values from -0.25 to 0.25
- b_qkv: bfloat16 [1920], P('shard'), may hold values from -3 to 3
- norm_gain: bfloat16 [640], P('shard'), may hold values from 0.25 to 1.75
- w_out: bfloat16 [640, 640], P(None, 'shard'), may hold values from -0.25 to 0.25
Outputs:
- balanced_out: bfloat16 [3584, 64, 640], P(('dp', 'shard'))
- grad_input: bfloat16 [5120, 64, 640], P(('dp', 'shard'))
- grad_w_out: float32 [640, 640], P(None, 'shard')
Inputs may be any that keep to these rules, and one draw needn't show every extreme that they name: `window_len`: 0 marks an empty slot. Every device holds 1 to 10 windows, at least one of 64 patches. `move_dest`: A window stays on its device or moves to one of the next 3 dp indices, wrapping; empty slots name their own index. A device sends at most one window to each other device and receives at most one; after the moves no device holds more than 7 windows, and some device holds 7. `move_slot`: -1 for empty slots; the windows that one device holds after the moves have distinct slots.
All inputs are finite; a program needn't handle non-finite values.
Results may differ from a plain program's by a relative error of at most 0.012.
Values may be sent and summed in bfloat16 or wider, within the bound.
No kernel may reach another device: no remote copies, remote signals or barrier semaphores. Data moves between devices by JAX's collectives and lax.ppermute only.
A program may use at most 64 MiB of HBM per device.

v0:
```python
import jax
import jax.numpy as jnp
from jax import lax
from jax.sharding import PartitionSpec as P

HEADS = 8
MOVES = 3


norm_eps = 1e-06


def from_behind(array, axis, by):
    devices = lax.axis_size(axis)
    return lax.ppermute(array, axis, [(i, (i + by) % devices) for i in range(devices)])


def window_block(windows_in, lengths, w_qkv, b_qkv, norm_gain, w_out):
    num_windows, patches, channels = windows_in.shape
    inner_width = w_out.shape[0]
    head_size = inner_width // HEADS
    head_shape = (num_windows, patches, HEADS, head_size)
    values = windows_in.astype(jnp.float32)
    inv_rms = lax.rsqrt(jnp.mean(values * values, axis=-1, keepdims=True) + norm_eps)
    normed = (values * inv_rms * norm_gain.astype(jnp.float32)).astype(jnp.bfloat16)
    projected = jnp.einsum("wpd,de->wpe", normed, w_qkv, preferred_element_type=jnp.float32)
    projected = (projected + b_qkv.astype(jnp.float32)).astype(jnp.bfloat16)
    query_vecs = projected[..., :inner_width].reshape(head_shape)
    key_vecs = projected[..., inner_width : 2 * inner_width].reshape(head_shape)
    value_vecs = projected[..., 2 * inner_width :].reshape(head_shape)
    scores = jnp.einsum(
        "wqhe,wkhe->whqk", query_vecs, key_vecs, preferred_element_type=jnp.float32
    ) * head_size ** (-0.5)
    position = jnp.arange(patches)
    allowed = position[None, :] < jnp.maximum(lengths, 1)[:, None]
    weights = jnp.where(allowed[:, None, None, :], jnp.exp(scores), 0.0)
    attn_probs = (weights / jnp.sum(weights, axis=-1, keepdims=True)).astype(jnp.bfloat16)
    attended = jnp.einsum(
        "whqk,wkhe->wqhe", attn_probs, value_vecs, preferred_element_type=jnp.float32
    )
    attended = attended.astype(jnp.bfloat16).reshape(num_windows, patches, inner_width)
    projected_out = jnp.einsum("wpi,id->wpd", attended, w_out, preferred_element_type=jnp.float32)
    row_mask = (position[None, :] < lengths[:, None]).astype(jnp.float32)[..., None]
    return (((values + projected_out) * row_mask).astype(jnp.bfloat16), attended)


def pick_row(table, index, axis):
    return lax.dynamic_index_in_dim(table, index, axis, keepdims=False)


def arrival_table(dest_table, slot_table, my_index, kept_slots):
    slot_ids = jnp.arange(kept_slots)
    matches = (dest_table == my_index) & (slot_table >= 0)
    return (matches[None] & (slot_table[None] == slot_ids[:, None, None])).astype(jnp.float32)


def outward(own_rows, arrivals, dest_table, my_index):
    count_dp = lax.axis_size("dp")
    mine_dest = pick_row(dest_table, my_index, 0)
    keep_map = pick_row(arrivals, my_index, 1).astype(jnp.bfloat16)
    placed = jnp.einsum("bs,spd->bpd", keep_map, own_rows, preferred_element_type=jnp.float32)
    for distance in range(1, MOVES + 1):
        target = (my_index + distance) % count_dp
        chosen = (mine_dest == target).astype(jnp.bfloat16)
        parcel = jnp.einsum(
            "s,spd->pd", chosen, own_rows, preferred_element_type=jnp.float32
        ).astype(jnp.bfloat16)
        arrived = from_behind(parcel, "dp", distance)
        source = (my_index - distance) % count_dp
        landing = jnp.sum(pick_row(arrivals, source, 1), axis=1)
        placed = placed + landing[:, None, None] * arrived.astype(jnp.float32)[None]
    return placed.astype(jnp.bfloat16)


def inward(held_rows, arrivals, dest_table, my_index):
    count_dp = lax.axis_size("dp")
    mine_dest = pick_row(dest_table, my_index, 0)
    keep_map = pick_row(arrivals, my_index, 1).astype(jnp.bfloat16)
    own_rows = jnp.einsum("bs,bpd->spd", keep_map, held_rows, preferred_element_type=jnp.float32)
    for distance in range(1, MOVES + 1):
        source = (my_index - distance) % count_dp
        landing = jnp.sum(pick_row(arrivals, source, 1), axis=1).astype(jnp.bfloat16)
        parcel = jnp.einsum(
            "b,bpd->pd", landing, held_rows, preferred_element_type=jnp.float32
        ).astype(jnp.bfloat16)
        arrived = from_behind(parcel, "dp", -distance)
        target = (my_index + distance) % count_dp
        chosen = (mine_dest == target).astype(jnp.float32)
        own_rows = own_rows + chosen[:, None, None] * arrived.astype(jnp.float32)[None]
    return own_rows.astype(jnp.bfloat16)


def shards(
    activations, cotangent, window_len, move_dest, move_slot, w_qkv, b_qkv, norm_gain, w_out
):
    my_index = lax.axis_index("dp")
    kept_slots = cotangent.shape[0]
    patches = activations.shape[1]
    dest_table = move_dest[:, 0, :]
    slot_table = move_slot[:, 0, :]
    len_table = window_len[:, 0, :]
    full_qkv, full_bias, full_gain, full_out = (
        lax.all_gather(w_qkv, "shard", axis=0, tiled=True),
        lax.all_gather(b_qkv, "shard", axis=0, tiled=True),
        lax.all_gather(norm_gain, "shard", axis=0, tiled=True),
        lax.all_gather(w_out, "shard", axis=1, tiled=True),
    )
    arrivals = arrival_table(dest_table, slot_table, my_index, kept_slots)

    def block_at(windows_in, lengths):
        return window_block(windows_in, lengths, full_qkv, full_bias, full_gain, full_out)

    lengths = pick_row(len_table, my_index, 0)
    result, backward, attended = jax.vjp(
        lambda windows_in: block_at(windows_in, lengths), activations, has_aux=True
    )
    balanced_out = outward(result, arrivals, dest_table, my_index)
    upstream = inward(cotangent, arrivals, dest_table, my_index)
    (grad_input,) = backward(upstream)
    row_mask = (jnp.arange(patches)[None, :] < lengths[:, None]).astype(jnp.bfloat16)[..., None]
    local_grad = jnp.einsum(
        "wpi,wpd->id", attended, upstream * row_mask, preferred_element_type=jnp.float32
    )
    shared = lax.psum_scatter(local_grad, "shard", scatter_dimension=1, tiled=True)
    grad_w_out = lax.psum(shared, "dp")
    return (balanced_out, grad_input, grad_w_out)


def solution(mesh):
    return jax.shard_map(
        shards,
        mesh=mesh,
        in_specs=(
            P(("dp", "shard"), None, None),
            P(("dp", "shard"), None, None),
            P(None, "shard", None),
            P(None, "shard", None),
            P(None, "shard", None),
            P("shard", None),
            P("shard"),
            P("shard"),
            P(None, "shard"),
        ),
        out_specs=(
            P(("dp", "shard"), None, None),
            P(("dp", "shard"), None, None),
            P(None, "shard"),
        ),
        check_vma=False,
    )
```

profile of v0, /device:TPU:1, one launch (start us, length us, event | category | flops | bytes accessed | tf_op | source)
XLA Modules:
  0.0 480.7 jit_solution(9375568457185918636)
XLA Ops:
  7.2 0.7 all-gather.2.cloned.1.call-update
  8.0 0.8 copy.77
  8.8 0.7 fusion.77
  10.3 12.5 %collective-permute-start.5 = (bf16[64,640]{1,0:T(8,128)(2,1)S(1)}, bf16[64,640]{1,0:T(8,128)(2,1)S(1)}, u32[]{:S(2)}, u32[]{:S(2)}) collective-permute-start(bf16[64,640]{1,0:T(8,128)(2,1)S(1)} %bitcast.96), channel_id=1, source_target_pairs={{0,464},{16,480},{32,496},{48,0},{64,16},{80,32},{96,48},{112,64},... | collective-permute-start | bytes 245768 | tf_op jit(solution)/shard_map/ppermute | solution.py:15
  23.3 0.6 copy.148
  24.0 2.6 collective-permute-start.4
  27.1 0.6 copy.149
  27.7 0.6 collective-permute-start.3
  28.9 0.6 iota_compare_fusion.2
  29.7 0.6 fusion.69
  30.4 22.8 %all_gather.15 = bf16[640,640]{0,1:T(8,128)(2,1)} all-gather(bf16[640,40]{0,1:T(8,128)(2,1)S(1)} %copy-done.14), channel_id=1, replica_groups=mesh['dp'=32,'shard'=16] {'shard'}, dimensions={1}, use_global_device_ids=true | all-gather | bytes 870400 | tf_op jit(solution)/shard_map/all_gather | solution.py:106
  53.2 0.6 fusion.99
  55.4 31.8 %all-reduce.6 = (bf16[1920]{0:T(1024)(128)(2,1)S(1)}, bf16[640]{0:T(1024)(128)(2,1)S(1)}) all-reduce(bf16[1920]{0:T(1024)(128)(2,1)S(1)} %dynamic-update-slice.1, bf16[640]{0:T(1024)(128)(2,1)S(1)} %dynamic-update-slice), channel_id=1, replica_groups=mesh['dp'=32,'shard'=16] {'shard'}, use_global_device_ids=true, to_apply=%add.4 | all-reduce | flops 2560 | bytes 10240
  87.2 0.6 convert_element_type.173
  87.8 0.7 compare_reduce_fusion.2
  89.1 0.6 convert_element_type.191
  89.6 0.5 convert_element_type.187
  90.9 0.9 convert_element_type.194
  91.8 0.9 convert_element_type.190
  92.7 1.4 fusion.25
  94.1 0.9 copy-done.2
  95.1 1.8 fusion.39
  96.9 3.2 reshape.185
  100.1 4.1 add_convert_fusion
  104.3 1.5 fusion.98
  105.8 3.2 reshape.181
  109.0 3.2 reshape.183
  112.2 3.2 reshape.182
  115.4 2.8 fusion.15
  118.2 1.0 fusion.37
  119.7 2.1 copy.55
  121.8 2.9 reshape.184
  124.7 2.7 fusion.21
  127.5 0.6 fusion.27
  128.1 0.6 fusion.29
  128.7 0.6 fusion.31
  129.8 1.5 fusion.5
  131.3 1.3 fusion.36
  132.6 2.3 fusion.35
  134.9 0.6 copy.150
  135.6 15.4 %collective-permute-start.2 = (bf16[64,640]{1,0:T(8,128)(2,1)}, bf16[64,640]{1,0:T(8,128)(2,1)}, u32[]{:S(2)}, u32[]{:S(2)}) collective-permute-start(bf16[64,640]{1,0:T(8,128)(2,1)} %bitcast.93), channel_id=1, source_target_pairs={{0,48},{16,64},{32,80},{48,96},{64,112},{80,128},{96,144},{112,160... | collective-permute-start | bytes 245768 | tf_op jit(solution)/shard_map/ppermute | solution.py:15
  150.9 0.6 copy.151
  151.6 1.9 collective-permute-start.1
  153.5 0.6 copy.152
  154.2 0.6 collective-permute-start
  154.7 2.1 copy.66
  156.8 2.9 reshape.188
  159.7 3.3 copy.63
  163.1 2.9 reshape.187
  166.0 3.6 convolution_bitcast_fusion
  170.2 3.0 fusion.38
  173.2 2.1 copy.60
  175.3 2.9 reshape.186
  178.2 5.0 %fusion.22 = (f32[10,64]{1,0:T(8,128)S(1)}, bf16[10,64,640]{2,1,0:T(8,128)(2,1)S(1)}) fusion(bf16[10,64,640]{2,1,0:T(8,128)(2,1)} %param.9, f32[640]{0:T(1024)S(1)} %convert_element_type.171, bf16[640,1920]{1,0:T(8,128)(2,1)} %all-gather.2.cloned.1.call-done, bf16[10,64,640]{2,1,0:T(8,128)(2,1)} %reshape.188, bf16[10,64,640]{2,1,0:T(8,128)(2,1)} %reshape.187, ...), kind=kOutput, calls=%fused_computation.33 | convolution fusion | flops 1582693760 | bytes 6558720 | tf_op jit(solution)/shard_map/transpose(jvp(wpd,de->wpe))/dot_general | solution.py:26
  183.3 2.0 fusion.16
  185.3 0.9 convert_element_type.185
  186.2 0.9 convert_element_type.183
  187.1 0.9 convert_element_type.181
  188.0 91.3 %all-reduce.12.cloned.1.call-done = f32[640,640]{0,1:T(8,128)} async-done(((f32[640,640]{0,1:T(8,128)}), f32[640,640]{0,1:T(8,128)}) %all-reduce.12.cloned.1.call-update) | async-done | bytes 1638416
  279.3 1.5 constant_dynamic-slice_fusion.1
  280.9 1.9 add_convert_fusion.1
  282.7 0.9 copy.67
  283.6 189.0 %all-reduce.10.cloned.1.call-done = f32[640,40]{0,1:T(8,128)} async-done(((f32[640,40]{0,1:T(8,128)}), f32[640,40]{0,1:T(8,128)}) %all-reduce.10.cloned.1.call-update) | async-done | bytes 102416 | tf_op jit(solution)/shard_map/psum | solution.py:125
  472.6 1.5 copy.157
  (115 shorter events, 5.4 us)
Async XLA Ops:
  7.2 2.7 copy-start
  7.2 92.9 %all-gather.2.cloned.1.call-start = ((), (), s32[]{:S(2)}) async-start(), calls=%async_computation | async-start | bytes 2611200 | tf_op jit(solution)/shard_map/all_gather | solution.py:103
  7.9 271.4 %all-reduce.12.cloned.1.call-start = ((), (), s32[]{:S(2)}) async-start(), calls=%async_computation.2 | async-start | bytes 3276800
  9.6 19.9 %copy-start.13 = (f32[7,32,10]{2,0,1:T(8,128)}, f32[7,32,10]{2,0,1:T(8,128)S(1)}, u32[]{:S(2)}) copy-start(f32[7,32,10]{2,0,1:T(8,128)S(1)} %fusion.73) | copy-start | bytes 26884
  9.7 18.6 %copy-start.18 = (s32[32,1,10]{0,1,2:T(1,128)S(1)}, s32[32,1,10]{0,1,2:T(1,128)}, u32[]{:S(2)}) copy-start(s32[32,1,10]{0,1,2:T(1,128)} %param.11) | copy-start | bytes 3844
  9.7 18.9 %copy-start.3 = (bf16[10,64,640]{2,1,0:T(8,128)(2,1)S(1)}, bf16[10,64,640]{2,1,0:T(8,128)(2,1)}, u32[]{:S(2)}) copy-start(bf16[10,64,640]{2,1,0:T(8,128)(2,1)} %param.9) | copy-start | bytes 2457604
  9.8 19.0 %copy-start.31 = (f32[7]{0:T(128)}, f32[7]{0:T(128)S(1)}, u32[]{:S(2)}) copy-start(f32[7]{0:T(128)S(1)} %get-tuple-element.12) | copy-start | bytes 88
  9.8 19.0 %copy-start.33 = (f32[7]{0:T(128)}, f32[7]{0:T(128)S(1)}, u32[]{:S(2)}) copy-start(f32[7]{0:T(128)S(1)} %get-tuple-element.13) | copy-start | bytes 88
  9.8 19.0 %copy-start.35 = (f32[7]{0:T(128)}, f32[7]{0:T(128)S(1)}, u32[]{:S(2)}) copy-start(f32[7]{0:T(128)S(1)} %get-tuple-element.14) | copy-start | bytes 88
  10.3 80.5 %collective-permute-start.5 = (bf16[64,640]{1,0:T(8,128)(2,1)S(1)}, bf16[64,640]{1,0:T(8,128)(2,1)S(1)}, u32[]{:S(2)}, u32[]{:S(2)}) collective-permute-start(bf16[64,640]{1,0:T(8,128)(2,1)S(1)} %bitcast.96), channel_id=1, source_target_pairs={{0,464},{16,480},{32,496},{48,0},{64,16},{80,32},{96,48},{112,64},... | collective-permute-start | bytes 245768 | tf_op jit(solution)/shard_map/ppermute | solution.py:15
  24.0 66.9 %collective-permute-start.4 = (bf16[64,640]{1,0:T(8,128)(2,1)}, bf16[64,640]{1,0:T(8,128)(2,1)}, u32[]{:S(2)}, u32[]{:S(2)}) collective-permute-start(bf16[64,640]{1,0:T(8,128)(2,1)} %bitcast.91), channel_id=1, source_target_pairs={{0,480},{16,496},{32,0},{48,16},{64,32},{80,48},{96,64},{112,80},{... | collective-permute-start | bytes 245768 | tf_op jit(solution)/shard_map/ppermute | solution.py:15
  27.7 64.1 %collective-permute-start.3 = (bf16[64,640]{1,0:T(8,128)(2,1)}, bf16[64,640]{1,0:T(8,128)(2,1)}, u32[]{:S(2)}, u32[]{:S(2)}) collective-permute-start(bf16[64,640]{1,0:T(8,128)(2,1)} %bitcast.92), channel_id=1, source_target_pairs={{0,496},{16,0},{32,16},{48,32},{64,48},{80,64},{96,80},{112,96},{1... | collective-permute-start | bytes 245768 | tf_op jit(solution)/shard_map/ppermute | solution.py:15
  29.6 0.8 copy-start.14
  29.6 23.6 %copy-start.36 = (u32[512]{0:T(512)S(1)}, u32[512]{0:T(512)}, u32[]{:S(2)}) copy-start(u32[512]{0:T(512)} %constant.128) | copy-start | bytes 6148
  29.6 25.3 %copy-start.37 = (bf16[120]{0:T(256)(128)(2,1)S(1)}, bf16[120]{0:T(256)(128)(2,1)}, u32[]{:S(2)}) copy-start(bf16[120]{0:T(256)(128)(2,1)} %param.15) | copy-start | bytes 724
  29.6 25.6 %copy-start.38 = (bf16[40]{0:T(256)(128)(2,1)S(1)}, bf16[40]{0:T(256)(128)(2,1)}, u32[]{:S(2)}) copy-start(bf16[40]{0:T(256)(128)(2,1)} %param.16) | copy-start | bytes 244
  29.6 58.2 %copy-start.17 = (s32[32,1,10]{0,1,2:T(1,128)S(1)}, s32[32,1,10]{0,1,2:T(1,128)}, u32[]{:S(2)}) copy-start(s32[32,1,10]{0,1,2:T(1,128)} %param.12) | copy-start | bytes 3844
  88.5 2.3 copy-start.22
  88.5 2.3 copy-start.24
  88.5 2.3 copy-start.26
  92.7 1.4 copy-start.5
  92.7 2.3 copy-start.12
  94.1 0.9 copy-start.2
  115.4 2.8 copy-start.10
  115.4 2.8 copy-start.28
  118.2 1.0 copy-start.15
  118.2 1.5 copy-start.39
  124.7 2.7 copy-start.27
  124.7 3.3 copy-start.25
  124.7 4.6 copy-start.40
  127.4 1.8 copy-start.1
  127.5 1.2 copy-start.23
  128.0 1.2 copy-start.16
  128.1 1.3 copy-start.7
  128.1 1.7 copy-start.11
  128.1 1.7 copy-start.29
  129.8 1.5 copy-start.8
  131.3 1.3 copy-start.9
  135.6 49.7 %collective-permute-start.2 = (bf16[64,640]{1,0:T(8,128)(2,1)}, bf16[64,640]{1,0:T(8,128)(2,1)}, u32[]{:S(2)}, u32[]{:S(2)}) collective-permute-start(bf16[64,640]{1,0:T(8,128)(2,1)} %bitcast.93), channel_id=1, source_target_pairs={{0,48},{16,64},{32,80},{48,96},{64,112},{80,128},{96,144},{112,160... | collective-permute-start | bytes 245768 | tf_op jit(solution)/shard_map/ppermute | solution.py:15
  151.6 34.6 %collective-permute-start.1 = (bf16[64,640]{1,0:T(8,128)(2,1)}, bf16[64,640]{1,0:T(8,128)(2,1)}, u32[]{:S(2)}, u32[]{:S(2)}) collective-permute-start(bf16[64,640]{1,0:T(8,128)(2,1)} %bitcast.94), channel_id=1, source_target_pairs={{0,32},{16,48},{32,64},{48,80},{64,96},{80,112},{96,128},{112,144}... | collective-permute-start | bytes 245768 | tf_op jit(solution)/shard_map/ppermute | solution.py:15
  154.2 33.0 %collective-permute-start = (bf16[64,640]{1,0:T(8,128)(2,1)}, bf16[64,640]{1,0:T(8,128)(2,1)}, u32[]{:S(2)}, u32[]{:S(2)}) collective-permute-start(bf16[64,640]{1,0:T(8,128)(2,1)} %bitcast.95), channel_id=1, source_target_pairs={{0,16},{16,32},{32,48},{48,64},{64,80},{80,96},{96,112},{112,128},... | collective-permute-start | bytes 245768 | tf_op jit(solution)/shard_map/ppermute | solution.py:15
  169.6 0.6 copy-start.30
  169.6 303.0 %all-reduce.10.cloned.1.call-start = ((), (), s32[]{:S(2)}) async-start(), calls=%async_computation.1 | async-start | bytes 204800 | tf_op jit(solution)/shard_map/psum | solution.py:125
  178.2 5.0 %copy-start.4 = (bf16[10,64,640]{2,1,0:T(8,128)(2,1)S(1)}, bf16[10,64,640]{2,1,0:T(8,128)(2,1)}, u32[]{:S(2)}) copy-start(bf16[10,64,640]{2,1,0:T(8,128)(2,1)} %param.9) | copy-start | bytes 2457604
  178.2 5.0 %copy-start.6 = (f32[64,640]{1,0:T(8,128)S(1)}, f32[64,640]{1,0:T(8,128)}, u32[]{:S(2)}) copy-start(f32[64,640]{1,0:T(8,128)} %copy-done.5) | copy-start | bytes 491524
  178.2 5.0 %copy-start.19 = (f32[10]{0:T(128)S(1)}, f32[10]{0:T(128)}, u32[]{:S(2)}) copy-start(f32[10]{0:T(128)} %convert_element_type.195) | copy-start | bytes 124
  178.2 5.0 %copy-start.20 = (f32[10]{0:T(128)S(1)}, f32[10]{0:T(128)}, u32[]{:S(2)}) copy-start(f32[10]{0:T(128)} %convert_element_type.191) | copy-start | bytes 124
  178.2 5.1 %copy-start.21 = (f32[10]{0:T(128)S(1)}, f32[10]{0:T(128)}, u32[]{:S(2)}) copy-start(f32[10]{0:T(128)} %convert_element_type.187) | copy-start | bytes 124
  183.3 97.6 %copy-start.32 = (f32[7]{0:T(128)S(1)}, f32[7]{0:T(128)}, u32[]{:S(2)}) copy-start(f32[7]{0:T(128)} %copy-done.31) | copy-start | bytes 88
  183.3 97.6 %copy-start.34 = (f32[7]{0:T(128)S(1)}, f32[7]{0:T(128)}, u32[]{:S(2)}) copy-start(f32[7]{0:T(128)} %copy-done.33) | copy-start | bytes 88
Sparse Core Ops, SparseCore 0:
  11.1 66.3 all-gather.1
  169.7 109.5 all-reduce.11
  282.2 190.3 all-reduce.9
where the time goes:
time: 482 us; the launch traced here: 481 us
  waiting for transfers between devices  281 us (58%)
  blocking collectives  54.6 us (11%)
  local copies, waits for them, and re-layouts  47.6 us (10%)
  matrix products  34.6 us (7%)
  starting transfers between devices  33.9 us (7%)
  between operations  16.3 us (3%)
  other arithmetic  12.7 us (3%)
    psum x1, waiting for transfers between devices, shards(): grad_w_out = lax.psum(shared, 'dp')  189 us
    unnamed x4, waiting for transfers between devices  92 us
    ppermute x6, starting transfers between devices, from_behind(): lax.ppermute(array, axis, [(i, (i + by) % devices) for i in range(devices)])  33.5 us
    unnamed x1, blocking collectives  31.8 us
    all_gather x1, blocking collectives, shards(): lax.all_gather(w_out, 'shard', axis=1, tiled=True)  22.8 us
  transfers between devices with their start and end apart: 9, of which 2 were waited for; matrix products, arithmetic and copies ran while one was open for 11% of the time, Pallas kernels for 0%

commit v1 on v0

v1 whole, which is shorter than its diff:
```python
import functools

import jax
import jax.numpy as jnp
from jax import lax
from jax.experimental import pallas as pl
from jax.experimental.pallas import tpu as pltpu
from jax.sharding import PartitionSpec as P

HEADS = 8
MOVES = 3
EPS = 1e-06
HALF = 320
PADH = 384
GROUP = 128
VMEM_LIMIT = 56 * 1024 * 1024

f32 = jnp.float32
bf16 = jnp.bfloat16


def permute_dp(array, by):
    n = lax.axis_size("dp")
    return lax.ppermute(array, "dp", [(i, (i + by) % n) for i in range(n)])


def swap_cores(array):
    n = lax.axis_size("dp")
    return lax.ppermute(array, "dp", [(i, i ^ 1) for i in range(n)])


def dot(a, b, ca, cb):
    return lax.dot_general(a, b, (((ca,), (cb,)), ((), ())), preferred_element_type=f32)


def pack_kernel(
    len_ref, dest_ref, slot_ref, act_ref, wqkv_ref, bias_ref, gain_ref, wout_ref,
    blob_ref, par_a_ref, par_b_ref, stage, pick, sems, blob_sems,
):
    n_dp = len_ref.shape[0]
    slots = len_ref.shape[2]
    n_shard = blob_ref.shape[0]
    me = lax.axis_index("dp")
    core = lax.rem(me, 2)
    for d in range(1, MOVES + 1):
        pick[d - 1] = 0
        target = lax.rem(me + d, n_dp)
        for s in range(slots):
            @pl.when((len_ref[me, 0, s] > 0) & (dest_ref[me, 0, s] == target))
            def _(d=d, s=s):
                pick[d - 1] = s
    moves = [
        pltpu.make_async_copy(act_ref.at[pick[1]], par_a_ref.at[0], sems.at[0]),
        pltpu.make_async_copy(act_ref.at[pick[2]], par_a_ref.at[1], sems.at[1]),
        pltpu.make_async_copy(act_ref.at[pick[0]], par_b_ref, sems.at[2]),
    ]
    for m in moves:
        m.start()
    inner = wout_ref.shape[0]
    wout_t = wout_ref[...].astype(f32).T.astype(bf16)
    stage[:, 4 * HALF:] = jnp.zeros((stage.shape[0], stage.shape[1] - 4 * HALF), bf16)
    for c in range(2):
        @pl.when(core == c)
        def _(c=c):
            stage[:, 0 : 4 * HALF] = jnp.concatenate(
                [
                    wqkv_ref[:, g * inner + c * HALF : g * inner + (c + 1) * HALF].astype(f32)
                    for g in range(3)
                ]
                + [wout_t[:, c * HALF : (c + 1) * HALF].astype(f32)],
                axis=1,
            ).astype(bf16)
    tail = jnp.concatenate(
        [
            jnp.pad(bias_ref[...].astype(f32), ((0, 0), (0, 128 - bias_ref.shape[1]))),
            jnp.pad(gain_ref[...].astype(f32), ((0, 0), (0, 128 - gain_ref.shape[1]))),
            jnp.zeros((14, 128), f32),
        ],
        axis=0,
    ).astype(bf16)
    stage[0:16, 4 * HALF :] = tail
    copies = [
        pltpu.make_async_copy(stage, blob_ref.at[s], blob_sems.at[s]) for s in range(n_shard)
    ]
    for cp in copies:
        cp.start()
    for cp in copies:
        cp.wait()
    for m in moves:
        m.wait()


def pack(tables, act, wqkv, bias, gain, wout, n_shard):
    rows = wqkv.shape[0]
    cols = 4 * HALF + 128
    window = act.shape[1:]
    smem = pl.BlockSpec(memory_space=pltpu.SMEM)
    vmem = pl.BlockSpec(memory_space=pltpu.VMEM)
    hbm = pl.BlockSpec(memory_space=pl.ANY)
    return pl.pallas_call(
        pack_kernel,
        out_shape=(
            jax.ShapeDtypeStruct((n_shard, rows, cols), bf16),
            jax.ShapeDtypeStruct((2,) + window, bf16),
            jax.ShapeDtypeStruct(window, bf16),
        ),
        in_specs=[smem, smem, smem, hbm, vmem, vmem, vmem, vmem],
        out_specs=(hbm, hbm, hbm),
        scratch_shapes=[
            pltpu.VMEM((rows, cols), bf16),
            pltpu.SMEM((MOVES,), jnp.int32),
            pltpu.SemaphoreType.DMA((MOVES,)),
            pltpu.SemaphoreType.DMA((n_shard,)),
        ],
        compiler_params=pltpu.CompilerParams(vmem_limit_bytes=VMEM_LIMIT),
        name="pack_weights",
    )(*tables, act, wqkv, bias, gain, wout)


def block_kernel(
    len_ref, dest_ref, slot_ref, act_ref, arr_a_ref, arr_b_ref, cot_ref, own_ref, oth_ref,
    out_ref, grad_ref, ret_c_ref, ret_d_ref, gt_own_ref, gt_oth_ref,
    xb, cotb, g_own, g_oth, gbuf, zeros, bias_row, gain_row, nrm, ub, wqkv, wo, qkv, da, att, dproj,
    code, lens, win_sems, load_sems, out_sems,
):
    n_dp = len_ref.shape[0]
    slots = len_ref.shape[2]
    kept = xb.shape[0]
    patches, ch = xb.shape[1:]
    n_shard, rows = own_ref.shape[:2]
    tokens = kept * patches
    me = lax.axis_index("dp")
    core = lax.rem(me, 2)

    loads = [
        pltpu.make_async_copy(own_ref, g_own, load_sems.at[0]),
        pltpu.make_async_copy(oth_ref, g_oth, load_sems.at[1]),
        pltpu.make_async_copy(cot_ref, cotb, load_sems.at[2]),
    ]
    for cp in loads:
        cp.start()
    xb[...] = jnp.zeros(xb.shape, bf16)
    zeros[...] = jnp.zeros(zeros.shape, bf16)
    for b in range(kept):
        code[b] = -1
        lens[b] = 0
    arrived = {1: arr_b_ref.at[0], 2: arr_a_ref.at[0], 3: arr_b_ref.at[1]}
    for d in range(MOVES + 1):
        row = lax.rem(me - d + n_dp, n_dp)
        for s in range(slots):
            @pl.when((len_ref[row, 0, s] > 0) & (dest_ref[row, 0, s] == me))
            def _(d=d, s=s, row=row):
                b = slot_ref[row, 0, s]
                code[b] = d
                lens[b] = len_ref[row, 0, s]
                source = act_ref.at[s] if d == 0 else arrived[d]
                pltpu.make_async_copy(source, xb.at[b], win_sems.at[b]).start()

    loads[0].wait()
    for s in range(n_shard):
        tail = g_own[s, 0:16, 4 * HALF :].astype(f32)
        bias_row[0:1, 120 * s : 120 * s + 120] = tail[0:1, 0:120]
        gain_row[0:1, rows * s : rows * s + rows] = tail[1:2, 0:rows]
    loads[1].wait()
    pad = jnp.zeros((2 * rows, PADH - HALF), f32)
    for h, g in enumerate((g_own, g_oth)):
        for t in range(n_shard // 2):
            both = jnp.concatenate(
                [g[2 * t, :, 0 : 4 * HALF].astype(f32), g[2 * t + 1, :, 0 : 4 * HALF].astype(f32)],
                axis=0,
            )
            at = pl.ds(2 * rows * t, 2 * rows)
            for k in range(4):
                piece = jnp.concatenate(
                    [both[:, k * HALF : (k + 1) * HALF], pad], axis=1
                ).astype(bf16)
                if k < 3:
                    wqkv[at, (3 * h + k) * PADH : (3 * h + k + 1) * PADH] = piece
                else:
                    wo[at, h * PADH : (h + 1) * PADH] = piece

    bias = []
    for h in range(2):
        for k in range(3):
            low = bias_row[0:1, 2 * k * HALF : (2 * k + 1) * HALF]
            high = bias_row[0:1, (2 * k + 1) * HALF : (2 * k + 2) * HALF]
            first = core == h
            bias.append(jnp.where(first, low, high))
            bias.append(jnp.zeros((1, PADH - HALF), f32))
    bias = jnp.concatenate(bias, axis=1)

    loads[2].wait()
    position = lax.broadcasted_iota(jnp.int32, (patches, 1), 0)
    gain = gain_row[...]
    for b in range(kept):
        @pl.when(code[b] >= 0)
        def _(b=b):
            pltpu.make_async_copy(act_ref.at[0], xb.at[b], win_sems.at[b]).wait()

        x = xb[b].astype(f32)
        inv = lax.rsqrt(jnp.mean(x * x, axis=-1, keepdims=True) + EPS)
        at = pl.ds(b * patches, patches)
        nrm[at, :] = (x * inv * gain).astype(bf16)
        live = position < lens[b]
        ub[at, :] = jnp.where(live, cotb[b].astype(f32), 0.0).astype(bf16)

    qkv[0:tokens, :] = (dot(nrm[...], wqkv[...], 1, 0) + bias).astype(bf16)
    qkv[tokens:, :] = jnp.zeros((qkv.shape[0] - tokens, qkv.shape[1]), bf16)
    da[0:tokens, :] = dot(ub[...], wo[...], 1, 0).astype(bf16)
    da[tokens:, :] = jnp.zeros((da.shape[0] - tokens, da.shape[1]), bf16)

    heads = 4
    head = HALF // heads
    scale = head ** (-0.5)
    lane_head = lax.broadcasted_iota(jnp.int32, (GROUP, PADH), 1) // head
    head_mask = [(lane_head == h).astype(f32).astype(bf16) for h in range(heads)]
    q_pos = lax.broadcasted_iota(jnp.int32, (GROUP, GROUP), 0)
    k_pos = lax.broadcasted_iota(jnp.int32, (GROUP, GROUP), 1)
    lower = jnp.where(q_pos < patches, 0, patches)

    def by_head(m):
        return jnp.concatenate([m * head_mask[h] for h in range(heads)], axis=0)

    def pair(j, _):
        at = pl.ds(pl.multiple_of(j * GROUP, GROUP), GROUP)
        len0 = jnp.maximum(lens[2 * j], 1)
        second = jnp.minimum(2 * j + 1, kept - 1)
        len1 = jnp.maximum(lens[second], 1)
        upper = jnp.where(q_pos < patches, len0, patches + len1)
        allowed = (k_pos >= lower) & (k_pos < upper)
        for h in range(2):
            base = 3 * h * PADH
            q = qkv[at, base : base + PADH]
            k = qkv[at, base + PADH : base + 2 * PADH]
            v = qkv[at, base + 2 * PADH : base + 3 * PADH]
            d_att = da[at, h * PADH : (h + 1) * PADH]
            k_heads = by_head(k)
            v_heads = by_head(v)
            scores = dot(q, k_heads, 1, 1) * scale
            d_probs = dot(d_att, v_heads, 1, 1)
            probs, d_scores = [], []
            for i in range(heads):
                lanes = slice(i * GROUP, (i + 1) * GROUP)
                weights = jnp.where(allowed, jnp.exp(scores[:, lanes]), 0.0)
                p = weights / jnp.sum(weights, axis=-1, keepdims=True)
                dp = d_probs[:, lanes].astype(bf16).astype(f32)
                mean = jnp.sum(dp * p, axis=-1, keepdims=True)
                probs.append(p.astype(bf16))
                d_scores.append((p * (dp - mean) * scale).astype(bf16))
            att[at, h * PADH : (h + 1) * PADH] = dot(
                jnp.concatenate(probs, axis=1), v_heads, 1, 0
            ).astype(bf16)
            dproj[at, base : base + PADH] = dot(
                jnp.concatenate(d_scores, axis=1), k_heads, 1, 0
            ).astype(bf16)
            dproj[at, base + PADH : base + 2 * PADH] = dot(
                jnp.concatenate(d_scores, axis=0), by_head(q), 0, 0
            ).astype(bf16)
            dproj[at, base + 2 * PADH : base + 3 * PADH] = dot(
                jnp.concatenate(probs, axis=0), by_head(d_att), 0, 0
            ).astype(bf16)
        return 0

    lax.fori_loop(0, qkv.shape[0] // GROUP, pair, 0)

    attended = att[0:tokens, :]
    gt = dot(ub[...], attended, 0, 0)
    gt_own_ref[...] = gt[:, 0:HALF]
    gt_oth_ref[...] = gt[:, PADH : PADH + HALF].astype(bf16)
    added = dot(attended, wo[...], 1, 1)
    d_nrm = dot(dproj[0:tokens, :], wqkv[...], 1, 1)
    for b in range(kept):
        at = slice(b * patches, (b + 1) * patches)
        x = xb[b].astype(f32)
        live = position < lens[b]
        out_ref[b] = jnp.where(live, x + added[at], 0.0).astype(bf16)
        inv = lax.rsqrt(jnp.mean(x * x, axis=-1, keepdims=True) + EPS)
        t = d_nrm[at].astype(bf16).astype(f32) * gain
        along = jnp.mean(t * x, axis=-1, keepdims=True)
        dx = t * inv - x * (inv * inv * inv * along)
        gbuf[b] = (ub[at, :].astype(f32) + dx).astype(bf16)

    def own_copy(s, source):
        return pltpu.make_async_copy(source, grad_ref.at[s], out_sems.at[s])

    for s in range(slots):
        stays = (len_ref[me, 0, s] > 0) & (dest_ref[me, 0, s] == me)

        @pl.when(stays)
        def _(s=s):
            own_copy(s, gbuf.at[slot_ref[me, 0, s]]).start()

        @pl.when(jnp.logical_not(stays))
        def _(s=s):
            own_copy(s, zeros).start()

    returned = {1: ret_c_ref.at[0], 2: ret_d_ref, 3: ret_c_ref.at[1]}
    for b in range(kept):
        for d in range(1, MOVES + 1):
            @pl.when(code[b] == d)
            def _(b=b, d=d):
                cp = pltpu.make_async_copy(gbuf.at[b], returned[d], win_sems.at[b])
                cp.start()
                cp.wait()
    for s in range(slots):
        own_copy(s, zeros).wait()


def block(tables, act, arr_a, arr_b, cot, own, oth):
    kept, patches, ch = cot.shape
    slots = act.shape[0]
    tokens = kept * patches
    padded = -(-tokens // GROUP) * GROUP
    smem = pl.BlockSpec(memory_space=pltpu.SMEM)
    vmem = pl.BlockSpec(memory_space=pltpu.VMEM)
    hbm = pl.BlockSpec(memory_space=pl.ANY)
    window = (patches, ch)
    return pl.pallas_call(
        block_kernel,
        out_shape=(
            jax.ShapeDtypeStruct(cot.shape, bf16),
            jax.ShapeDtypeStruct(act.shape, bf16),
            jax.ShapeDtypeStruct((2,) + window, bf16),
            jax.ShapeDtypeStruct(window, bf16),
            jax.ShapeDtypeStruct((ch, HALF), f32),
            jax.ShapeDtypeStruct((ch, HALF), bf16),
        ),
        in_specs=[smem] * 3 + [hbm] * 6,
        out_specs=(vmem, hbm, hbm, hbm, vmem, vmem),
        scratch_shapes=[
            pltpu.VMEM(cot.shape, bf16),
            pltpu.VMEM(cot.shape, bf16),
            pltpu.VMEM(own.shape, bf16),
            pltpu.VMEM(own.shape, bf16),
            pltpu.VMEM(cot.shape, bf16),
            pltpu.VMEM(window, bf16),
            pltpu.VMEM((1, 6 * HALF), f32),
            pltpu.VMEM((1, ch), f32),
            pltpu.VMEM((tokens, ch), bf16),
            pltpu.VMEM((tokens, ch), bf16),
            pltpu.VMEM((ch, 6 * PADH), bf16),
            pltpu.VMEM((ch, 2 * PADH), bf16),
            pltpu.VMEM((padded, 6 * PADH), bf16),
            pltpu.VMEM((padded, 2 * PADH), bf16),
            pltpu.VMEM((padded, 2 * PADH), bf16),
            pltpu.VMEM((padded, 6 * PADH), bf16),
            pltpu.SMEM((kept,), jnp.int32),
            pltpu.SMEM((kept,), jnp.int32),
            pltpu.SemaphoreType.DMA((kept,)),
            pltpu.SemaphoreType.DMA((3,)),
            pltpu.SemaphoreType.DMA((slots,)),
        ],
        compiler_params=pltpu.CompilerParams(vmem_limit_bytes=VMEM_LIMIT),
        name="window_block",
    )(*tables, act, arr_a, arr_b, cot, own, oth)


def place_kernel(len_ref, dest_ref, back_c_ref, back_d_ref, grad_in_ref, grad_ref, sems):
    n_dp = len_ref.shape[0]
    slots = len_ref.shape[2]
    me = lax.axis_index("dp")
    back = {1: back_c_ref.at[0], 2: back_d_ref.at[0], 3: back_d_ref.at[1]}
    for wait in (False, True):
        for d in range(1, MOVES + 1):
            target = lax.rem(me + d, n_dp)
            for s in range(slots):
                @pl.when((len_ref[me, 0, s] > 0) & (dest_ref[me, 0, s] == target))
                def _(d=d, s=s, wait=wait):
                    cp = pltpu.make_async_copy(back[d], grad_ref.at[s], sems.at[d - 1])
                    if wait:
                        cp.wait()
                    else:
                        cp.start()


def place(tables, back_c, back_d, grad):
    smem = pl.BlockSpec(memory_space=pltpu.SMEM)
    hbm = pl.BlockSpec(memory_space=pl.ANY)
    return pl.pallas_call(
        place_kernel,
        out_shape=jax.ShapeDtypeStruct(grad.shape, bf16),
        in_specs=[smem, smem, hbm, hbm, hbm],
        out_specs=hbm,
        scratch_shapes=[pltpu.SemaphoreType.DMA((MOVES,))],
        input_output_aliases={4: 0},
        name="place_returned",
    )(tables[0], tables[1], back_c, back_d, grad)


def add_kernel(parts_ref, out_ref):
    n = parts_ref.shape[0]
    for c in range(2):
        total = parts_ref[c].astype(f32)
        for z in range(1, n // 2):
            total = total + parts_ref[2 * z + c].astype(f32)
        out_ref[c * HALF : (c + 1) * HALF, :] = total.T


def add_shares(parts):
    n, rows, half = parts.shape
    vmem = pl.BlockSpec(memory_space=pltpu.VMEM)
    return pl.pallas_call(
        add_kernel,
        out_shape=jax.ShapeDtypeStruct((2 * half, rows), f32),
        in_specs=[vmem],
        out_specs=vmem,
        compiler_params=pltpu.CompilerParams(vmem_limit_bytes=VMEM_LIMIT),
        name="add_shares",
    )(parts)


def shards(
    activations, cotangent, window_len, move_dest, move_slot, w_qkv, b_qkv, norm_gain, w_out
):
    n_shard = lax.axis_size("shard")
    rows = w_qkv.shape[0]
    tables = (window_len, move_dest, move_slot)
    blob, par_a, par_b = pack(
        tables, activations, w_qkv, b_qkv[None], norm_gain[None], w_out, n_shard
    )
    arr_a = permute_dp(par_a, 2)
    own = lax.all_to_all(blob, "shard", 0, 0)
    arr_b = permute_dp(jnp.stack([par_b, arr_a[1]]), 1)
    oth = swap_cores(own)
    out, grad, ret_c, ret_d, gt_own, gt_oth = block(
        tables, activations, arr_a, arr_b, cotangent, own, oth
    )
    gt_in = swap_cores(gt_oth)
    back_c = permute_dp(ret_c, -1)
    share = (gt_own + gt_in.astype(f32)).astype(bf16).reshape(n_shard, rows, HALF)
    chunks = lax.all_to_all(share, "shard", 0, 0)
    summed = jnp.sum(chunks.astype(f32), axis=0).astype(bf16)
    back_d = permute_dp(jnp.stack([ret_d, back_c[1]]), -2)
    parts = lax.all_gather(summed, "dp", axis=0)
    grad_w_out = add_shares(parts)
    grad_input = place(tables, back_c, back_d, grad)
    return (out, grad_input, grad_w_out)


def solution(mesh):
    return jax.shard_map(
        shards,
        mesh=mesh,
        in_specs=(
            P(("dp", "shard"), None, None),
            P(("dp", "shard"), None, None),
            P(None, "shard", None),
            P(None, "shard", None),
            P(None, "shard", None),
            P("shard", None),
            P("shard"),
            P("shard"),
            P(None, "shard"),
        ),
        out_specs=(
            P(("dp", "shard"), None, None),
            P(("dp", "shard"), None, None),
            P(None, "shard"),
        ),
        check_vma=False,
    )
```

time: 482 us -> 161 us (0.33)
  the two profiles are of different devices: /device:TPU:1 before, /device:TPU:11 now
where the time goes in v1:
time: 161 us; the launch traced here: 160 us
  blocking collectives  69.1 us (43%)
  Pallas kernels  33.4 us (21%)
  starting transfers between devices  24.4 us (15%)
  waiting for transfers between devices  20.5 us (13%)
  local copies, waits for them, and re-layouts  10.1 us (6%)
  other arithmetic  2.21 us (1%)
    all_gather x1, blocking collectives, shards(): parts = lax.all_gather(summed, 'dp', axis=0)  43 us
    all_to_all x1, blocking collectives, shards(): own = lax.all_to_all(blob, 'shard', 0, 0)  26.1 us
    pallas_call x1, Pallas kernels, block(): pl.pallas_call(block_kernel, out_shape=(jax.ShapeDtypeStruct(cot.shape, b...  19.2 us
    ppermute x4, waiting for transfers between devices, permute_dp(): return lax.ppermute(array, 'dp', [(i, (i + by) % n) for i in range(n)])  18.9 us
    ppermute x2, starting transfers between devices, swap_cores(): return lax.ppermute(array, 'dp', [(i, i ^ 1) for i in range(n)])  12.6 us
    pallas_call x1, Pallas kernels, pack(): pl.pallas_call(pack_kernel, out_shape=(jax.ShapeDtypeStruct((n_shard, row...  10.4 us
    unnamed x23, local copies, waits for them, and re-layouts  10 us
    ppermute x4, starting transfers between devices, permute_dp(): return lax.ppermute(array, 'dp', [(i, (i + by) % n) for i in range(n)])  5.96 us
  transfers between devices with their start and end apart: 7, of which 4 were waited for; matrix products, arithmetic and copies ran while one was open for 1% of the time, Pallas kernels for 1%

profile of v1, /device:TPU:11, one launch (start us, length us, event | category | flops | bytes accessed | tf_op | source)
XLA Modules:
  0.0 160.5 jit_solution(2289132775702950264)
XLA Ops:
  0.6 1.4 copy.17.len_ref
  2.0 1.4 copy.18.dest_ref
  3.4 1.4 copy.19.slot_ref
  4.7 1.6 %copy.16.wout_ref = bf16[640,40]{1,0:T(8,128)(2,1)} copy(bf16[640,40]{0,1:T(8,128)(2,1)} %param.17) | data formatting | bytes 102400 | tf_op args[8]
  6.3 10.4 %pack_weights.1 = (bf16[16,40,1408]{2,1,0:T(8,128)(2,1)}, bf16[2,64,640]{2,1,0:T(8,128)(2,1)}, bf16[64,640]{1,0:T(8,128)(2,1)}) custom-call(s32[32,1,10]{2,1,0:T(1,128)} %copy.17.len_ref, s32[32,1,10]{2,1,0:T(1,128)} %copy.18.dest_ref, s32[32,1,10]{2,1,0:T(1,128)} %copy.19.slot_ref, bf16[10,64,640]{2,1,0:T(8,128)(2,1)} %act_ref.3, ...), custom_call_target="tpu_custom_call" | custom-call | tf_op jit(solution)/shard_map/pack_weights/pallas_call | solution.py:100
  16.7 0.0 copy-start.8
  16.7 0.0 copy-start.7
  16.8 26.1 %all_to_all.10.own_ref = bf16[16,40,1408]{2,1,0:T(8,128)(2,1)S(1)} all-to-all(bf16[16,40,1408]{2,1,0:T(8,128)(2,1)} %get-tuple-element.14), channel_id=1, replica_groups=mesh['dp'=32,'shard'=16] {'shard'}, dimensions={0} | all-to-all | bytes 3604480 | tf_op jit(solution)/shard_map/all_to_all | solution.py:422
  42.8 0.0 copy-start
  42.8 6.3 %collective-permute-start.2 = (bf16[16,40,1408]{2,1,0:T(8,128)(2,1)S(1)}, bf16[16,40,1408]{2,1,0:T(8,128)(2,1)S(1)}, u32[]{:S(2)}, u32[]{:S(2)}) collective-permute-start(bf16[16,40,1408]{2,1,0:T(8,128)(2,1)S(1)} %all_to_all.10.own_ref), channel_id=1, source_target_pairs={{0,16},{16,0},{32,48},{48,32},{64,80},{80,64},{96,112},{112,96},{1... | collective-permute-start | bytes 5406728 | tf_op jit(solution)/shard_map/ppermute | solution.py:29
  49.1 0.0 copy-done.8
  49.1 3.8 %collective-permute-start = (bf16[2,64,640]{2,1,0:T(8,128)(2,1)S(1)}, bf16[2,64,640]{2,1,0:T(8,128)(2,1)S(1)}, u32[]{:S(2)}, u32[]{:S(2)}) collective-permute-start(bf16[2,64,640]{2,1,0:T(8,128)(2,1)S(1)} %copy-done.8), channel_id=1, source_target_pairs={{0,32},{16,48},{32,64},{48,80},{64,96},{80,112},{96,128},{112,144}... | collective-permute-start | bytes 491528 | tf_op jit(solution)/shard_map/ppermute | solution.py:24
  52.9 12.1 %collective-permute-done.arr_a_ref = bf16[2,64,640]{2,1,0:T(8,128)(2,1)S(1)} collective-permute-done((bf16[2,64,640]{2,1,0:T(8,128)(2,1)S(1)}, bf16[2,64,640]{2,1,0:T(8,128)(2,1)S(1)}, u32[]{:S(2)}, u32[]{:S(2)}) %collective-permute-start) | collective-permute-done | bytes 163872 | tf_op jit(solution)/shard_map/ppermute | solution.py:24
  65.0 0.0 copy-start.3
  65.1 0.0 copy-done.7
  65.1 0.0 collective-permute-start.1
  65.1 2.3 %collective-permute-done.1.arr_b_ref = bf16[2,64,640]{2,1,0:T(8,128)(2,1)S(1)} collective-permute-done((bf16[2,64,640]{2,1,0:T(8,128)(2,1)S(1)}, bf16[2,64,640]{2,1,0:T(8,128)(2,1)S(1)}, u32[]{:S(2)}, u32[]{:S(2)}) %collective-permute-start.1) | collective-permute-done | bytes 163872 | tf_op jit(solution)/shard_map/ppermute | solution.py:24
  67.4 0.0 copy-start.5
  67.4 0.0 collective-permute-done.2.oth_ref
  67.4 0.0 copy-done
  67.4 0.0 copy-done.3
  67.4 0.7 copy-done.5
  68.0 0.0 copy-start.1
  68.0 1.2 copy-done.1
  69.3 19.2 %window_block.1 = (bf16[7,64,640]{2,1,0:T(8,128)(2,1)}, bf16[10,64,640]{2,1,0:T(8,128)(2,1)}, bf16[2,64,640]{2,1,0:T(8,128)(2,1)}, bf16[64,640]{1,0:T(8,128)(2,1...) custom-call(s32[32,1,10]{2,1,0:T(1,128)} %copy.17.len_ref, s32[32,1,10]{2,1,0:T(1,128)} %copy.18.dest_ref, ...), custom_call_target="tpu_custom_call" | custom-call | tf_op jit(solution)/shard_map/window_block/pallas_call | solution.py:318
  88.5 0.0 copy-start.6
  88.5 6.3 %collective-permute-start.5 = (bf16[640,320]{1,0:T(8,128)(2,1)}, bf16[640,320]{1,0:T(8,128)(2,1)S(1)}, u32[]{:S(2)}, u32[]{:S(2)}) collective-permute-start(bf16[640,320]{1,0:T(8,128)(2,1)} %get-tuple-element.20), channel_id=1, source_target_pairs={{0,16},{16,0},{32,48},{48,32},{64,80},{80,64},{96,112},{112,96},{1... | collective-permute-start | bytes 1228808 | tf_op jit(solution)/shard_map/ppermute | solution.py:29
  94.9 0.0 collective-permute-start.3
  94.9 1.7 %collective-permute-done.5 = bf16[640,320]{1,0:T(8,128)(2,1)S(1)} collective-permute-done((bf16[640,320]{1,0:T(8,128)(2,1)}, bf16[640,320]{1,0:T(8,128)(2,1)S(1)}, u32[]{:S(2)}, u32[]{:S(2)}) %collective-permute-start.5) | collective-permute-done | bytes 409632 | tf_op jit(solution)/shard_map/ppermute | solution.py:29
  96.6 2.1 %add_convert_fusion = bf16[640,320]{1,0:T(8,128)(2,1)} fusion(f32[640,320]{1,0:T(8,128)} %get-tuple-element.19, bf16[640,320]{1,0:T(8,128)(2,1)S(1)} %collective-permute-done.5), kind=kLoop, calls=%fused_computation | loop fusion | flops 614400 | bytes 1638400 | tf_op jit(solution)/shard_map/convert_element_type | solution.py:430
  98.6 5.8 %all-to-all-start.1 = ((bf16[16,40,320]{2,1,0:T(8,128)(2,1)}), bf16[16,40,320]{2,1,0:T(8,128)(2,1)S(1)}, u32[]{:S(2)}, u32[]{:S(2)}) async-start(bf16[16,40,320]{2,1,0:T(8,128)(2,1)} %bitcast.4), calls=%async_computation.1 | async-start | bytes 983040 | tf_op jit(solution)/shard_map/all_to_all | solution.py:431
  104.4 0.0 collective-permute-done.3.back_c_ref
  104.4 0.0 copy-start.2
  104.5 0.0 copy-done.6
  104.5 2.2 %collective-permute-start.4 = (bf16[2,64,640]{2,1,0:T(8,128)(2,1)S(1)}, bf16[2,64,640]{2,1,0:T(8,128)(2,1)S(1)}, u32[]{:S(2)}, u32[]{:S(2)}) collective-permute-start(bf16[2,64,640]{2,1,0:T(8,128)(2,1)S(1)} %pad_maximum_fusion.1), channel_id=1, source_target_pairs={{0,480},{16,496},{32,0},{48,16},{64,32},{80,48},{96,64},{112,80},{... | collective-permute-start | bytes 491528 | tf_op jit(solution)/shard_map/ppermute | solution.py:24
  106.7 4.5 %collective-permute-done.4.back_d_ref = bf16[2,64,640]{2,1,0:T(8,128)(2,1)S(1)} collective-permute-done((bf16[2,64,640]{2,1,0:T(8,128)(2,1)S(1)}, bf16[2,64,640]{2,1,0:T(8,128)(2,1)S(1)}, u32[]{:S(2)}, u32[]{:S(2)}) %collective-permute-start.4) | collective-permute-done | bytes 163872 | tf_op jit(solution)/shard_map/ppermute | solution.py:24
  111.2 0.0 copy-start.4
  111.2 0.0 copy-done.2
  111.2 0.7 copy-done.4
  111.8 1.6 place_returned.1
  113.4 0.0 all-to-all-done.1
  113.4 0.1 reduce_sum.12
  113.5 43.0 %all-gather = bf16[1280,320]{1,0:T(8,128)(2,1)} all-gather(bf16[40,320]{1,0:T(8,128)(2,1)S(1)} %reduce_sum.12), channel_id=2, replica_groups=mesh['dp'=32,'shard'=16] {'dp'}, dimensions={0}, use_global_device_ids=true | all-gather | bytes 844800 | tf_op jit(solution)/shard_map/all_gather | solution.py:434
  156.5 2.2 %add_shares.1 = f32[640,40]{1,0:T(8,128)} custom-call(bf16[32,40,320]{2,1,0:T(8,128)(2,1)} %bitcast.6), custom_call_target="tpu_custom_call" | custom-call | tf_op jit(solution)/shard_map/add_shares/pallas_call | solution.py:402
  158.7 1.8 %copy.22 = f32[640,40]{0,1:T(8,128)} copy(f32[640,40]{1,0:T(8,128)} %add_shares.1) | data formatting | bytes 204800
  (4 shorter events, 0.1 us)
Async XLA Ops:
  16.7 32.4 %copy-start.8 = (bf16[2,64,640]{2,1,0:T(8,128)(2,1)S(1)}, bf16[2,64,640]{2,1,0:T(8,128)(2,1)}, u32[]{:S(2)}) copy-start(bf16[2,64,640]{2,1,0:T(8,128)(2,1)} %get-tuple-element.12) | copy-start | bytes 491524
  16.7 48.3 %copy-start.7 = (bf16[64,640]{1,0:T(8,128)(2,1)S(1)}, bf16[64,640]{1,0:T(8,128)(2,1)}, u32[]{:S(2)}) copy-start(bf16[64,640]{1,0:T(8,128)(2,1)} %get-tuple-element.13) | copy-start | bytes 245764
  42.8 24.6 %copy-start = (bf16[16,40,1408]{2,1,0:T(8,128)(2,1)}, bf16[16,40,1408]{2,1,0:T(8,128)(2,1)S(1)}, u32[]{:S(2)}) copy-start(bf16[16,40,1408]{2,1,0:T(8,128)(2,1)S(1)} %all_to_all.10.own_ref) | copy-start | bytes 5406724
  42.8 24.5 %collective-permute-start.2 = (bf16[16,40,1408]{2,1,0:T(8,128)(2,1)S(1)}, bf16[16,40,1408]{2,1,0:T(8,128)(2,1)S(1)}, u32[]{:S(2)}, u32[]{:S(2)}) collective-permute-start(bf16[16,40,1408]{2,1,0:T(8,128)(2,1)S(1)} %all_to_all.10.own_ref), channel_id=1, source_target_pairs={{0,16},{16,0},{32,48},{48,32},{64,80},{80,64},{96,112},{112,96},{1... | collective-permute-start | bytes 5406728 | tf_op jit(solution)/shard_map/ppermute | solution.py:29
  49.1 15.9 %collective-permute-start = (bf16[2,64,640]{2,1,0:T(8,128)(2,1)S(1)}, bf16[2,64,640]{2,1,0:T(8,128)(2,1)S(1)}, u32[]{:S(2)}, u32[]{:S(2)}) collective-permute-start(bf16[2,64,640]{2,1,0:T(8,128)(2,1)S(1)} %copy-done.8), channel_id=1, source_target_pairs={{0,32},{16,48},{32,64},{48,80},{64,96},{80,112},{96,128},{112,144}... | collective-permute-start | bytes 491528 | tf_op jit(solution)/shard_map/ppermute | solution.py:24
  65.0 2.3 %copy-start.3 = (bf16[2,64,640]{2,1,0:T(8,128)(2,1)}, bf16[2,64,640]{2,1,0:T(8,128)(2,1)S(1)}, u32[]{:S(2)}) copy-start(bf16[2,64,640]{2,1,0:T(8,128)(2,1)S(1)} %collective-permute-done.arr_a_ref) | copy-start | bytes 491524
  65.1 2.3 %collective-permute-start.1 = (bf16[2,64,640]{2,1,0:T(8,128)(2,1)S(1)}, bf16[2,64,640]{2,1,0:T(8,128)(2,1)S(1)}, u32[]{:S(2)}, u32[]{:S(2)}) collective-permute-start(bf16[2,64,640]{2,1,0:T(8,128)(2,1)S(1)} %pad_maximum_fusion), channel_id=1, source_target_pairs={{0,16},{16,32},{32,48},{48,64},{64,80},{80,96},{96,112},{112,128},... | collective-permute-start | bytes 491528 | tf_op jit(solution)/shard_map/ppermute | solution.py:24
  67.4 0.7 copy-start.5
  68.0 1.2 copy-start.1
  88.5 15.9 %copy-start.6 = (bf16[64,640]{1,0:T(8,128)(2,1)S(1)}, bf16[64,640]{1,0:T(8,128)(2,1)}, u32[]{:S(2)}) copy-start(bf16[64,640]{1,0:T(8,128)(2,1)} %get-tuple-element.17) | copy-start | bytes 245764
  88.5 8.0 %collective-permute-start.5 = (bf16[640,320]{1,0:T(8,128)(2,1)}, bf16[640,320]{1,0:T(8,128)(2,1)S(1)}, u32[]{:S(2)}, u32[]{:S(2)}) collective-permute-start(bf16[640,320]{1,0:T(8,128)(2,1)} %get-tuple-element.20), channel_id=1, source_target_pairs={{0,16},{16,0},{32,48},{48,32},{64,80},{80,64},{96,112},{112,96},{1... | collective-permute-start | bytes 1228808 | tf_op jit(solution)/shard_map/ppermute | solution.py:29
  94.9 9.5 %collective-permute-start.3 = (bf16[2,64,640]{2,1,0:T(8,128)(2,1)}, bf16[2,64,640]{2,1,0:T(8,128)(2,1)S(1)}, u32[]{:S(2)}, u32[]{:S(2)}) collective-permute-start(bf16[2,64,640]{2,1,0:T(8,128)(2,1)} %get-tuple-element.16), channel_id=1, source_target_pairs={{0,496},{16,0},{32,16},{48,32},{64,48},{80,64},{96,80},{112,96},{1... | collective-permute-start | bytes 491528 | tf_op jit(solution)/shard_map/ppermute | solution.py:24
  98.6 14.8 %all-to-all-start.1 = ((bf16[16,40,320]{2,1,0:T(8,128)(2,1)}), bf16[16,40,320]{2,1,0:T(8,128)(2,1)S(1)}, u32[]{:S(2)}, u32[]{:S(2)}) async-start(bf16[16,40,320]{2,1,0:T(8,128)(2,1)} %bitcast.4), calls=%async_computation.1 | async-start | bytes 983040 | tf_op jit(solution)/shard_map/all_to_all | solution.py:431
  104.4 6.7 %copy-start.2 = (bf16[2,64,640]{2,1,0:T(8,128)(2,1)}, bf16[2,64,640]{2,1,0:T(8,128)(2,1)S(1)}, u32[]{:S(2)}) copy-start(bf16[2,64,640]{2,1,0:T(8,128)(2,1)S(1)} %collective-permute-done.3.back_c_ref) | copy-start | bytes 491524
  104.5 6.7 %collective-permute-start.4 = (bf16[2,64,640]{2,1,0:T(8,128)(2,1)S(1)}, bf16[2,64,640]{2,1,0:T(8,128)(2,1)S(1)}, u32[]{:S(2)}, u32[]{:S(2)}) collective-permute-start(bf16[2,64,640]{2,1,0:T(8,128)(2,1)S(1)} %pad_maximum_fusion.1), channel_id=1, source_target_pairs={{0,480},{16,496},{32,0},{48,16},{64,32},{80,48},{96,64},{112,80},{... | collective-permute-start | bytes 491528 | tf_op jit(solution)/shard_map/ppermute | solution.py:24
  111.2 0.7 copy-start.4

commit v2 on v1

v2 whole, which is shorter than its diff:
```python
import functools

import jax
import jax.numpy as jnp
from jax import lax
from jax.experimental import pallas as pl
from jax.experimental.pallas import tpu as pltpu
from jax.sharding import PartitionSpec as P

HEADS = 8
MOVES = 3
EPS = 1e-06
HALF = 320
PADH = 384
CODES, LENS, STAYS, LEAVES, PLAN = 0, 16, 32, 48, 64
VMEM_LIMIT = 40 * 1024 * 1024
PACK_VMEM_LIMIT = 60 * 1024 * 1024

f32 = jnp.float32
bf16 = jnp.bfloat16


def permute_dp(array, by):
    n = lax.axis_size("dp")
    return lax.ppermute(array, "dp", [(i, (i + by) % n) for i in range(n)])


def swap_cores(array):
    n = lax.axis_size("dp")
    return lax.ppermute(array, "dp", [(i, i ^ 1) for i in range(n)])


def dot(a, b, ca, cb):
    return lax.dot_general(a, b, (((ca,), (cb,)), ((), ())), preferred_element_type=f32)


def pack_kernel(
    len_ref, dest_ref, slot_ref, act_ref, wqkv_ref, bias_ref, gain_ref, wout_ref,
    blob_ref, par_a_ref, par_b_ref, plan_ref, stage, sems, blob_sems,
):
    slots, _, n_dp = len_ref.shape
    n_shard = blob_ref.shape[0]
    inner = wout_ref.shape[1]
    me = lax.axis_index("dp")
    core = lax.rem(me, 2)
    for i in range(plan_ref.shape[0]):
        plan_ref[i] = 0 if LENS <= i < STAYS else -1
    for s in range(slots):
        live = len_ref[s, 0, me] > 0
        dest = dest_ref[s, 0, me]

        @pl.when(live & (dest == me))
        def _(s=s):
            b = slot_ref[s, 0, me]
            plan_ref[CODES + b] = s
            plan_ref[LENS + b] = len_ref[s, 0, me]
            plan_ref[STAYS + s] = b

        for d in range(1, MOVES + 1):
            @pl.when(live & (dest == lax.rem(me + d, n_dp)))
            def _(d=d, s=s):
                plan_ref[LEAVES + d] = s

    leaving = [
        pltpu.make_async_copy(
            act_ref.at[jnp.maximum(plan_ref[LEAVES + d], 0)], to, sems.at[d - 1]
        )
        for d, to in ((1, par_b_ref), (2, par_a_ref.at[0]), (3, par_a_ref.at[1]))
    ]
    for cp in leaving:
        cp.start()

    for c in range(2):
        @pl.when(core == c)
        def _(c=c):
            stage[:, 0 : 4 * HALF] = jnp.concatenate(
                [
                    wqkv_ref[:, g * inner + c * HALF : g * inner + (c + 1) * HALF].astype(f32)
                    for g in range(3)
                ]
                + [wout_ref[:, c * HALF : (c + 1) * HALF].astype(f32)],
                axis=1,
            ).astype(bf16)
    stage[:, 4 * HALF :] = jnp.zeros((stage.shape[0], stage.shape[1] - 4 * HALF), bf16)
    tail = jnp.concatenate(
        [
            jnp.pad(bias_ref[...].astype(f32), ((0, 0), (0, 128 - bias_ref.shape[1]))),
            jnp.pad(gain_ref[...].astype(f32), ((0, 0), (0, 128 - gain_ref.shape[1]))),
            jnp.zeros((14, 128), f32),
        ],
        axis=0,
    ).astype(bf16)
    stage[0:16, 4 * HALF :] = tail
    copies = [
        pltpu.make_async_copy(stage, blob_ref.at[s], blob_sems.at[s]) for s in range(n_shard)
    ]
    for cp in copies:
        cp.start()

    for d in range(1, MOVES + 1):
        row = lax.rem(me - d + n_dp, n_dp)
        for s in range(slots):
            @pl.when((len_ref[s, 0, row] > 0) & (dest_ref[s, 0, row] == me))
            def _(d=d, s=s, row=row):
                b = slot_ref[s, 0, row]
                plan_ref[CODES + b] = slots + d - 1
                plan_ref[LENS + b] = len_ref[s, 0, row]

    for cp in leaving:
        cp.wait()
    for cp in copies:
        cp.wait()


def pack(tables, act, wqkv, bias, gain, wout_t, n_shard):
    rows = wqkv.shape[0]
    cols = 4 * HALF + 128
    window = act.shape[1:]
    smem = pl.BlockSpec(memory_space=pltpu.SMEM)
    vmem = pl.BlockSpec(memory_space=pltpu.VMEM)
    hbm = pl.BlockSpec(memory_space=pl.ANY)
    return pl.pallas_call(
        pack_kernel,
        out_shape=(
            jax.ShapeDtypeStruct((n_shard, rows, cols), bf16),
            jax.ShapeDtypeStruct((2,) + window, bf16),
            jax.ShapeDtypeStruct(window, bf16),
            jax.ShapeDtypeStruct((PLAN,), jnp.int32),
        ),
        in_specs=[smem, smem, smem, hbm, vmem, vmem, vmem, vmem],
        out_specs=(hbm, vmem, vmem, smem),
        scratch_shapes=[
            pltpu.VMEM((rows, cols), bf16),
            pltpu.SemaphoreType.DMA((MOVES,)),
            pltpu.SemaphoreType.DMA((n_shard,)),
        ],
        compiler_params=pltpu.CompilerParams(vmem_limit_bytes=PACK_VMEM_LIMIT),
        name="pack_weights",
    )(*tables, act, wqkv, bias, gain, wout_t)


def block_kernel(
    plan_ref, act_ref, arr_a_ref, arr_b_ref, cot_ref, g_own, g_oth,
    out_ref, grad_ref, ret_c_ref, ret_d_ref, gt_own_ref, gt_oth_ref,
    xb, cotb, gbuf, zeros, bias_row, gain_row, nrm, ub, wqkv, wo, qkv, da, att, dproj, gt_own, gt_oth,
    win_sems, load_sems, out_sems,
):
    slots = act_ref.shape[0]
    kept = xb.shape[0]
    patches, ch = xb.shape[1:]
    n_shard, rows = g_own.shape[:2]
    tokens = kept * patches
    me = lax.axis_index("dp")
    core = lax.rem(me, 2)

    loads = [
        pltpu.make_async_copy(cot_ref, cotb, load_sems.at[0]),
    ]
    for cp in loads:
        cp.start()
    xb[...] = jnp.zeros(xb.shape, bf16)
    zeros[...] = jnp.zeros(zeros.shape, bf16)
    code = [plan_ref[CODES + b] for b in range(kept)]
    lens = [plan_ref[LENS + b] for b in range(kept)]
    arrived = [arr_b_ref.at[0], arr_a_ref.at[0], arr_b_ref.at[1]]
    for b in range(kept):
        @pl.when((code[b] >= 0) & (code[b] < slots))
        def _(b=b):
            pltpu.make_async_copy(act_ref.at[code[b]], xb.at[b], win_sems.at[b]).start()

        for d in range(MOVES):
            @pl.when(code[b] == slots + d)
            def _(b=b, d=d):
                pltpu.make_async_copy(arrived[d], xb.at[b], win_sems.at[b]).start()

    def zero_copy(s):
        return pltpu.make_async_copy(zeros, grad_ref.at[s], out_sems.at[s])

    for s in range(slots):
        @pl.when(plan_ref[STAYS + s] < 0)
        def _(s=s):
            zero_copy(s).start()

    returned = [ret_c_ref.at[0], ret_d_ref, ret_c_ref.at[1]]

    def ready(b):
        @pl.when((code[b] >= 0) & (code[b] < slots))
        def _():
            pltpu.make_async_copy(gbuf.at[b], grad_ref.at[code[b]], win_sems.at[b]).start()

        for d in range(MOVES):
            @pl.when(code[b] == slots + d)
            def _(d=d):
                pltpu.make_async_copy(gbuf.at[b], returned[d], win_sems.at[b]).start()

    for s in range(n_shard):
        tail = g_own[s, 0:16, 4 * HALF :].astype(f32)
        bias_row[0:1, 120 * s : 120 * s + 120] = tail[0:1, 0:120]
        gain_row[0:1, rows * s : rows * s + rows] = tail[1:2, 0:rows]
    pad = jnp.zeros((2 * rows, PADH - HALF), f32)
    for h, g in enumerate((g_own, g_oth)):
        for t in range(n_shard // 2):
            both = jnp.concatenate(
                [g[2 * t, :, 0 : 4 * HALF].astype(f32), g[2 * t + 1, :, 0 : 4 * HALF].astype(f32)],
                axis=0,
            )
            at = pl.ds(2 * rows * t, 2 * rows)
            for k in range(4):
                piece = jnp.concatenate(
                    [both[:, k * HALF : (k + 1) * HALF], pad], axis=1
                ).astype(bf16)
                if k < 3:
                    wqkv[at, (3 * h + k) * PADH : (3 * h + k + 1) * PADH] = piece
                else:
                    wo[at, h * PADH : (h + 1) * PADH] = piece

    bias = []
    for h in range(2):
        for k in range(3):
            low = bias_row[0:1, 2 * k * HALF : (2 * k + 1) * HALF]
            high = bias_row[0:1, (2 * k + 1) * HALF : (2 * k + 2) * HALF]
            first = core == h
            bias.append(jnp.where(first, low, high))
            bias.append(jnp.zeros((1, PADH - HALF), f32))
    bias = jnp.concatenate(bias, axis=1)

    loads[0].wait()
    position = lax.broadcasted_iota(jnp.int32, (patches, 1), 0)
    gain = gain_row[...]
    for b in range(kept):
        @pl.when(code[b] >= 0)
        def _(b=b):
            pltpu.make_async_copy(act_ref.at[0], xb.at[b], win_sems.at[b]).wait()

        x = xb[b].astype(f32)
        inv = lax.rsqrt(jnp.mean(x * x, axis=-1, keepdims=True) + EPS)
        at = pl.ds(b * patches, patches)
        nrm[at, :] = (x * inv * gain).astype(bf16)
        live = position < lens[b]
        ub[at, :] = jnp.where(live, cotb[b].astype(f32), 0.0).astype(bf16)

    qkv[...] = (dot(nrm[...], wqkv[...], 1, 0) + bias).astype(bf16)
    da[...] = dot(ub[...], wo[...], 1, 0).astype(bf16)

    head = HALF // 4
    scale = head ** (-0.5)
    lanes = (slice(0, 256), slice(128, 384))
    lane = lax.broadcasted_iota(jnp.int32, (patches, 256), 1)
    masks = []
    for i in range(4):
        low = i * head - lanes[i // 2].start
        masks.append(((lane >= low) & (lane < low + head)).astype(f32))
    low_masks = [m.astype(bf16) for m in masks]
    key_pos = lax.broadcasted_iota(jnp.int32, (patches, 2 * patches), 0)

    def by_head(m, g):
        return jnp.concatenate([m * low_masks[2 * g], m * low_masks[2 * g + 1]], axis=0)

    def joined(a, b):
        return jnp.concatenate([a[:, :128], a[:, 128:] + b[:, :128], b[:, 128:]], axis=1).astype(bf16)

    def stacked(m):
        return jnp.concatenate([m[:, :patches], m[:, patches:]], axis=0)

    def scored(w, h, g):
        at = pl.ds(w * patches, patches)
        base = 3 * h * PADH
        low = lanes[g].start
        q, k, v = [
            qkv[at, base + i * PADH + low : base + i * PADH + low + 256] for i in range(3)
        ]
        q_heads = by_head(q, g)
        d_heads = by_head(da[at, h * PADH + low : h * PADH + low + 256], g)
        return q_heads, d_heads, k, v, dot(k, q_heads, 1, 1), dot(v, d_heads, 1, 1)

    def softmaxed(w, h, g, q_heads, d_heads, k, v, scores, d_probs):
        allowed = key_pos < jnp.maximum(lens[w], 1)
        weights = jnp.where(allowed, jnp.exp(scores * scale), 0.0)
        probs = weights * (1.0 / jnp.sum(weights, axis=0, keepdims=True))
        d_probs = d_probs.astype(bf16).astype(f32)
        mean = jnp.sum(d_probs * probs, axis=0, keepdims=True)
        d_scores = (probs * (d_probs - mean) * scale).astype(bf16)
        return q_heads, d_heads, k, v, probs.astype(bf16), d_scores

    def combined(w, h, g, q_heads, d_heads, k, v, probs, d_scores):
        return (
            dot(stacked(probs), by_head(v, g), 0, 0),
            dot(stacked(d_scores), by_head(k, g), 0, 0),
            dot(d_scores, q_heads, 1, 0),
            dot(probs, d_heads, 1, 0),
        )

    def stored(w, h, first, second):
        at = pl.ds(w * patches, patches)
        base = 3 * h * PADH
        o, dq, dk, dv = [joined(x, y) for x, y in zip(first, second)]
        att[at, h * PADH : (h + 1) * PADH] = o
        dproj[at, base : base + PADH] = dq
        dproj[at, base + PADH : base + 2 * PADH] = dk
        dproj[at, base + 2 * PADH : base + 3 * PADH] = dv

    todo = [(w, h, g) for w in range(kept) for h in range(2) for g in range(2)]
    step = 14
    for first in range(0, len(todo), step):
        some = todo[first : first + step]
        state = [scored(*p) for p in some]
        state = [softmaxed(*p, *c) for p, c in zip(some, state)]
        state = [combined(*p, *c) for p, c in zip(some, state)]
        for i in range(0, len(some), 2):
            stored(some[i][0], some[i][1], state[i], state[i + 1])

    attended = att[...]
    gt = dot(ub[...], attended, 0, 0)
    gt_own[...] = gt[:, 0:HALF]
    gt_oth[...] = gt[:, PADH : PADH + HALF].astype(bf16)
    done = [
        pltpu.make_async_copy(gt_oth, gt_oth_ref, load_sems.at[0]),
        pltpu.make_async_copy(gt_own, gt_own_ref, load_sems.at[1]),
    ]
    for cp in done:
        cp.start()
    added = dot(attended, wo[...], 1, 1)
    for b in range(kept):
        at = slice(b * patches, (b + 1) * patches)
        live = position < lens[b]
        cotb[b] = jnp.where(live, xb[b].astype(f32) + added[at], 0.0).astype(bf16)
    done.append(pltpu.make_async_copy(cotb, out_ref, load_sems.at[2]))
    done[2].start()
    d_nrm = dot(dproj[...], wqkv[...], 1, 1)
    for b in range(kept):
        at = slice(b * patches, (b + 1) * patches)
        x = xb[b].astype(f32)
        inv = lax.rsqrt(jnp.mean(x * x, axis=-1, keepdims=True) + EPS)
        t = d_nrm[at].astype(bf16).astype(f32) * gain
        along = jnp.mean(t * x, axis=-1, keepdims=True)
        dx = t * inv - x * (inv * inv * inv * along)
        gbuf[b] = (ub[at, :].astype(f32) + dx).astype(bf16)
        ready(b)

    for b in range(kept):
        @pl.when(code[b] >= 0)
        def _(b=b):
            pltpu.make_async_copy(gbuf.at[b], grad_ref.at[0], win_sems.at[b]).wait()
    for s in range(slots):
        @pl.when(plan_ref[STAYS + s] < 0)
        def _(s=s):
            zero_copy(s).wait()
    for cp in done:
        cp.wait()


def block(plan, act, arr_a, arr_b, cot, own, oth):
    kept, patches, ch = cot.shape
    slots = act.shape[0]
    tokens = kept * patches
    smem = pl.BlockSpec(memory_space=pltpu.SMEM)
    vmem = pl.BlockSpec(memory_space=pltpu.VMEM)
    hbm = pl.BlockSpec(memory_space=pl.ANY)
    window = (patches, ch)
    return pl.pallas_call(
        block_kernel,
        out_shape=(
            jax.ShapeDtypeStruct(cot.shape, bf16),
            jax.ShapeDtypeStruct(act.shape, bf16),
            jax.ShapeDtypeStruct((2,) + window, bf16),
            jax.ShapeDtypeStruct(window, bf16),
            jax.ShapeDtypeStruct((ch, HALF), f32),
            jax.ShapeDtypeStruct((ch, HALF), bf16),
        ),
        in_specs=[smem] + [hbm] * 4 + [vmem] * 2,
        out_specs=(hbm,) * 6,
        scratch_shapes=[
            pltpu.VMEM(cot.shape, bf16),
            pltpu.VMEM(cot.shape, bf16),
            pltpu.VMEM(cot.shape, bf16),
            pltpu.VMEM(window, bf16),
            pltpu.VMEM((1, 6 * HALF), f32),
            pltpu.VMEM((1, ch), f32),
            pltpu.VMEM((tokens, ch), bf16),
            pltpu.VMEM((tokens, ch), bf16),
            pltpu.VMEM((ch, 6 * PADH), bf16),
            pltpu.VMEM((ch, 2 * PADH), bf16),
            pltpu.VMEM((tokens, 6 * PADH), bf16),
            pltpu.VMEM((tokens, 2 * PADH), bf16),
            pltpu.VMEM((tokens, 2 * PADH), bf16),
            pltpu.VMEM((tokens, 6 * PADH), bf16),
            pltpu.VMEM((ch, HALF), f32),
            pltpu.VMEM((ch, HALF), bf16),
            pltpu.SemaphoreType.DMA((kept,)),
            pltpu.SemaphoreType.DMA((3,)),
            pltpu.SemaphoreType.DMA((slots,)),
        ],
        compiler_params=pltpu.CompilerParams(vmem_limit_bytes=VMEM_LIMIT),
        name="window_block",
    )(plan, act, arr_a, arr_b, cot, own, oth)


def finish_kernel(
    plan_ref, parts_ref, back_c_ref, back_d_ref, grad_in_ref, grad_ref, total_ref, sems
):
    back = [back_c_ref.at[0], back_d_ref.at[0], back_d_ref.at[1]]
    copies = []
    for d in range(MOVES):
        s = plan_ref[LEAVES + d + 1]
        cp = pltpu.make_async_copy(back[d], grad_ref.at[jnp.maximum(s, 0)], sems.at[d])
        copies.append((s >= 0, cp))
    for moved, cp in copies:
        @pl.when(moved)
        def _(cp=cp):
            cp.start()

    n = parts_ref.shape[0]
    halves = []
    for c in range(2):
        total = parts_ref[c].astype(f32)
        for z in range(1, n // 2):
            total = total + parts_ref[2 * z + c].astype(f32)
        halves.append(total)
    total_ref[...] = jnp.concatenate(halves, axis=1)
    for moved, cp in copies:
        @pl.when(moved)
        def _(cp=cp):
            cp.wait()


def finish(plan, parts, back_c, back_d, grad):
    n, rows, half = parts.shape
    smem = pl.BlockSpec(memory_space=pltpu.SMEM)
    vmem = pl.BlockSpec(memory_space=pltpu.VMEM)
    hbm = pl.BlockSpec(memory_space=pl.ANY)
    return pl.pallas_call(
        finish_kernel,
        out_shape=(
            jax.ShapeDtypeStruct(grad.shape, bf16),
            jax.ShapeDtypeStruct((rows, 2 * half), f32),
        ),
        in_specs=[smem, vmem, vmem, vmem, hbm],
        out_specs=(hbm, vmem),
        scratch_shapes=[pltpu.SemaphoreType.DMA((MOVES,))],
        input_output_aliases={4: 0},
        compiler_params=pltpu.CompilerParams(vmem_limit_bytes=VMEM_LIMIT),
        name="finish",
    )(plan, parts, back_c, back_d, grad)


def shards(
    activations, cotangent, window_len, move_dest, move_slot, w_qkv, b_qkv, norm_gain, w_out
):
    n_shard = lax.axis_size("shard")
    rows = w_qkv.shape[0]
    tables = [t.transpose(2, 1, 0) for t in (window_len, move_dest, move_slot)]
    blob, par_a, par_b, plan = pack(
        tables, activations, w_qkv, b_qkv[None], norm_gain[None], w_out.T, n_shard
    )
    arr_a = permute_dp(par_a, 2)
    own = lax.all_to_all(blob, "shard", 0, 0)
    arr_b = permute_dp(jnp.stack([par_b, arr_a[1]]), 1)
    own, arr_b = lax.optimization_barrier((own, arr_b))
    oth = swap_cores(own)
    out, grad, ret_c, ret_d, gt_own, gt_oth = block(
        plan, activations, arr_a, arr_b, cotangent, own, oth
    )
    gt_in = swap_cores(gt_oth)
    back_c = permute_dp(ret_c, -1)
    share = (gt_own + gt_in.astype(f32)).astype(bf16).reshape(n_shard, rows, HALF)
    chunks = lax.all_to_all(share, "shard", 0, 0)
    summed = jnp.sum(chunks.astype(f32), axis=0).astype(bf16)
    back_d = permute_dp(jnp.stack([ret_d, back_c[1]]), -2)
    parts = lax.all_gather(summed, "dp", axis=0)
    grad_input, total = finish(plan, parts, back_c, back_d, grad)
    return (out, grad_input, total.T)


def solution(mesh):
    return jax.shard_map(
        shards,
        mesh=mesh,
        in_specs=(
            P(("dp", "shard"), None, None),
            P(("dp", "shard"), None, None),
            P(None, "shard", None),
            P(None, "shard", None),
            P(None, "shard", None),
            P("shard", None),
            P("shard"),
            P("shard"),
            P(None, "shard"),
        ),
        out_specs=(
            P(("dp", "shard"), None, None),
            P(("dp", "shard"), None, None),
            P(None, "shard"),
        ),
        check_vma=False,
    )
```

time: 161 us -> 119 us (0.74)
  the two profiles are of different devices: /device:TPU:11 before, /device:TPU:1 now
where the time goes in v2:
time: 119 us
  starting transfers between devices  36.9 us (31%)
  blocking collectives  32.3 us (27%)
  waiting for transfers between devices  29.2 us (25%)
  Pallas kernels  17.8 us (15%)
  other arithmetic  1.91 us (2%)
    all_gather x1, blocking collectives, shards(): parts = lax.all_gather(summed, 'dp', axis=0)  32.3 us
    ppermute x4, waiting for transfers between devices, permute_dp(): return lax.ppermute(array, 'dp', [(i, (i + by) % n) for i in range(n)])  19.3 us
    ppermute x4, starting transfers between devices, permute_dp(): return lax.ppermute(array, 'dp', [(i, (i + by) % n) for i in range(n)])  16.2 us
    pallas_call x1, Pallas kernels, block(): pl.pallas_call(block_kernel, out_shape=(jax.ShapeDtypeStruct(cot.shape, b...  12.9 us
    ppermute x2, starting transfers between devices, swap_cores(): return lax.ppermute(array, 'dp', [(i, i ^ 1) for i in range(n)])  8.77 us
    all_to_all x1, starting transfers between devices, shards(): own = lax.all_to_all(blob, 'shard', 0, 0)  7.73 us
    ppermute x2, waiting for transfers between devices, swap_cores(): return lax.ppermute(array, 'dp', [(i, i ^ 1) for i in range(n)])  5.04 us
    all_to_all x1, waiting for transfers between devices, shards(): own = lax.all_to_all(blob, 'shard', 0, 0)  4.84 us
  transfers between devices with their start and end apart: 8, of which 6 were waited for; matrix products, arithmetic and copies ran while one was open for 1% of the time, Pallas kernels for 0%

profile of v2, /device:TPU:1, one launch (start us, length us, event | category | flops | bytes accessed | tf_op | source)
XLA Modules:
  0.0 119.0 jit_solution(16025938646715777334)
XLA Ops:
  0.6 3.6 %pack_weights.1 = (bf16[16,40,1408]{2,1,0:T(8,128)(2,1)}, bf16[2,64,640]{2,1,0:T(8,128)(2,1)}, bf16[64,640]{1,0:T(8,128)(2,1)}, s32[64]{0:T(128)}) custom-call(s32[10,1,32]{2,1,0:T(1,128)} %bitcast.15, s32[10,1,32]{2,1,0:T(1,128)} %bitcast.16, s32[10,1,32]{2,1,0:T(1,128)} %bitcast.17, bf16[10,64,640]{2,1,0:T(8,128)(2,1)} %act_ref.3, ...), custom_call_target="tpu_custom_call" | custom-call | tf_op jit(solution)/shard_map/pack_weights/pallas_call | solution.py:122
  4.2 0.0 copy-start.5
  4.2 0.0 copy-start
  4.2 0.0 copy-start.1
  4.2 0.0 copy-start.3
  4.2 7.7 %all-to-all-start = ((bf16[16,40,1408]{2,1,0:T(8,128)(2,1)}), bf16[16,40,1408]{2,1,0:T(8,128)(2,1)S(1)}, u32[]{:S(2)}, u32[]{:S(2)}) async-start(bf16[16,40,1408]{2,1,0:T(8,128)(2,1)} %get-tuple-element.19), calls=%async_computation | async-start | bytes 3604480 | tf_op jit(solution)/shard_map/all_to_all | solution.py:456
  12.0 3.5 %collective-permute-start = (bf16[2,64,640]{2,1,0:T(8,128)(2,1)}, bf16[2,64,640]{2,1,0:T(8,128)(2,1)S(1)}, u32[]{:S(2)}, u32[]{:S(2)}) collective-permute-start(bf16[2,64,640]{2,1,0:T(8,128)(2,1)} %get-tuple-element.18), channel_id=1, source_target_pairs={{0,32},{16,48},{32,64},{48,80},{64,96},{80,112},{96,128},{112,144}... | collective-permute-start | bytes 491528 | tf_op jit(solution)/shard_map/ppermute | solution.py:25
  15.5 11.4 %collective-permute-done.arr_a_ref = bf16[2,64,640]{2,1,0:T(8,128)(2,1)S(1)} collective-permute-done((bf16[2,64,640]{2,1,0:T(8,128)(2,1)}, bf16[2,64,640]{2,1,0:T(8,128)(2,1)S(1)}, u32[]{:S(2)}, u32[]{:S(2)}) %collective-permute-start) | collective-permute-done | bytes 163872 | tf_op jit(solution)/shard_map/ppermute | solution.py:25
  26.9 0.0 copy-done.5
  27.0 0.0 collective-permute-start.1
  27.0 2.4 %collective-permute-done.1.arr_b_ref = bf16[2,64,640]{2,1,0:T(8,128)(2,1)S(1)} collective-permute-done((bf16[2,64,640]{2,1,0:T(8,128)(2,1)S(1)}, bf16[2,64,640]{2,1,0:T(8,128)(2,1)S(1)}, u32[]{:S(2)}, u32[]{:S(2)}) %collective-permute-start.1) | collective-permute-done | bytes 163872 | tf_op jit(solution)/shard_map/ppermute | solution.py:25
  29.4 4.8 %all-to-all-done.g_own = bf16[16,40,1408]{2,1,0:T(8,128)(2,1)S(1)} async-done(((bf16[16,40,1408]{2,1,0:T(8,128)(2,1)}), bf16[16,40,1408]{2,1,0:T(8,128)(2,1)S(1)}, u32[]{:S(2)}, u32[]{:S(2)}) %all-to-all-start) | async-done | bytes 1802272 | tf_op jit(solution)/shard_map/all_to_all | solution.py:456
  34.3 6.7 %collective-permute-start.2 = (bf16[16,40,1408]{2,1,0:T(8,128)(2,1)S(1)}, bf16[16,40,1408]{2,1,0:T(8,128)(2,1)S(1)}, u32[]{:S(2)}, u32[]{:S(2)}) collective-permute-start(bf16[16,40,1408]{2,1,0:T(8,128)(2,1)S(1)} %all-to-all-done.g_own), channel_id=1, source_target_pairs={{0,16},{16,0},{32,48},{48,32},{64,80},{80,64},{96,112},{112,96},{1... | collective-permute-start | bytes 5406728 | tf_op jit(solution)/shard_map/ppermute | solution.py:30
  41.0 3.3 %collective-permute-done.2.g_oth = bf16[16,40,1408]{2,1,0:T(8,128)(2,1)S(1)} collective-permute-done((bf16[16,40,1408]{2,1,0:T(8,128)(2,1)S(1)}, bf16[16,40,1408]{2,1,0:T(8,128)(2,1)S(1)}, u32[]{:S(2)}, u32[]{:S(2)}) %collective-permute-start.2) | collective-permute-done | bytes 1802272 | tf_op jit(solution)/shard_map/ppermute | solution.py:30
  44.3 0.0 copy-done
  44.3 0.0 copy-done.1
  44.3 0.0 copy-done.3
  44.3 12.9 %window_block.1 = (bf16[7,64,640]{2,1,0:T(8,128)(2,1)}, bf16[10,64,640]{2,1,0:T(8,128)(2,1)}, bf16[2,64,640]{2,1,0:T(8,128)(2,1)S(1)}, bf16[64,640]{1,0:T(8,128)...) custom-call(s32[64]{0:T(128)S(1)} %copy-done.3, bf16[10,64,640]{2,1,0:T(8,128)(2,1)S(1)} %copy-done, ...), custom_call_target="tpu_custom_call" | custom-call | tf_op jit(solution)/shard_map/window_block/pallas_call | solution.py:360
  57.2 0.0 copy-start.2
  57.3 0.0 copy-start.4
  57.3 2.1 %collective-permute-start.3 = (bf16[640,320]{1,0:T(8,128)(2,1)S(1)}, bf16[640,320]{1,0:T(8,128)(2,1)S(1)}, u32[]{:S(2)}, u32[]{:S(2)}) collective-permute-start(bf16[640,320]{1,0:T(8,128)(2,1)S(1)} %get-tuple-element.25), channel_id=1, source_target_pairs={{0,16},{16,0},{32,48},{48,32},{64,80},{80,64},{96,112},{112,96},{1... | collective-permute-start | bytes 1228808 | tf_op jit(solution)/shard_map/ppermute | solution.py:30
  59.3 1.7 %collective-permute-done.3 = bf16[640,320]{1,0:T(8,128)(2,1)S(1)} collective-permute-done((bf16[640,320]{1,0:T(8,128)(2,1)S(1)}, bf16[640,320]{1,0:T(8,128)(2,1)S(1)}, u32[]{:S(2)}, u32[]{:S(2)}) %collective-permute-start.3) | collective-permute-done | bytes 409632 | tf_op jit(solution)/shard_map/ppermute | solution.py:30
  61.0 0.9 add_convert_fusion
  61.9 0.0 copy-done.2
  61.9 0.0 copy-done.4
  61.9 4.2 %all-to-all-start.1 = ((bf16[16,40,320]{2,1,0:T(8,128)(2,1)}), bf16[16,40,320]{2,1,0:T(8,128)(2,1)S(1)}, u32[]{:S(2)}, u32[]{:S(2)}) async-start(bf16[16,40,320]{2,1,0:T(8,128)(2,1)} %bitcast.7), calls=%async_computation.1 | async-start | bytes 983040 | tf_op jit(solution)/shard_map/all_to_all | solution.py:466
  66.2 0.4 collective-permute-start.4
  66.6 5.5 %collective-permute-done.4.back_c_ref = bf16[2,64,640]{2,1,0:T(8,128)(2,1)S(1)} collective-permute-done((bf16[2,64,640]{2,1,0:T(8,128)(2,1)}, bf16[2,64,640]{2,1,0:T(8,128)(2,1)S(1)}, u32[]{:S(2)}, u32[]{:S(2)}) %collective-permute-start.4) | collective-permute-done | bytes 163872 | tf_op jit(solution)/shard_map/ppermute | solution.py:25
  72.1 0.9 pad_maximum_fusion.1
  73.1 12.2 %collective-permute-start.5 = (bf16[2,64,640]{2,1,0:T(8,128)(2,1)S(1)}, bf16[2,64,640]{2,1,0:T(8,128)(2,1)S(1)}, u32[]{:S(2)}, u32[]{:S(2)}) collective-permute-start(bf16[2,64,640]{2,1,0:T(8,128)(2,1)S(1)} %pad_maximum_fusion.1), channel_id=1, source_target_pairs={{0,480},{16,496},{32,0},{48,16},{64,32},{80,48},{96,64},{112,80},{... | collective-permute-start | bytes 491528 | tf_op jit(solution)/shard_map/ppermute | solution.py:25
  85.2 0.0 all-to-all-done.1
  85.2 0.1 reduce_sum.12
  85.3 32.3 %all-gather = bf16[1280,320]{1,0:T(8,128)(2,1)S(1)} all-gather(bf16[40,320]{1,0:T(8,128)(2,1)S(1)} %reduce_sum.12), channel_id=2, replica_groups=mesh['dp'=32,'shard'=16] {'dp'}, dimensions={0}, use_global_device_ids=true | all-gather | bytes 844800 | tf_op jit(solution)/shard_map/all_gather | solution.py:469
  117.6 0.0 collective-permute-done.5.back_d_ref
  117.6 1.3 %finish.1 = (bf16[10,64,640]{2,1,0:T(8,128)(2,1)}, f32[40,640]{1,0:T(8,128)}) custom-call(s32[64]{0:T(128)S(1)} %copy-done.3, bf16[32,40,320]{2,1,0:T(8,128)(2,1)S(1)} %bitcast.11, bf16[2,64,640]{2,1,0:T(8,128)(2,1)S(1)} %collective-permute-done.4.back_c_ref, ...), custom_call_target="tpu_custom_call", output_to_operand_aliasing={{0}: (4, {})} | custom-call | tf_op jit(solution)/shard_map/finish/pallas_call | solution.py:431
  (3 shorter events, 0.0 us)
Async XLA Ops:
  4.2 22.7 %copy-start.5 = (bf16[64,640]{1,0:T(8,128)(2,1)S(1)}, bf16[64,640]{1,0:T(8,128)(2,1)}, u32[]{:S(2)}) copy-start(bf16[64,640]{1,0:T(8,128)(2,1)} %get-tuple-element.20) | copy-start | bytes 245764
  4.2 40.1 %copy-start = (bf16[10,64,640]{2,1,0:T(8,128)(2,1)S(1)}, bf16[10,64,640]{2,1,0:T(8,128)(2,1)}, u32[]{:S(2)}) copy-start(bf16[10,64,640]{2,1,0:T(8,128)(2,1)} %act_ref.3) | copy-start | bytes 2457604
  4.2 40.1 %copy-start.1 = (bf16[7,64,640]{2,1,0:T(8,128)(2,1)S(1)}, bf16[7,64,640]{2,1,0:T(8,128)(2,1)}, u32[]{:S(2)}) copy-start(bf16[7,64,640]{2,1,0:T(8,128)(2,1)} %cot_ref.1) | copy-start | bytes 1720324
  4.2 40.1 %copy-start.3 = (s32[64]{0:T(128)S(1)}, s32[64]{0:T(128)}, u32[]{:S(2)}) copy-start(s32[64]{0:T(128)} %get-tuple-element.17.plan_ref) | copy-start | bytes 772
  4.2 30.0 %all-to-all-start = ((bf16[16,40,1408]{2,1,0:T(8,128)(2,1)}), bf16[16,40,1408]{2,1,0:T(8,128)(2,1)S(1)}, u32[]{:S(2)}, u32[]{:S(2)}) async-start(bf16[16,40,1408]{2,1,0:T(8,128)(2,1)} %get-tuple-element.19), calls=%async_computation | async-start | bytes 3604480 | tf_op jit(solution)/shard_map/all_to_all | solution.py:456
  12.0 14.9 %collective-permute-start = (bf16[2,64,640]{2,1,0:T(8,128)(2,1)}, bf16[2,64,640]{2,1,0:T(8,128)(2,1)S(1)}, u32[]{:S(2)}, u32[]{:S(2)}) collective-permute-start(bf16[2,64,640]{2,1,0:T(8,128)(2,1)} %get-tuple-element.18), channel_id=1, source_target_pairs={{0,32},{16,48},{32,64},{48,80},{64,96},{80,112},{96,128},{112,144}... | collective-permute-start | bytes 491528 | tf_op jit(solution)/shard_map/ppermute | solution.py:25
  27.0 2.4 %collective-permute-start.1 = (bf16[2,64,640]{2,1,0:T(8,128)(2,1)S(1)}, bf16[2,64,640]{2,1,0:T(8,128)(2,1)S(1)}, u32[]{:S(2)}, u32[]{:S(2)}) collective-permute-start(bf16[2,64,640]{2,1,0:T(8,128)(2,1)S(1)} %pad_maximum_fusion), channel_id=1, source_target_pairs={{0,16},{16,32},{32,48},{48,64},{64,80},{80,96},{96,112},{112,128},... | collective-permute-start | bytes 491528 | tf_op jit(solution)/shard_map/ppermute | solution.py:25
  34.3 10.1 %collective-permute-start.2 = (bf16[16,40,1408]{2,1,0:T(8,128)(2,1)S(1)}, bf16[16,40,1408]{2,1,0:T(8,128)(2,1)S(1)}, u32[]{:S(2)}, u32[]{:S(2)}) collective-permute-start(bf16[16,40,1408]{2,1,0:T(8,128)(2,1)S(1)} %all-to-all-done.g_own), channel_id=1, source_target_pairs={{0,16},{16,0},{32,48},{48,32},{64,80},{80,64},{96,112},{112,96},{1... | collective-permute-start | bytes 5406728 | tf_op jit(solution)/shard_map/ppermute | solution.py:30
  57.2 4.7 %copy-start.2 = (bf16[64,640]{1,0:T(8,128)(2,1)}, bf16[64,640]{1,0:T(8,128)(2,1)S(1)}, u32[]{:S(2)}) copy-start(bf16[64,640]{1,0:T(8,128)(2,1)S(1)} %get-tuple-element.27) | copy-start | bytes 245764
  57.3 4.7 %copy-start.4 = (bf16[2,64,640]{2,1,0:T(8,128)(2,1)}, bf16[2,64,640]{2,1,0:T(8,128)(2,1)S(1)}, u32[]{:S(2)}) copy-start(bf16[2,64,640]{2,1,0:T(8,128)(2,1)S(1)} %get-tuple-element.26) | copy-start | bytes 491524
  57.3 3.8 %collective-permute-start.3 = (bf16[640,320]{1,0:T(8,128)(2,1)S(1)}, bf16[640,320]{1,0:T(8,128)(2,1)S(1)}, u32[]{:S(2)}, u32[]{:S(2)}) collective-permute-start(bf16[640,320]{1,0:T(8,128)(2,1)S(1)} %get-tuple-element.25), channel_id=1, source_target_pairs={{0,16},{16,0},{32,48},{48,32},{64,80},{80,64},{96,112},{112,96},{1... | collective-permute-start | bytes 1228808 | tf_op jit(solution)/shard_map/ppermute | solution.py:30
  61.9 23.3 %all-to-all-start.1 = ((bf16[16,40,320]{2,1,0:T(8,128)(2,1)}), bf16[16,40,320]{2,1,0:T(8,128)(2,1)S(1)}, u32[]{:S(2)}, u32[]{:S(2)}) async-start(bf16[16,40,320]{2,1,0:T(8,128)(2,1)} %bitcast.7), calls=%async_computation.1 | async-start | bytes 983040 | tf_op jit(solution)/shard_map/all_to_all | solution.py:466
  66.2 6.0 %collective-permute-start.4 = (bf16[2,64,640]{2,1,0:T(8,128)(2,1)}, bf16[2,64,640]{2,1,0:T(8,128)(2,1)S(1)}, u32[]{:S(2)}, u32[]{:S(2)}) collective-permute-start(bf16[2,64,640]{2,1,0:T(8,128)(2,1)} %copy-done.4), channel_id=1, source_target_pairs={{0,496},{16,0},{32,16},{48,32},{64,48},{80,64},{96,80},{112,96},{1... | collective-permute-start | bytes 491528 | tf_op jit(solution)/shard_map/ppermute | solution.py:25
  73.1 44.6 %collective-permute-start.5 = (bf16[2,64,640]{2,1,0:T(8,128)(2,1)S(1)}, bf16[2,64,640]{2,1,0:T(8,128)(2,1)S(1)}, u32[]{:S(2)}, u32[]{:S(2)}) collective-permute-start(bf16[2,64,640]{2,1,0:T(8,128)(2,1)S(1)} %pad_maximum_fusion.1), channel_id=1, source_target_pairs={{0,480},{16,496},{32,0},{48,16},{64,32},{80,48},{96,64},{112,80},{... | collective-permute-start | bytes 491528 | tf_op jit(solution)/shard_map/ppermute | solution.py:25

commit v3 on v2

v3 whole, which is shorter than its diff:
```python
import functools

import jax
import jax.numpy as jnp
from jax import lax
from jax.experimental import pallas as pl
from jax.experimental.pallas import tpu as pltpu
from jax.sharding import PartitionSpec as P

HEADS = 8
MOVES = 3
EPS = 1e-06
HALF = 320
PADH = 384
LANES = 128
CODES, LENS, STAYS, LEAVES, PLAN = 0, 16, 32, 48, 64
VMEM_LIMIT = 40 * 1024 * 1024
PACK_VMEM_LIMIT = 60 * 1024 * 1024

f32 = jnp.float32
bf16 = jnp.bfloat16


def permute_dp(array, by):
    n = lax.axis_size("dp")
    return lax.ppermute(array, "dp", [(i, (i + by) % n) for i in range(n)])


def swap_cores(array):
    n = lax.axis_size("dp")
    return lax.ppermute(array, "dp", [(i, i ^ 1) for i in range(n)])


def dot(a, b, ca, cb):
    return lax.dot_general(a, b, (((ca,), (cb,)), ((), ())), preferred_element_type=f32)


def tiles_of(groups):
    full = [g[:, t * LANES : (t + 1) * LANES] for g in groups for t in range(2)]
    half = [g[:, 2 * LANES : HALF] for g in groups]
    return full + [
        jnp.concatenate(half[0:2], axis=1),
        jnp.concatenate(half[2:4], axis=1),
    ]


def groups_of(tiles, rows):
    at = [tiles[t * rows : (t + 1) * rows] for t in range(10)]
    pad = jnp.zeros((rows, LANES // 2), f32)
    groups = []
    for g in range(4):
        both = at[8 + g // 2]
        half = both[:, (g % 2) * (LANES // 2) : (g % 2 + 1) * (LANES // 2)]
        groups.append(jnp.concatenate([at[2 * g], at[2 * g + 1], half, pad], axis=1))
    return groups


def share_tiles(x):
    low = x[0:24, 2 * LANES : HALF]
    high = jnp.concatenate([x[24:40, 2 * LANES : HALF], jnp.zeros((8, LANES // 2), f32)], axis=0)
    return jnp.concatenate(
        [x[:, 0:LANES], x[:, LANES : 2 * LANES], jnp.concatenate([low, high], axis=1)], axis=0
    )


def share_block(t):
    half = jnp.concatenate([t[80:104, 0 : LANES // 2], t[80:96, LANES // 2 :]], axis=0)
    return jnp.concatenate([t[0:40], t[40:80], half], axis=1)


SHARE = (104, LANES)


def pack_kernel(
    len_ref, dest_ref, slot_ref, act_ref, wqkv_ref, bias_ref, gain_ref, wout_ref,
    blob_ref, par_a_ref, par_b_ref, plan_ref, stage, sems, blob_sems,
):
    slots, _, n_dp = len_ref.shape
    n_shard = blob_ref.shape[0]
    inner = wout_ref.shape[1]
    me = lax.axis_index("dp")
    core = lax.rem(me, 2)
    for i in range(plan_ref.shape[0]):
        plan_ref[i] = 0 if LENS <= i < STAYS else -1
    for s in range(slots):
        live = len_ref[s, 0, me] > 0
        dest = dest_ref[s, 0, me]

        @pl.when(live & (dest == me))
        def _(s=s):
            b = slot_ref[s, 0, me]
            plan_ref[CODES + b] = s
            plan_ref[LENS + b] = len_ref[s, 0, me]
            plan_ref[STAYS + s] = b

        for d in range(1, MOVES + 1):
            @pl.when(live & (dest == lax.rem(me + d, n_dp)))
            def _(d=d, s=s):
                plan_ref[LEAVES + d] = s

    leaving = [
        pltpu.make_async_copy(
            act_ref.at[jnp.maximum(plan_ref[LEAVES + d], 0)], to, sems.at[d - 1]
        )
        for d, to in ((1, par_b_ref), (2, par_a_ref.at[0]), (3, par_a_ref.at[1]))
    ]
    for cp in leaving:
        cp.start()

    tail = [
        jnp.pad(r[...].astype(f32), ((0, 0), (0, LANES - r.shape[1])))
        for r in (bias_ref, gain_ref)
    ] + [jnp.zeros((6, LANES), f32)]
    for c in range(2):
        @pl.when(core == c)
        def _(c=c):
            groups = [
                wqkv_ref[:, g * inner + c * HALF : g * inner + (c + 1) * HALF].astype(f32)
                for g in range(3)
            ] + [wout_ref[:, c * HALF : (c + 1) * HALF].astype(f32)]
            stage[...] = jnp.concatenate(tiles_of(groups) + tail, axis=0).astype(bf16)
    copies = [
        pltpu.make_async_copy(stage, blob_ref.at[s], blob_sems.at[s]) for s in range(n_shard)
    ]
    for cp in copies:
        cp.start()

    for d in range(1, MOVES + 1):
        row = lax.rem(me - d + n_dp, n_dp)
        for s in range(slots):
            @pl.when((len_ref[s, 0, row] > 0) & (dest_ref[s, 0, row] == me))
            def _(d=d, s=s, row=row):
                b = slot_ref[s, 0, row]
                plan_ref[CODES + b] = slots + d - 1
                plan_ref[LENS + b] = len_ref[s, 0, row]

    for cp in leaving:
        cp.wait()
    for cp in copies:
        cp.wait()


def pack(tables, act, wqkv, bias, gain, wout_t, n_shard):
    rows = wqkv.shape[0]
    block_rows = 10 * rows + 8
    window = act.shape[1:]
    smem = pl.BlockSpec(memory_space=pltpu.SMEM)
    vmem = pl.BlockSpec(memory_space=pltpu.VMEM)
    hbm = pl.BlockSpec(memory_space=pl.ANY)
    return pl.pallas_call(
        pack_kernel,
        out_shape=(
            jax.ShapeDtypeStruct((n_shard, block_rows, LANES), bf16),
            jax.ShapeDtypeStruct((2,) + window, bf16),
            jax.ShapeDtypeStruct(window, bf16),
            jax.ShapeDtypeStruct((PLAN,), jnp.int32),
        ),
        in_specs=[smem, smem, smem, hbm, vmem, vmem, vmem, vmem],
        out_specs=(hbm, vmem, vmem, smem),
        scratch_shapes=[
            pltpu.VMEM((block_rows, LANES), bf16),
            pltpu.SemaphoreType.DMA((MOVES,)),
            pltpu.SemaphoreType.DMA((n_shard,)),
        ],
        compiler_params=pltpu.CompilerParams(vmem_limit_bytes=PACK_VMEM_LIMIT),
        name="pack_weights",
    )(*tables, act, wqkv, bias, gain, wout_t)


def unpack_weights(g, wqkv, wo, bias_row, gain_row):
    n_shard = g.shape[0]
    rows = g.shape[1] // 10
    for s in range(n_shard):
        tail = g[s].astype(f32)[10 * rows :]
        bias_row[0:1, 3 * rows * s : 3 * rows * (s + 1)] = tail[0:1, 0 : 3 * rows]
        gain_row[0:1, rows * s : rows * (s + 1)] = tail[1:2, 0:rows]
    for t in range(n_shard // 2):
        pair = [groups_of(g[2 * t + i].astype(f32), rows) for i in range(2)]
        at = pl.ds(2 * rows * t, 2 * rows)
        for k in range(4):
            piece = jnp.concatenate([pair[0][k], pair[1][k]], axis=0).astype(bf16)
            if k < 3:
                wqkv[at, k * PADH : (k + 1) * PADH] = piece
            else:
                wo[at, :] = piece


def bias_of(bias_row, low_half):
    parts = []
    for k in range(3):
        low = bias_row[0:1, 2 * k * HALF : (2 * k + 1) * HALF]
        high = bias_row[0:1, (2 * k + 1) * HALF : (2 * k + 2) * HALF]
        parts += [jnp.where(low_half, low, high), jnp.zeros((1, PADH - HALF), f32)]
    return jnp.concatenate(parts, axis=1)


def attention(lens, patches, qkv, da, att, dproj):
    head = HALF // 4
    scale = head ** (-0.5)
    starts = (0, LANES)
    lane = lax.broadcasted_iota(jnp.int32, (patches, 2 * LANES), 1)
    masks = []
    for i in range(4):
        low = i * head - starts[i // 2]
        masks.append(((lane >= low) & (lane < low + head)).astype(f32).astype(bf16))
    key_pos = lax.broadcasted_iota(jnp.int32, (patches, 2 * patches), 0)

    def by_head(m, g):
        return jnp.concatenate([m * masks[2 * g], m * masks[2 * g + 1]], axis=0)

    def joined(a, b):
        return jnp.concatenate(
            [a[:, :LANES], a[:, LANES:] + b[:, :LANES], b[:, LANES:]], axis=1
        ).astype(bf16)

    def stacked(m):
        return jnp.concatenate([m[:, :patches], m[:, patches:]], axis=0)

    def scored(w, g):
        at = pl.ds(w * patches, patches)
        low = starts[g]
        q, k, v = [qkv[at, i * PADH + low : i * PADH + low + 2 * LANES] for i in range(3)]
        q_heads = by_head(q, g)
        d_heads = by_head(da[at, low : low + 2 * LANES], g)
        return q_heads, d_heads, k, v, dot(k, q_heads, 1, 1), dot(v, d_heads, 1, 1)

    def softmaxed(w, g, q_heads, d_heads, k, v, scores, d_probs):
        allowed = key_pos < jnp.maximum(lens[w], 1)
        weights = jnp.where(allowed, jnp.exp(scores * scale), 0.0)
        probs = weights * (1.0 / jnp.sum(weights, axis=0, keepdims=True))
        d_probs = d_probs.astype(bf16).astype(f32)
        mean = jnp.sum(d_probs * probs, axis=0, keepdims=True)
        d_scores = (probs * (d_probs - mean) * scale).astype(bf16)
        return q_heads, d_heads, k, v, probs.astype(bf16), d_scores

    def combined(w, g, q_heads, d_heads, k, v, probs, d_scores):
        return (
            dot(stacked(probs), by_head(v, g), 0, 0),
            dot(stacked(d_scores), by_head(k, g), 0, 0),
            dot(d_scores, q_heads, 1, 0),
            dot(probs, d_heads, 1, 0),
        )

    todo = [(w, g) for w in range(len(lens)) for g in range(2)]
    step = 14
    for first in range(0, len(todo), step):
        some = todo[first : first + step]
        state = [scored(*p) for p in some]
        state = [softmaxed(*p, *c) for p, c in zip(some, state)]
        state = [combined(*p, *c) for p, c in zip(some, state)]
        for i in range(0, len(some), 2):
            at = pl.ds(some[i][0] * patches, patches)
            o, dq, dk, dv = [joined(x, y) for x, y in zip(state[i], state[i + 1])]
            att[at, :] = o
            dproj[at, 0:PADH] = dq
            dproj[at, PADH : 2 * PADH] = dk
            dproj[at, 2 * PADH :] = dv


def first_half_kernel(
    plan_ref, act_ref, arr_a_ref, arr_b_ref, cot_ref, g_ref,
    x_ref, nrm_ref, ub_ref, added_ref, dn_ref, gt_ref,
    xb, cotb, bias_row, gain_row, nrm, ub, wqkv, wo, qkv, da, att, dproj, added, dn, gt,
    win_sems, sems,
):
    slots = act_ref.shape[0]
    kept, patches, ch = xb.shape
    n_shard = g_ref.shape[0]
    rows = g_ref.shape[1] // 10
    core = lax.rem(lax.axis_index("dp"), 2)
    cot_copy = pltpu.make_async_copy(cot_ref, cotb, sems.at[0])
    cot_copy.start()
    xb[...] = jnp.zeros(xb.shape, bf16)
    code = [plan_ref[CODES + b] for b in range(kept)]
    lens = [plan_ref[LENS + b] for b in range(kept)]
    arrived = [arr_b_ref.at[0], arr_a_ref.at[0], arr_b_ref.at[1]]
    for b in range(kept):
        @pl.when((code[b] >= 0) & (code[b] < slots))
        def _(b=b):
            pltpu.make_async_copy(act_ref.at[code[b]], xb.at[b], win_sems.at[b]).start()

        for d in range(MOVES):
            @pl.when(code[b] == slots + d)
            def _(b=b, d=d):
                pltpu.make_async_copy(arrived[d], xb.at[b], win_sems.at[b]).start()

    unpack_weights(g_ref, wqkv, wo, bias_row, gain_row)
    bias = bias_of(bias_row, core == 0)
    gain = gain_row[...]
    cot_copy.wait()
    position = lax.broadcasted_iota(jnp.int32, (patches, 1), 0)
    for b in range(kept):
        @pl.when(code[b] >= 0)
        def _(b=b):
            pltpu.make_async_copy(act_ref.at[0], xb.at[b], win_sems.at[b]).wait()

        x = xb[b].astype(f32)
        inv = lax.rsqrt(jnp.mean(x * x, axis=-1, keepdims=True) + EPS)
        at = pl.ds(b * patches, patches)
        nrm[at, :] = (x * inv * gain).astype(bf16)
        ub[at, :] = jnp.where(position < lens[b], cotb[b].astype(f32), 0.0).astype(bf16)
    out = [
        pltpu.make_async_copy(v, r, sems.at[i])
        for i, (v, r) in enumerate(
            [(xb, x_ref), (nrm, nrm_ref), (ub, ub_ref), (gt, gt_ref), (added, added_ref), (dn, dn_ref)]
        )
    ]
    for cp in out[0:3]:
        cp.start()

    qkv[...] = (dot(nrm[...], wqkv[...], 1, 0) + bias).astype(bf16)
    da[...] = dot(ub[...], wo[...], 1, 0).astype(bf16)
    attention(lens, patches, qkv, da, att, dproj)
    whole = dot(ub[...], att[...], 0, 0)
    for s in range(n_shard):
        gt[s] = share_tiles(whole[s * rows : (s + 1) * rows]).astype(bf16)
    out[3].start()
    added[...] = dot(att[...], wo[...], 1, 1)
    out[4].start()
    dn[...] = dot(dproj[...], wqkv[...], 1, 1)
    out[5].start()
    for cp in out:
        cp.wait()


def second_half_kernel(
    plan_ref, x_ref, nrm_ref, ub_ref, added_ref, dn_ref, g_ref,
    out_ref, grad_ref, ret_c_ref, ret_d_ref, gt_ref,
    xb, nrm, ub, added, dn, outb, gbuf, zeros, bias_row, gain_row, wqkv, wo, qkv, da, att, dproj, gt,
    in_sems, zero_sems, win_sems, sems,
):
    slots = grad_ref.shape[0]
    kept, patches, ch = xb.shape
    n_shard = g_ref.shape[0]
    rows = g_ref.shape[1] // 10
    core = lax.rem(lax.axis_index("dp"), 2)
    loads = [
        pltpu.make_async_copy(r, v, in_sems.at[i])
        for i, (r, v) in enumerate(
            [(nrm_ref, nrm), (ub_ref, ub), (x_ref, xb), (added_ref, added), (dn_ref, dn)]
        )
    ]
    for cp in loads:
        cp.start()
    zeros[...] = jnp.zeros(zeros.shape, bf16)
    code = [plan_ref[CODES + b] for b in range(kept)]
    lens = [plan_ref[LENS + b] for b in range(kept)]

    def zero_copy(s):
        return pltpu.make_async_copy(zeros, grad_ref.at[s], zero_sems.at[s])

    for s in range(slots):
        @pl.when(plan_ref[STAYS + s] < 0)
        def _(s=s):
            zero_copy(s).start()

    returned = [ret_c_ref.at[0], ret_d_ref, ret_c_ref.at[1]]

    def ready(b):
        @pl.when((code[b] >= 0) & (code[b] < slots))
        def _():
            pltpu.make_async_copy(gbuf.at[b], grad_ref.at[code[b]], win_sems.at[b]).start()

        for d in range(MOVES):
            @pl.when(code[b] == slots + d)
            def _(d=d):
                pltpu.make_async_copy(gbuf.at[b], returned[d], win_sems.at[b]).start()

    unpack_weights(g_ref, wqkv, wo, bias_row, gain_row)
    bias = bias_of(bias_row, core == 1)
    gain = gain_row[...]
    loads[0].wait()
    loads[1].wait()
    qkv[...] = (dot(nrm[...], wqkv[...], 1, 0) + bias).astype(bf16)
    da[...] = dot(ub[...], wo[...], 1, 0).astype(bf16)
    attention(lens, patches, qkv, da, att, dproj)
    whole = dot(ub[...], att[...], 0, 0)
    for s in range(n_shard):
        gt[s] = share_tiles(whole[s * rows : (s + 1) * rows])
    gt_copy = pltpu.make_async_copy(gt, gt_ref, sems.at[0])
    gt_copy.start()
    for cp in loads[2:]:
        cp.wait()
    position = lax.broadcasted_iota(jnp.int32, (patches, 1), 0)
    total = added[...] + dot(att[...], wo[...], 1, 1)
    for b in range(kept):
        at = slice(b * patches, (b + 1) * patches)
        outb[b] = jnp.where(position < lens[b], xb[b].astype(f32) + total[at], 0.0).astype(bf16)
    out_copy = pltpu.make_async_copy(outb, out_ref, sems.at[1])
    out_copy.start()
    d_nrm = dn[...] + dot(dproj[...], wqkv[...], 1, 1)
    for b in range(kept):
        at = slice(b * patches, (b + 1) * patches)
        x = xb[b].astype(f32)
        inv = lax.rsqrt(jnp.mean(x * x, axis=-1, keepdims=True) + EPS)
        t = d_nrm[at].astype(bf16).astype(f32) * gain
        along = jnp.mean(t * x, axis=-1, keepdims=True)
        dx = t * inv - x * (inv * inv * inv * along)
        gbuf[b] = (ub[at, :].astype(f32) + dx).astype(bf16)
        ready(b)

    for b in range(kept):
        @pl.when(code[b] >= 0)
        def _(b=b):
            pltpu.make_async_copy(gbuf.at[b], grad_ref.at[0], win_sems.at[b]).wait()
    for s in range(slots):
        @pl.when(plan_ref[STAYS + s] < 0)
        def _(s=s):
            zero_copy(s).wait()
    gt_copy.wait()
    out_copy.wait()


def half_cost(tokens, patches, ch):
    work = 2 * tokens * HALF * (9 * ch + 6 * patches)
    return pl.CostEstimate(flops=work, bytes_accessed=8 * 1024 * 1024, transcendentals=4 * tokens * patches)


def half_scratch(tokens, ch):
    return [
        pltpu.VMEM((ch, 3 * PADH), bf16),
        pltpu.VMEM((ch, PADH), bf16),
        pltpu.VMEM((tokens, 3 * PADH), bf16),
        pltpu.VMEM((tokens, PADH), bf16),
        pltpu.VMEM((tokens, PADH), bf16),
        pltpu.VMEM((tokens, 3 * PADH), bf16),
    ]


def first_half(plan, act, arr_a, arr_b, cot, own):
    kept, patches, ch = cot.shape
    tokens = kept * patches
    share = (own.shape[0],) + SHARE
    smem = pl.BlockSpec(memory_space=pltpu.SMEM)
    vmem = pl.BlockSpec(memory_space=pltpu.VMEM)
    hbm = pl.BlockSpec(memory_space=pl.ANY)
    row = pltpu.VMEM((1, ch), f32)
    wide = pltpu.VMEM((tokens, ch), f32)
    narrow = pltpu.VMEM((tokens, ch), bf16)
    return pl.pallas_call(
        first_half_kernel,
        out_shape=(
            jax.ShapeDtypeStruct(cot.shape, bf16),
            jax.ShapeDtypeStruct((tokens, ch), bf16),
            jax.ShapeDtypeStruct((tokens, ch), bf16),
            jax.ShapeDtypeStruct((tokens, ch), f32),
            jax.ShapeDtypeStruct((tokens, ch), f32),
            jax.ShapeDtypeStruct(share, bf16),
        ),
        in_specs=[smem] + [hbm] * 4 + [vmem],
        out_specs=(hbm,) * 6,
        scratch_shapes=[
            pltpu.VMEM(cot.shape, bf16),
            pltpu.VMEM(cot.shape, bf16),
            pltpu.VMEM((1, 6 * HALF), f32),
            row, narrow, narrow,
            *half_scratch(tokens, ch),
            wide, wide,
            pltpu.VMEM(share, bf16),
            pltpu.SemaphoreType.DMA((kept,)),
            pltpu.SemaphoreType.DMA((6,)),
        ],
        compiler_params=pltpu.CompilerParams(vmem_limit_bytes=VMEM_LIMIT),
        cost_estimate=half_cost(tokens, patches, ch),
        name="first_half",
    )(plan, act, arr_a, arr_b, cot, own)


def second_half(plan, x, nrm, ub, added, dn, oth, slots):
    kept, patches, ch = x.shape
    tokens = kept * patches
    share = (oth.shape[0],) + SHARE
    window = (patches, ch)
    smem = pl.BlockSpec(memory_space=pltpu.SMEM)
    vmem = pl.BlockSpec(memory_space=pltpu.VMEM)
    hbm = pl.BlockSpec(memory_space=pl.ANY)
    row = pltpu.VMEM((1, ch), f32)
    wide = pltpu.VMEM((tokens, ch), f32)
    narrow = pltpu.VMEM((tokens, ch), bf16)
    held = pltpu.VMEM(x.shape, bf16)
    return pl.pallas_call(
        second_half_kernel,
        out_shape=(
            jax.ShapeDtypeStruct(x.shape, bf16),
            jax.ShapeDtypeStruct((slots,) + window, bf16),
            jax.ShapeDtypeStruct((2,) + window, bf16),
            jax.ShapeDtypeStruct(window, bf16),
            jax.ShapeDtypeStruct(share, f32),
        ),
        in_specs=[smem] + [hbm] * 5 + [vmem],
        out_specs=(hbm,) * 5,
        scratch_shapes=[
            held, narrow, narrow, wide, wide, held, held,
            pltpu.VMEM(window, bf16),
            pltpu.VMEM((1, 6 * HALF), f32),
            row,
            *half_scratch(tokens, ch),
            pltpu.VMEM(share, f32),
            pltpu.SemaphoreType.DMA((5,)),
            pltpu.SemaphoreType.DMA((slots,)),
            pltpu.SemaphoreType.DMA((kept,)),
            pltpu.SemaphoreType.DMA((2,)),
        ],
        compiler_params=pltpu.CompilerParams(vmem_limit_bytes=VMEM_LIMIT),
        cost_estimate=half_cost(tokens, patches, ch),
        name="second_half",
    )(plan, x, nrm, ub, added, dn, oth)


def finish_kernel(
    plan_ref, parts_ref, back_c_ref, back_d_ref, grad_in_ref, grad_ref, total_ref, sems
):
    back = [back_c_ref.at[0], back_d_ref.at[0], back_d_ref.at[1]]
    copies = []
    for d in range(MOVES):
        s = plan_ref[LEAVES + d + 1]
        cp = pltpu.make_async_copy(back[d], grad_ref.at[jnp.maximum(s, 0)], sems.at[d])
        copies.append((s >= 0, cp))
    for moved, cp in copies:
        @pl.when(moved)
        def _(cp=cp):
            cp.start()

    n = parts_ref.shape[0]
    halves = []
    for h in range(2):
        total = parts_ref[1 - h].astype(f32)
        for z in range(1, n // 2):
            total = total + parts_ref[2 * z + 1 - h].astype(f32)
        halves.append(share_block(total))
    total_ref[...] = jnp.concatenate(halves, axis=1)
    for moved, cp in copies:
        @pl.when(moved)
        def _(cp=cp):
            cp.wait()


def finish(plan, parts, back_c, back_d, grad, rows):
    smem = pl.BlockSpec(memory_space=pltpu.SMEM)
    vmem = pl.BlockSpec(memory_space=pltpu.VMEM)
    hbm = pl.BlockSpec(memory_space=pl.ANY)
    return pl.pallas_call(
        finish_kernel,
        out_shape=(
            jax.ShapeDtypeStruct(grad.shape, bf16),
            jax.ShapeDtypeStruct((rows, 2 * HALF), f32),
        ),
        in_specs=[smem, vmem, vmem, vmem, hbm],
        out_specs=(hbm, vmem),
        scratch_shapes=[pltpu.SemaphoreType.DMA((MOVES,))],
        input_output_aliases={4: 0},
        compiler_params=pltpu.CompilerParams(vmem_limit_bytes=VMEM_LIMIT),
        name="finish",
    )(plan, parts, back_c, back_d, grad)


def shards(
    activations, cotangent, window_len, move_dest, move_slot, w_qkv, b_qkv, norm_gain, w_out
):
    n_shard = lax.axis_size("shard")
    rows = w_qkv.shape[0]
    tables = [t.transpose(2, 1, 0) for t in (window_len, move_dest, move_slot)]
    blob, par_a, par_b, plan = pack(
        tables, activations, w_qkv, b_qkv[None], norm_gain[None], w_out.T, n_shard
    )
    arr_a = permute_dp(par_a, 2)
    own = lax.all_to_all(blob, "shard", 0, 0)
    arr_b = permute_dp(jnp.stack([par_b, arr_a[1]]), 1)
    own, arr_b = lax.optimization_barrier((own, arr_b))
    oth = swap_cores(own)
    x, nrm, ub, added, dn, gt_out = first_half(
        plan, activations, arr_a, arr_b, cotangent, own
    )
    gt_in = swap_cores(gt_out)
    out, grad, ret_c, ret_d, gt = second_half(
        plan, x, nrm, ub, added, dn, oth, activations.shape[0]
    )
    back_c = permute_dp(ret_c, -1)
    share = (gt + gt_in.astype(f32)).astype(bf16)
    chunks = lax.all_to_all(share, "shard", 0, 0)
    summed = jnp.sum(chunks.astype(f32), axis=0).astype(bf16)
    back_d = permute_dp(jnp.stack([ret_d, back_c[1]]), -2)
    parts = lax.all_gather(summed, "dp", axis=0)
    grad_input, total = finish(plan, parts, back_c, back_d, grad, rows)
    return (out, grad_input, total.T)


def solution(mesh):
    return jax.shard_map(
        shards,
        mesh=mesh,
        in_specs=(
            P(("dp", "shard"), None, None),
            P(("dp", "shard"), None, None),
            P(None, "shard", None),
            P(None, "shard", None),
            P(None, "shard", None),
            P("shard", None),
            P("shard"),
            P("shard"),
            P(None, "shard"),
        ),
        out_specs=(
            P(("dp", "shard"), None, None),
            P(("dp", "shard"), None, None),
            P(None, "shard"),
        ),
        check_vma=False,
    )
```

time: 119 us -> 115 us (0.966)
  waiting for transfers between devices: 29.2 us -> 22.9 us
  Pallas kernels: 17.8 us -> 22.5 us
  starting transfers between devices: 36.9 us -> 35.3 us
    ppermute x2, waiting for transfers between devices: 5.04 us -> 0.01 us  [swap_cores(): return lax.ppermute(array, 'dp', [(i, i ^ 1) for i in range(n)])]
    pallas_call x2 -> x3, Pallas kernels: 16.5 us -> 20.5 us  [the longest x1 8.88 us: first_half(): pl.pallas_call(first_half_kernel, out_shape=(jax.ShapeDtypeStruct(cot.sha...]
  transfers between devices with their start and end apart: 8 -> 8, of which waited for: 6 -> 4; matrix products, arithmetic and copies ran while one was open for 1% -> 0% of each run, Pallas kernels for 0% -> 15%
where the time goes in v3:
time: 115 us
  starting transfers between devices  35.3 us (31%)
  blocking collectives  32.3 us (28%)
  waiting for transfers between devices  22.9 us (20%)
  Pallas kernels  22.5 us (20%)
    all_gather x1, blocking collectives, shards(): parts = lax.all_gather(summed, 'dp', axis=0)  32.3 us
    ppermute x4, waiting for transfers between devices, permute_dp(): return lax.ppermute(array, 'dp', [(i, (i + by) % n) for i in range(n)])  19.1 us
    ppermute x4, starting transfers between devices, permute_dp(): return lax.ppermute(array, 'dp', [(i, (i + by) % n) for i in range(n)])  15.7 us
    pallas_call x1, Pallas kernels, first_half(): pl.pallas_call(first_half_kernel, out_shape=(jax.ShapeDtypeStruct(cot.sha...  8.88 us
    ppermute x2, starting transfers between devices, swap_cores(): return lax.ppermute(array, 'dp', [(i, i ^ 1) for i in range(n)])  8.33 us
    pallas_call x1, Pallas kernels, second_half(): pl.pallas_call(second_half_kernel, out_shape=(jax.ShapeDtypeStruct(x.shap...  8.13 us
    all_to_all x1, starting transfers between devices, shards(): own = lax.all_to_all(blob, 'shard', 0, 0)  7.73 us
    all_to_all x1, waiting for transfers between devices, shards(): own = lax.all_to_all(blob, 'shard', 0, 0)  3.73 us
  transfers between devices with their start and end apart: 8, of which 4 were waited for; matrix products, arithmetic and copies ran while one was open for 0% of the time, Pallas kernels for 15%

profile of v3, /device:TPU:1, one launch (start us, length us, event | category | flops | bytes accessed | tf_op | source)
XLA Modules:
  0.0 114.8 jit_solution(9578001920638589701)
XLA Ops:
  0.6 3.5 %pack_weights.1 = (bf16[16,408,128]{2,1,0:T(8,128)(2,1)}, bf16[2,64,640]{2,1,0:T(8,128)(2,1)}, bf16[64,640]{1,0:T(8,128)(2,1)}, s32[64]{0:T(128)}) custom-call(s32[10,1,32]{2,1,0:T(1,128)} %bitcast.14, s32[10,1,32]{2,1,0:T(1,128)} %bitcast.15, s32[10,1,32]{2,1,0:T(1,128)} %bitcast.16, bf16[10,64,640]{2,1,0:T(8,128)(2,1)} %act_ref.3, ...), custom_call_target="tpu_custom_call" | custom-call | tf_op jit(solution)/shard_map/pack_weights/pallas_call | solution.py:150
  4.1 0.0 copy-start.4
  4.1 0.0 copy-start.3
  4.1 0.0 copy-start
  4.1 0.0 copy-start.1
  4.2 0.0 copy-start.2
  4.2 7.7 %all-to-all-start = ((bf16[16,408,128]{2,1,0:T(8,128)(2,1)}), bf16[16,408,128]{2,1,0:T(8,128)(2,1)S(1)}, u32[]{:S(2)}, u32[]{:S(2)}) async-start(bf16[16,408,128]{2,1,0:T(8,128)(2,1)} %get-tuple-element.24), calls=%async_computation | async-start | bytes 3342336 | tf_op jit(solution)/shard_map/all_to_all | solution.py:567
  11.9 0.0 copy-done.4
  11.9 3.5 %collective-permute-start = (bf16[2,64,640]{2,1,0:T(8,128)(2,1)S(1)}, bf16[2,64,640]{2,1,0:T(8,128)(2,1)S(1)}, u32[]{:S(2)}, u32[]{:S(2)}) collective-permute-start(bf16[2,64,640]{2,1,0:T(8,128)(2,1)S(1)} %copy-done.4), channel_id=1, source_target_pairs={{0,32},{16,48},{32,64},{48,80},{64,96},{80,112},{96,128},{112,144}... | collective-permute-start | bytes 491528 | tf_op jit(solution)/shard_map/ppermute | solution.py:26
  15.5 11.3 %collective-permute-done.arr_a_ref = bf16[2,64,640]{2,1,0:T(8,128)(2,1)S(1)} collective-permute-done((bf16[2,64,640]{2,1,0:T(8,128)(2,1)S(1)}, bf16[2,64,640]{2,1,0:T(8,128)(2,1)S(1)}, u32[]{:S(2)}, u32[]{:S(2)}) %collective-permute-start) | collective-permute-done | bytes 163872 | tf_op jit(solution)/shard_map/ppermute | solution.py:26
  26.8 0.0 copy-done.3
  26.9 0.0 collective-permute-start.1
  26.9 2.3 %collective-permute-done.1.arr_b_ref = bf16[2,64,640]{2,1,0:T(8,128)(2,1)S(1)} collective-permute-done((bf16[2,64,640]{2,1,0:T(8,128)(2,1)S(1)}, bf16[2,64,640]{2,1,0:T(8,128)(2,1)S(1)}, u32[]{:S(2)}, u32[]{:S(2)}) %collective-permute-start.1) | collective-permute-done | bytes 163872 | tf_op jit(solution)/shard_map/ppermute | solution.py:26
  29.2 3.7 %all-to-all-done.g_ref = bf16[16,408,128]{2,1,0:T(8,128)(2,1)S(1)} async-done(((bf16[16,408,128]{2,1,0:T(8,128)(2,1)}), bf16[16,408,128]{2,1,0:T(8,128)(2,1)S(1)}, u32[]{:S(2)}, u32[]{:S(2)}) %all-to-all-start) | async-done | bytes 1671200 | tf_op jit(solution)/shard_map/all_to_all | solution.py:567
  32.9 6.4 %collective-permute-start.2 = (bf16[16,408,128]{2,1,0:T(8,128)(2,1)S(1)}, bf16[16,408,128]{2,1,0:T(8,128)(2,1)S(1)}, u32[]{:S(2)}, u32[]{:S(2)}) collective-permute-start(bf16[16,408,128]{2,1,0:T(8,128)(2,1)S(1)} %all-to-all-done.g_ref), channel_id=1, source_target_pairs={{0,16},{16,0},{32,48},{48,32},{64,80},{80,64},{96,112},{112,96},{1... | collective-permute-start | bytes 5013512 | tf_op jit(solution)/shard_map/ppermute | solution.py:31
  39.3 0.0 copy-done
  39.3 0.0 copy-done.1
  39.3 0.0 copy-done.2
  39.3 8.9 %first_half.1 = (bf16[7,64,640]{2,1,0:T(8,128)(2,1)S(1)}, bf16[448,640]{1,0:T(8,128)(2,1)S(1)}, bf16[448,640]{1,0:T(8,128)(2,1)S(1)}, f32[448,640]{1,0:T(8,128)S...) custom-call(s32[64]{0:T(128)S(1)} %copy-done.1, bf16[10,64,640]{2,1,0:T(8,128)(2,1)S(1)} %copy-done, ...), custom_call_target="tpu_custom_call" | custom-call | flops 1761607680 | bytes 8388608 | tf_op jit(solution)/shard_map/first_half/pallas_call | solution.py:440
  48.2 1.9 %collective-permute-start.3 = (bf16[16,104,128]{2,1,0:T(8,128)(2,1)S(1)}, bf16[16,104,128]{2,1,0:T(8,128)(2,1)S(1)}, u32[]{:S(2)}, u32[]{:S(2)}) collective-permute-start(bf16[16,104,128]{2,1,0:T(8,128)(2,1)S(1)} %get-tuple-element.35), channel_id=1, source_target_pairs={{0,16},{16,0},{32,48},{48,32},{64,80},{80,64},{96,112},{112,96},{1... | collective-permute-start | bytes 1277960 | tf_op jit(solution)/shard_map/ppermute | solution.py:31
  50.1 0.0 collective-permute-done.2.g_ref
  50.2 8.1 %second_half.1 = (bf16[7,64,640]{2,1,0:T(8,128)(2,1)}, bf16[10,64,640]{2,1,0:T(8,128)(2,1)}, bf16[2,64,640]{2,1,0:T(8,128)(2,1)S(1)}, bf16[64,640]{1,0:T(8,128)(2,1)S(1)}, f32[16,104,128]{2,1,0:T(8,128)S(1)}) custom-call(s32[64]{0:T(128)S(1)} %copy-done.1, bf16[7,64,640]{2,1,0:T(8,128)(2,1)S(1)} %get-tuple-element.28.x_ref, ...), custom_call_target="tpu_custom_call" | custom-call | flops 1761607680 | bytes 8388608 | tf_op jit(solution)/shard_map/second_half/pallas_call | solution.py:481
  58.3 0.0 collective-permute-done.3
  58.3 0.8 add_convert_fusion
  59.1 3.6 %all-to-all-start.1 = ((bf16[16,104,128]{2,1,0:T(8,128)(2,1)}), bf16[16,104,128]{2,1,0:T(8,128)(2,1)S(1)}, u32[]{:S(2)}, u32[]{:S(2)}) async-start(bf16[16,104,128]{2,1,0:T(8,128)(2,1)} %add_convert_fusion), calls=%async_computation.1 | async-start | bytes 851968 | tf_op jit(solution)/shard_map/all_to_all | solution.py:580
  62.7 0.3 collective-permute-start.4
  63.0 5.5 %collective-permute-done.4.back_c_ref = bf16[2,64,640]{2,1,0:T(8,128)(2,1)S(1)} collective-permute-done((bf16[2,64,640]{2,1,0:T(8,128)(2,1)S(1)}, bf16[2,64,640]{2,1,0:T(8,128)(2,1)S(1)}, u32[]{:S(2)}, u32[]{:S(2)}) %collective-permute-start.4) | collective-permute-done | bytes 163872 | tf_op jit(solution)/shard_map/ppermute | solution.py:26
  68.6 11.8 %collective-permute-start.5 = (bf16[2,64,640]{2,1,0:T(8,128)(2,1)S(1)}, bf16[2,64,640]{2,1,0:T(8,128)(2,1)S(1)}, u32[]{:S(2)}, u32[]{:S(2)}) collective-permute-start(bf16[2,64,640]{2,1,0:T(8,128)(2,1)S(1)} %pad_maximum_fusion.1), channel_id=1, source_target_pairs={{0,480},{16,496},{32,0},{48,16},{64,32},{80,48},{96,64},{112,80},{... | collective-permute-start | bytes 491528 | tf_op jit(solution)/shard_map/ppermute | solution.py:26
  80.4 0.0 all-to-all-done.1
  80.4 0.1 reduce_sum.12
  80.5 32.3 %all-gather = bf16[3328,128]{1,0:T(8,128)(2,1)S(1)} all-gather(bf16[104,128]{1,0:T(8,128)(2,1)S(1)} %reduce_sum.12), channel_id=2, replica_groups=mesh['dp'=32,'shard'=16] {'dp'}, dimensions={0}, use_global_device_ids=true | all-gather | bytes 878592 | tf_op jit(solution)/shard_map/all_gather | solution.py:583
  112.8 0.0 collective-permute-done.5.back_d_ref
  112.8 2.0 %finish.1 = (bf16[10,64,640]{2,1,0:T(8,128)(2,1)}, f32[40,640]{1,0:T(8,128)}) custom-call(s32[64]{0:T(128)S(1)} %copy-done.1, bf16[32,104,128]{2,1,0:T(8,128)(2,1)S(1)} %bitcast.10, bf16[2,64,640]{2,1,0:T(8,128)(2,1)S(1)} %collective-permute-done.4.back_c_ref, ...), custom_call_target="tpu_custom_call", output_to_operand_aliasing={{0}: (4, {})} | custom-call | tf_op jit(solution)/shard_map/finish/pallas_call | solution.py:542
  (4 shorter events, 0.1 us)
Async XLA Ops:
  4.1 7.8 %copy-start.4 = (bf16[2,64,640]{2,1,0:T(8,128)(2,1)S(1)}, bf16[2,64,640]{2,1,0:T(8,128)(2,1)}, u32[]{:S(2)}) copy-start(bf16[2,64,640]{2,1,0:T(8,128)(2,1)} %get-tuple-element.23) | copy-start | bytes 491524
  4.1 22.7 %copy-start.3 = (bf16[64,640]{1,0:T(8,128)(2,1)S(1)}, bf16[64,640]{1,0:T(8,128)(2,1)}, u32[]{:S(2)}) copy-start(bf16[64,640]{1,0:T(8,128)(2,1)} %get-tuple-element.25) | copy-start | bytes 245764
  4.1 35.2 %copy-start = (bf16[10,64,640]{2,1,0:T(8,128)(2,1)S(1)}, bf16[10,64,640]{2,1,0:T(8,128)(2,1)}, u32[]{:S(2)}) copy-start(bf16[10,64,640]{2,1,0:T(8,128)(2,1)} %act_ref.3) | copy-start | bytes 2457604
  4.1 35.2 %copy-start.1 = (s32[64]{0:T(128)S(1)}, s32[64]{0:T(128)}, u32[]{:S(2)}) copy-start(s32[64]{0:T(128)} %get-tuple-element.22.plan_ref) | copy-start | bytes 772
  4.2 35.2 %copy-start.2 = (bf16[7,64,640]{2,1,0:T(8,128)(2,1)S(1)}, bf16[7,64,640]{2,1,0:T(8,128)(2,1)}, u32[]{:S(2)}) copy-start(bf16[7,64,640]{2,1,0:T(8,128)(2,1)} %cot_ref.1) | copy-start | bytes 1720324
  4.2 28.7 %all-to-all-start = ((bf16[16,408,128]{2,1,0:T(8,128)(2,1)}), bf16[16,408,128]{2,1,0:T(8,128)(2,1)S(1)}, u32[]{:S(2)}, u32[]{:S(2)}) async-start(bf16[16,408,128]{2,1,0:T(8,128)(2,1)} %get-tuple-element.24), calls=%async_computation | async-start | bytes 3342336 | tf_op jit(solution)/shard_map/all_to_all | solution.py:567
  11.9 14.9 %collective-permute-start = (bf16[2,64,640]{2,1,0:T(8,128)(2,1)S(1)}, bf16[2,64,640]{2,1,0:T(8,128)(2,1)S(1)}, u32[]{:S(2)}, u32[]{:S(2)}) collective-permute-start(bf16[2,64,640]{2,1,0:T(8,128)(2,1)S(1)} %copy-done.4), channel_id=1, source_target_pairs={{0,32},{16,48},{32,64},{48,80},{64,96},{80,112},{96,128},{112,144}... | collective-permute-start | bytes 491528 | tf_op jit(solution)/shard_map/ppermute | solution.py:26
  26.9 2.3 %collective-permute-start.1 = (bf16[2,64,640]{2,1,0:T(8,128)(2,1)S(1)}, bf16[2,64,640]{2,1,0:T(8,128)(2,1)S(1)}, u32[]{:S(2)}, u32[]{:S(2)}) collective-permute-start(bf16[2,64,640]{2,1,0:T(8,128)(2,1)S(1)} %pad_maximum_fusion), channel_id=1, source_target_pairs={{0,16},{16,32},{32,48},{48,64},{64,80},{80,96},{96,112},{112,128},... | collective-permute-start | bytes 491528 | tf_op jit(solution)/shard_map/ppermute | solution.py:26
  32.9 17.3 %collective-permute-start.2 = (bf16[16,408,128]{2,1,0:T(8,128)(2,1)S(1)}, bf16[16,408,128]{2,1,0:T(8,128)(2,1)S(1)}, u32[]{:S(2)}, u32[]{:S(2)}) collective-permute-start(bf16[16,408,128]{2,1,0:T(8,128)(2,1)S(1)} %all-to-all-done.g_ref), channel_id=1, source_target_pairs={{0,16},{16,0},{32,48},{48,32},{64,80},{80,64},{96,112},{112,96},{1... | collective-permute-start | bytes 5013512 | tf_op jit(solution)/shard_map/ppermute | solution.py:31
  48.2 10.1 %collective-permute-start.3 = (bf16[16,104,128]{2,1,0:T(8,128)(2,1)S(1)}, bf16[16,104,128]{2,1,0:T(8,128)(2,1)S(1)}, u32[]{:S(2)}, u32[]{:S(2)}) collective-permute-start(bf16[16,104,128]{2,1,0:T(8,128)(2,1)S(1)} %get-tuple-element.35), channel_id=1, source_target_pairs={{0,16},{16,0},{32,48},{48,32},{64,80},{80,64},{96,112},{112,96},{1... | collective-permute-start | bytes 1277960 | tf_op jit(solution)/shard_map/ppermute | solution.py:31
  59.1 21.3 %all-to-all-start.1 = ((bf16[16,104,128]{2,1,0:T(8,128)(2,1)}), bf16[16,104,128]{2,1,0:T(8,128)(2,1)S(1)}, u32[]{:S(2)}, u32[]{:S(2)}) async-start(bf16[16,104,128]{2,1,0:T(8,128)(2,1)} %add_convert_fusion), calls=%async_computation.1 | async-start | bytes 851968 | tf_op jit(solution)/shard_map/all_to_all | solution.py:580
  62.7 5.8 %collective-permute-start.4 = (bf16[2,64,640]{2,1,0:T(8,128)(2,1)S(1)}, bf16[2,64,640]{2,1,0:T(8,128)(2,1)S(1)}, u32[]{:S(2)}, u32[]{:S(2)}) collective-permute-start(bf16[2,64,640]{2,1,0:T(8,128)(2,1)S(1)} %get-tuple-element.36), channel_id=1, source_target_pairs={{0,496},{16,0},{32,16},{48,32},{64,48},{80,64},{96,80},{112,96},{1... | collective-permute-start | bytes 491528 | tf_op jit(solution)/shard_map/ppermute | solution.py:26
  68.6 44.2 %collective-permute-start.5 = (bf16[2,64,640]{2,1,0:T(8,128)(2,1)S(1)}, bf16[2,64,640]{2,1,0:T(8,128)(2,1)S(1)}, u32[]{:S(2)}, u32[]{:S(2)}) collective-permute-start(bf16[2,64,640]{2,1,0:T(8,128)(2,1)S(1)} %pad_maximum_fusion.1), channel_id=1, source_target_pairs={{0,480},{16,496},{32,0},{48,16},{64,32},{80,48},{96,64},{112,80},{... | collective-permute-start | bytes 491528 | tf_op jit(solution)/shard_map/ppermute | solution.py:26

commit v4 on v3

--- a/solution.py
+++ b/solution.py
@@ -13,8 +13,9 @@
 HALF = 320
 PADH = 384
 LANES = 128
+KEPT = 7
 CODES, LENS, STAYS, LEAVES, PLAN = 0, 16, 32, 48, 64
-VMEM_LIMIT = 40 * 1024 * 1024
+VMEM_LIMIT = 24 * 1024 * 1024
 PACK_VMEM_LIMIT = 60 * 1024 * 1024
 
 f32 = jnp.float32
@@ -71,42 +72,9 @@
 SHARE = (104, LANES)
 
 
-def pack_kernel(
-    len_ref, dest_ref, slot_ref, act_ref, wqkv_ref, bias_ref, gain_ref, wout_ref,
-    blob_ref, par_a_ref, par_b_ref, plan_ref, stage, sems, blob_sems,
-):
-    slots, _, n_dp = len_ref.shape
-    n_shard = blob_ref.shape[0]
+def pack_kernel(wqkv_ref, bias_ref, gain_ref, wout_ref, blob_ref, stage, sems):
     inner = wout_ref.shape[1]
-    me = lax.axis_index("dp")
-    core = lax.rem(me, 2)
-    for i in range(plan_ref.shape[0]):
-        plan_ref[i] = 0 if LENS <= i < STAYS else -1
-    for s in range(slots):
-        live = len_ref[s, 0, me] > 0
-        dest = dest_ref[s, 0, me]
-
-        @pl.when(live & (dest == me))
-        def _(s=s):
-            b = slot_ref[s, 0, me]
-            plan_ref[CODES + b] = s
-            plan_ref[LENS + b] = len_ref[s, 0, me]
-            plan_ref[STAYS + s] = b
-
-        for d in range(1, MOVES + 1):
-            @pl.when(live & (dest == lax.rem(me + d, n_dp)))
-            def _(d=d, s=s):
-                plan_ref[LEAVES + d] = s
-
-    leaving = [
-        pltpu.make_async_copy(
-            act_ref.at[jnp.maximum(plan_ref[LEAVES + d], 0)], to, sems.at[d - 1]
-        )
-        for d, to in ((1, par_b_ref), (2, par_a_ref.at[0]), (3, par_a_ref.at[1]))
-    ]
-    for cp in leaving:
-        cp.start()
-
+    core = lax.rem(lax.axis_index("dp"), 2)
     tail = [
         jnp.pad(r[...].astype(f32), ((0, 0), (0, LANES - r.shape[1])))
         for r in (bias_ref, gain_ref)
@@ -119,12 +87,65 @@
                 for g in range(3)
             ] + [wout_ref[:, c * HALF : (c + 1) * HALF].astype(f32)]
             stage[...] = jnp.concatenate(tiles_of(groups) + tail, axis=0).astype(bf16)
+
     copies = [
-        pltpu.make_async_copy(stage, blob_ref.at[s], blob_sems.at[s]) for s in range(n_shard)
+        pltpu.make_async_copy(stage, blob_ref.at[s], sems.at[s]) for s in range(blob_ref.shape[0])
     ]
     for cp in copies:
         cp.start()
-
+    for cp in copies:
+        cp.wait()
+
+
+def pack(wqkv, bias, gain, wout_t, n_shard):
+    block_rows = 10 * wqkv.shape[0] + 8
+    vmem = pl.BlockSpec(memory_space=pltpu.VMEM)
+    hbm = pl.BlockSpec(memory_space=pl.ANY)
+    return pl.pallas_call(
+        pack_kernel,
+        out_shape=jax.ShapeDtypeStruct((n_shard, block_rows, LANES), bf16),
+        in_specs=[vmem] * 4,
+        out_specs=hbm,
+        scratch_shapes=[
+            pltpu.VMEM((block_rows, LANES), bf16),
+            pltpu.SemaphoreType.DMA((n_shard,)),
+        ],
+        compiler_params=pltpu.CompilerParams(vmem_limit_bytes=PACK_VMEM_LIMIT),
+        name="pack_weights",
+    )(wqkv, bias, gain, wout_t)
+
+
+def plan_kernel(
+    len_ref, dest_ref, slot_ref, act_ref, blob_ref, par_a_ref, par_b_ref, plan_ref, sems
+):
+    slots, _, n_dp = len_ref.shape
+    me = lax.axis_index("dp")
+    for i in range(plan_ref.shape[0]):
+        plan_ref[i] = 0 if LENS <= i < STAYS else -1
+    for s in range(slots):
+        live = len_ref[s, 0, me] > 0
+        dest = dest_ref[s, 0, me]
+
+        @pl.when(live & (dest == me))
+        def _(s=s):
+            b = slot_ref[s, 0, me]
+            plan_ref[CODES + b] = s
+            plan_ref[LENS + b] = len_ref[s, 0, me]
+            plan_ref[STAYS + s] = b
+
+        for d in range(1, MOVES + 1):
+            @pl.when(live & (dest == lax.rem(me + d, n_dp)))
+            def _(d=d, s=s):
+                plan_ref[LEAVES + d] = s
+
+    leaving = [
+        pltpu.make_async_copy(
+            act_ref.at[jnp.maximum(plan_ref[LEAVES + d], 0)], to, sems.at[d - 1]
+        )
+        for d, to in ((1, par_b_ref), (2, par_a_ref.at[0]), (3, par_a_ref.at[1]))
+    ]
+    for cp in leaving:
+        cp.start()
     for d in range(1, MOVES + 1):
         row = lax.rem(me - d + n_dp, n_dp)
         for s in range(slots):
@@ -136,35 +157,92 @@
 
     for cp in leaving:
         cp.wait()
-    for cp in copies:
-        cp.wait()
-
-
-def pack(tables, act, wqkv, bias, gain, wout_t, n_shard):
-    rows = wqkv.shape[0]
-    block_rows = 10 * rows + 8
+
+
+def make_plan(tables, act, blob):
     window = act.shape[1:]
     smem = pl.BlockSpec(memory_space=pltpu.SMEM)
     vmem = pl.BlockSpec(memory_space=pltpu.VMEM)
     hbm = pl.BlockSpec(memory_space=pl.ANY)
     return pl.pallas_call(
-        pack_kernel,
+        plan_kernel,
         out_shape=(
-            jax.ShapeDtypeStruct((n_shard, block_rows, LANES), bf16),
             jax.ShapeDtypeStruct((2,) + window, bf16),
             jax.ShapeDtypeStruct(window, bf16),
             jax.ShapeDtypeStruct((PLAN,), jnp.int32),
         ),
-        in_specs=[smem, smem, smem, hbm, vmem, vmem, vmem, vmem],
-        out_specs=(hbm, vmem, vmem, smem),
+        in_specs=[smem, smem, smem, hbm, hbm],
+        out_specs=(vmem, vmem, smem),
+        scratch_shapes=[pltpu.SemaphoreType.DMA((MOVES,))],
+        compiler_params=pltpu.CompilerParams(vmem_limit_bytes=PACK_VMEM_LIMIT),
+        cost_estimate=pl.CostEstimate(flops=0, bytes_accessed=4 * 1024 * 1024, transcendentals=0),
+        name="make_plan",
+    )(*tables, act, blob)
+
+
+def arrange_kernel(
+    plan_ref, act_ref, arr_a_ref, arr_b_ref, cot_ref, x_ref, scaled_ref, ub_ref, cotb, win_sems, sem
+):
+    slots = act_ref.shape[0]
+    kept, patches, ch = x_ref.shape
+    cot_copy = pltpu.make_async_copy(cot_ref, cotb, sem.at[0])
+    cot_copy.start()
+    code = [plan_ref[CODES + b] for b in range(kept)]
+    arrived = [arr_b_ref.at[0], arr_a_ref.at[0], arr_b_ref.at[1]]
+    for b in range(kept):
+        @pl.when((code[b] >= 0) & (code[b] < slots))
+        def _(b=b):
+            pltpu.make_async_copy(act_ref.at[code[b]], x_ref.at[b], win_sems.at[b]).start()
+
+        for d in range(MOVES):
+            @pl.when(code[b] == slots + d)
+            def _(b=b, d=d):
+                pltpu.make_async_copy(arrived[d], x_ref.at[b], win_sems.at[b]).start()
+
+        @pl.when(code[b] < 0)
+        def _(b=b):
+            x_ref[b] = jnp.zeros((patches, ch), bf16)
+
+    cot_copy.wait()
+    position = lax.broadcasted_iota(jnp.int32, (patches, 1), 0)
+    for b in range(kept):
+        live = position < plan_ref[LENS + b]
+        ub_ref[b * patches : (b + 1) * patches, :] = jnp.where(
+            live, cotb[b].astype(f32), 0.0
+        ).astype(bf16)
+    for b in range(kept):
+        @pl.when(code[b] >= 0)
+        def _(b=b):
+            pltpu.make_async_copy(act_ref.at[0], x_ref.at[b], win_sems.at[b]).wait()
+
+        x = x_ref[b].astype(f32)
+        inv = lax.rsqrt(jnp.mean(x * x, axis=-1, keepdims=True) + EPS)
+        scaled_ref[b * patches : (b + 1) * patches, :] = x * inv
+
+
+def arrange(plan, act, arr_a, arr_b, cot):
+    kept, patches, ch = cot.shape
+    smem = pl.BlockSpec(memory_space=pltpu.SMEM)
+    vmem = pl.BlockSpec(memory_space=pltpu.VMEM)
+    hbm = pl.BlockSpec(memory_space=pl.ANY)
+    return pl.pallas_call(
+        arrange_kernel,
+        out_shape=(
+            jax.ShapeDtypeStruct(cot.shape, bf16),
+            jax.ShapeDtypeStruct((kept * patches, ch), f32),
+            jax.ShapeDtypeStruct((kept * patches, ch), bf16),
+        ),
+        in_specs=[smem] + [hbm] * 4,
+        out_specs=(vmem,) * 3,
         scratch_shapes=[
-            pltpu.VMEM((block_rows, LANES), bf16),
-            pltpu.SemaphoreType.DMA((MOVES,)),
-            pltpu.SemaphoreType.DMA((n_shard,)),
+            pltpu.VMEM(cot.shape, bf16),
+            pltpu.SemaphoreType.DMA((kept,)),
+            pltpu.SemaphoreType.DMA((1,)),
         ],
-        compiler_params=pltpu.CompilerParams(vmem_limit_bytes=PACK_VMEM_LIMIT),
-        name="pack_weights",
-    )(*tables, act, wqkv, bias, gain, wout_t)
+        compiler_params=pltpu.CompilerParams(vmem_limit_bytes=VMEM_LIMIT // 3),
+        cost_estimate=pl.CostEstimate(flops=0, bytes_accessed=8 * 1024 * 1024, transcendentals=0),
+        name="arrange_windows",
+    )(plan, act, arr_a, arr_b, cot)
 
 
 def unpack_weights(g, wqkv, wo, bias_row, gain_row):
@@ -258,90 +336,39 @@
 
 
 def first_half_kernel(
-    plan_ref, act_ref, arr_a_ref, arr_b_ref, cot_ref, g_ref,
-    x_ref, nrm_ref, ub_ref, added_ref, dn_ref, gt_ref,
-    xb, cotb, bias_row, gain_row, nrm, ub, wqkv, wo, qkv, da, att, dproj, added, dn, gt,
-    win_sems, sems,
+    plan_ref, scaled, ub, g_ref, nrm, added, dn, gt,
+    bias_row, gain_row, wqkv, wo, qkv, da, att, dproj,
 ):
-    slots = act_ref.shape[0]
-    kept, patches, ch = xb.shape
+    tokens = scaled.shape[0]
+    patches = tokens // KEPT
     n_shard = g_ref.shape[0]
     rows = g_ref.shape[1] // 10
     core = lax.rem(lax.axis_index("dp"), 2)
-    cot_copy = pltpu.make_async_copy(cot_ref, cotb, sems.at[0])
-    cot_copy.start()
-    xb[...] = jnp.zeros(xb.shape, bf16)
-    code = [plan_ref[CODES + b] for b in range(kept)]
-    lens = [plan_ref[LENS + b] for b in range(kept)]
-    arrived = [arr_b_ref.at[0], arr_a_ref.at[0], arr_b_ref.at[1]]
-    for b in range(kept):
-        @pl.when((code[b] >= 0) & (code[b] < slots))
-        def _(b=b):
-            pltpu.make_async_copy(act_ref.at[code[b]], xb.at[b], win_sems.at[b]).start()
-
-        for d in range(MOVES):
-            @pl.when(code[b] == slots + d)
-            def _(b=b, d=d):
-                pltpu.make_async_copy(arrived[d], xb.at[b], win_sems.at[b]).start()
-
+    lens = [plan_ref[LENS + b] for b in range(KEPT)]
     unpack_weights(g_ref, wqkv, wo, bias_row, gain_row)
     bias = bias_of(bias_row, core == 0)
-    gain = gain_row[...]
-    cot_copy.wait()
-    position = lax.broadcasted_iota(jnp.int32, (patches, 1), 0)
-    for b in range(kept):
-        @pl.when(code[b] >= 0)
-        def _(b=b):
-            pltpu.make_async_copy(act_ref.at[0], xb.at[b], win_sems.at[b]).wait()
-
-        x = xb[b].astype(f32)
-        inv = lax.rsqrt(jnp.mean(x * x, axis=-1, keepdims=True) + EPS)
-        at = pl.ds(b * patches, patches)
-        nrm[at, :] = (x * inv * gain).astype(bf16)
-        ub[at, :] = jnp.where(position < lens[b], cotb[b].astype(f32), 0.0).astype(bf16)
-    out = [
-        pltpu.make_async_copy(v, r, sems.at[i])
-        for i, (v, r) in enumerate(
-            [(xb, x_ref), (nrm, nrm_ref), (ub, ub_ref), (gt, gt_ref), (added, added_ref), (dn, dn_ref)]
-        )
-    ]
-    for cp in out[0:3]:
-        cp.start()
-
+    nrm[...] = (scaled[...] * gain_row[...]).astype(bf16)
     qkv[...] = (dot(nrm[...], wqkv[...], 1, 0) + bias).astype(bf16)
     da[...] = dot(ub[...], wo[...], 1, 0).astype(bf16)
     attention(lens, patches, qkv, da, att, dproj)
     whole = dot(ub[...], att[...], 0, 0)
     for s in range(n_shard):
         gt[s] = share_tiles(whole[s * rows : (s + 1) * rows]).astype(bf16)
-    out[3].start()
     added[...] = dot(att[...], wo[...], 1, 1)
-    out[4].start()
     dn[...] = dot(dproj[...], wqkv[...], 1, 1)
-    out[5].start()
-    for cp in out:
-        cp.wait()
 
 
 def second_half_kernel(
-    plan_ref, x_ref, nrm_ref, ub_ref, added_ref, dn_ref, g_ref,
-    out_ref, grad_ref, ret_c_ref, ret_d_ref, gt_ref,
-    xb, nrm, ub, added, dn, outb, gbuf, zeros, bias_row, gain_row, wqkv, wo, qkv, da, att, dproj, gt,
-    in_sems, zero_sems, win_sems, sems,
+    plan_ref, xb, nrm, ub, added, dn, g_ref,
+    out_ref, grad_ref, ret_c_ref, ret_d_ref, gt,
+    outb, gbuf, zeros, bias_row, gain_row, wqkv, wo, qkv, da, att, dproj,
+    zero_sems, win_sems, out_sem,
 ):
     slots = grad_ref.shape[0]
     kept, patches, ch = xb.shape
     n_shard = g_ref.shape[0]
     rows = g_ref.shape[1] // 10
     core = lax.rem(lax.axis_index("dp"), 2)
-    loads = [
-        pltpu.make_async_copy(r, v, in_sems.at[i])
-        for i, (r, v) in enumerate(
-            [(nrm_ref, nrm), (ub_ref, ub), (x_ref, xb), (added_ref, added), (dn_ref, dn)]
-        )
-    ]
-    for cp in loads:
-        cp.start()
     zeros[...] = jnp.zeros(zeros.shape, bf16)
     code = [plan_ref[CODES + b] for b in range(kept)]
     lens = [plan_ref[LENS + b] for b in range(kept)]
@@ -369,24 +396,18 @@
     unpack_weights(g_ref, wqkv, wo, bias_row, gain_row)
     bias = bias_of(bias_row, core == 1)
     gain = gain_row[...]
-    loads[0].wait()
-    loads[1].wait()
     qkv[...] = (dot(nrm[...], wqkv[...], 1, 0) + bias).astype(bf16)
     da[...] = dot(ub[...], wo[...], 1, 0).astype(bf16)
     attention(lens, patches, qkv, da, att, dproj)
     whole = dot(ub[...], att[...], 0, 0)
     for s in range(n_shard):
         gt[s] = share_tiles(whole[s * rows : (s + 1) * rows])
-    gt_copy = pltpu.make_async_copy(gt, gt_ref, sems.at[0])
-    gt_copy.start()
-    for cp in loads[2:]:
-        cp.wait()
     position = lax.broadcasted_iota(jnp.int32, (patches, 1), 0)
     total = added[...] + dot(att[...], wo[...], 1, 1)
     for b in range(kept):
         at = slice(b * patches, (b + 1) * patches)
         outb[b] = jnp.where(position < lens[b], xb[b].astype(f32) + total[at], 0.0).astype(bf16)
-    out_copy = pltpu.make_async_copy(outb, out_ref, sems.at[1])
+    out_copy = pltpu.make_async_copy(outb, out_ref, out_sem.at[0])
     out_copy.start()
     d_nrm = dn[...] + dot(dproj[...], wqkv[...], 1, 1)
     for b in range(kept):
@@ -407,7 +428,6 @@
         @pl.when(plan_ref[STAYS + s] < 0)
         def _(s=s):
             zero_copy(s).wait()
-    gt_copy.wait()
     out_copy.wait()
 
 
@@ -427,43 +447,30 @@
     ]
 
 
-def first_half(plan, act, arr_a, arr_b, cot, own):
-    kept, patches, ch = cot.shape
-    tokens = kept * patches
+def first_half(plan, scaled, ub, own):
+    tokens, ch = scaled.shape
     share = (own.shape[0],) + SHARE
     smem = pl.BlockSpec(memory_space=pltpu.SMEM)
     vmem = pl.BlockSpec(memory_space=pltpu.VMEM)
-    hbm = pl.BlockSpec(memory_space=pl.ANY)
-    row = pltpu.VMEM((1, ch), f32)
-    wide = pltpu.VMEM((tokens, ch), f32)
-    narrow = pltpu.VMEM((tokens, ch), bf16)
     return pl.pallas_call(
         first_half_kernel,
         out_shape=(
-            jax.ShapeDtypeStruct(cot.shape, bf16),
-            jax.ShapeDtypeStruct((tokens, ch), bf16),
             jax.ShapeDtypeStruct((tokens, ch), bf16),
             jax.ShapeDtypeStruct((tokens, ch), f32),
             jax.ShapeDtypeStruct((tokens, ch), f32),
             jax.ShapeDtypeStruct(share, bf16),
         ),
-        in_specs=[smem] + [hbm] * 4 + [vmem],
-        out_specs=(hbm,) * 6,
+        in_specs=[smem, vmem, vmem, vmem],
+        out_specs=(vmem,) * 4,
         scratch_shapes=[
-            pltpu.VMEM(cot.shape, bf16),
-            pltpu.VMEM(cot.shape, bf16),
             pltpu.VMEM((1, 6 * HALF), f32),
-            row, narrow, narrow,
+            pltpu.VMEM((1, ch), f32),
             *half_scratch(tokens, ch),
-            wide, wide,
-            pltpu.VMEM(share, bf16),
-            pltpu.SemaphoreType.DMA((kept,)),
-            pltpu.SemaphoreType.DMA((6,)),
         ],
         compiler_params=pltpu.CompilerParams(vmem_limit_bytes=VMEM_LIMIT),
-        cost_estimate=half_cost(tokens, patches, ch),
+        cost_estimate=half_cost(tokens, tokens // KEPT, ch),
         name="first_half",
-    )(plan, act, arr_a, arr_b, cot, own)
+    )(plan, scaled, ub, own)
 
 
 def second_half(plan, x, nrm, ub, added, dn, oth, slots):
@@ -474,9 +481,6 @@
     smem = pl.BlockSpec(memory_space=pltpu.SMEM)
     vmem = pl.BlockSpec(memory_space=pltpu.VMEM)
     hbm = pl.BlockSpec(memory_space=pl.ANY)
-    row = pltpu.VMEM((1, ch), f32)
-    wide = pltpu.VMEM((tokens, ch), f32)
-    narrow = pltpu.VMEM((tokens, ch), bf16)
     held = pltpu.VMEM(x.shape, bf16)
     return pl.pallas_call(
         second_half_kernel,
@@ -487,19 +491,17 @@
             jax.ShapeDtypeStruct(window, bf16),
             jax.ShapeDtypeStruct(share, f32),
         ),
-        in_specs=[smem] + [hbm] * 5 + [vmem],
-        out_specs=(hbm,) * 5,
+        in_specs=[smem] + [vmem] * 6,
+        out_specs=(hbm,) * 4 + (vmem,),
         scratch_shapes=[
-            held, narrow, narrow, wide, wide, held, held,
+            held, held,
             pltpu.VMEM(window, bf16),
             pltpu.VMEM((1, 6 * HALF), f32),
-            row,
+            pltpu.VMEM((1, ch), f32),
             *half_scratch(tokens, ch),
-            pltpu.VMEM(share, f32),
-            pltpu.SemaphoreType.DMA((5,)),
             pltpu.SemaphoreType.DMA((slots,)),
             pltpu.SemaphoreType.DMA((kept,)),
-            pltpu.SemaphoreType.DMA((2,)),
+            pltpu.SemaphoreType.DMA((1,)),
         ],
         compiler_params=pltpu.CompilerParams(vmem_limit_bytes=VMEM_LIMIT),
         cost_estimate=half_cost(tokens, patches, ch),
@@ -560,17 +562,15 @@
     n_shard = lax.axis_size("shard")
     rows = w_qkv.shape[0]
     tables = [t.transpose(2, 1, 0) for t in (window_len, move_dest, move_slot)]
-    blob, par_a, par_b, plan = pack(
-        tables, activations, w_qkv, b_qkv[None], norm_gain[None], w_out.T, n_shard
-    )
+    blob = pack(w_qkv, b_qkv[None], norm_gain[None], w_out.T, n_shard)
+    own = lax.all_to_all(blob, "shard", 0, 0)
+    par_a, par_b, plan = make_plan(tables, activations, blob)
     arr_a = permute_dp(par_a, 2)
-    own = lax.all_to_all(blob, "shard", 0, 0)
     arr_b = permute_dp(jnp.stack([par_b, arr_a[1]]), 1)
-    own, arr_b = lax.optimization_barrier((own, arr_b))
+    x, scaled, ub = arrange(plan, activations, arr_a, arr_b, cotangent)
+    own, x, scaled, ub = lax.optimization_barrier((own, x, scaled, ub))
     oth = swap_cores(own)
-    x, nrm, ub, added, dn, gt_out = first_half(
-        plan, activations, arr_a, arr_b, cotangent, own
-    )
+    nrm, added, dn, gt_out = first_half(plan, scaled, ub, own)
     gt_in = swap_cores(gt_out)
     out, grad, ret_c, ret_d, gt = second_half(
         plan, x, nrm, ub, added, dn, oth, activations.shape[0]

time: 115 us -> 111 us (0.965)
  starting transfers between devices: 35.3 us -> 30.5 us
  local copies, waits for them, and re-layouts: 0.05 us -> 4.83 us
  waiting for transfers between devices: 22.9 us -> 19 us
  Pallas kernels: 22.5 us -> 21.1 us
    ppermute x4, starting transfers between devices: 15.7 us -> 7.96 us  [permute_dp(): return lax.ppermute(array, 'dp', [(i, (i + by) % n) for i in range(n)])]
    unnamed x10 -> x16, local copies, waits for them, and re-layouts: 0.03 us -> 4.81 us
    all_to_all x1, waiting for transfers between devices: 3.73 us -> 0.01 us  [shards(): own = lax.all_to_all(blob, 'shard', 0, 0)]
    all_to_all x1, starting transfers between devices: 3.56 us -> 6.36 us  [shards(): chunks = lax.all_to_all(share, 'shard', 0, 0)]
    pallas_call x1, Pallas kernels: 8.13 us -> 6.47 us  [second_half(): pl.pallas_call(second_half_kernel, out_shape=(jax.ShapeDtypeStruct(x.shap...]
    pallas_call x2 -> x4, Pallas kernels: 12.4 us -> 12.6 us  [the longest x1 4.8 us: first_half(): pl.pallas_call(first_half_kernel, out_shape=(jax.ShapeDtypeStruct((tokens...]
  transfers between devices with their start and end apart: 8 -> 8, of which waited for: 4 -> 4; matrix products, arithmetic and copies ran while one was open for 0% -> 1% of each run, Pallas kernels for 15% -> 15%
where the time goes in v4:
time: 111 us; the launch traced here: 110 us
  blocking collectives  32 us (29%)
  starting transfers between devices  30.5 us (27%)
  Pallas kernels  21.1 us (19%)
  waiting for transfers between devices  19 us (17%)
  local copies, waits for them, and re-layouts  4.83 us (4%)
  other arithmetic  1.84 us (2%)
    all_gather x1, blocking collectives, shards(): parts = lax.all_gather(summed, 'dp', axis=0)  32 us
    ppermute x4, waiting for transfers between devices, permute_dp(): return lax.ppermute(array, 'dp', [(i, (i + by) % n) for i in range(n)])  18.4 us
    ppermute x2, starting transfers between devices, swap_cores(): return lax.ppermute(array, 'dp', [(i, i ^ 1) for i in range(n)])  8.59 us
    ppermute x4, starting transfers between devices, permute_dp(): return lax.ppermute(array, 'dp', [(i, (i + by) % n) for i in range(n)])  7.96 us
    all_to_all x1, starting transfers between devices, shards(): own = lax.all_to_all(blob, 'shard', 0, 0)  7.6 us
    pallas_call x1, Pallas kernels, second_half(): pl.pallas_call(second_half_kernel, out_shape=(jax.ShapeDtypeStruct(x.shap...  6.47 us
    all_to_all x1, starting transfers between devices, shards(): chunks = lax.all_to_all(share, 'shard', 0, 0)  6.36 us
    unnamed x16, local copies, waits for them, and re-layouts  4.81 us
  transfers between devices with their start and end apart: 8, of which 4 were waited for; matrix products, arithmetic and copies ran while one was open for 1% of the time, Pallas kernels for 15%

profile of v4, /device:TPU:1, one launch (start us, length us, event | category | flops | bytes accessed | tf_op | source)
XLA Modules:
  0.0 110.1 jit_solution(7629342793656065052)
XLA Ops:
  0.6 2.5 %pack_weights.1.blob_ref = bf16[16,408,128]{2,1,0:T(8,128)(2,1)} custom-call(bf16[40,1920]{1,0:T(8,128)(2,1)} %wqkv_ref.1, bf16[1,120]{1,0:T(2,128)(2,1)} %bitcast.17, bf16[1,40]{1,0:T(2,128)(2,1)} %bitcast.18, bf16[40,640]{1,0:T(8,128)(2,1)} %bitcast.13), custom_call_target="tpu_custom_call" | custom-call | tf_op jit(solution)/shard_map/pack_weights/pallas_call | solution.py:104
  3.2 7.6 %all-to-all-start = ((bf16[16,408,128]{2,1,0:T(8,128)(2,1)}), bf16[16,408,128]{2,1,0:T(8,128)(2,1)S(1)}, u32[]{:S(2)}, u32[]{:S(2)}) async-start(bf16[16,408,128]{2,1,0:T(8,128)(2,1)} %pack_weights.1.blob_ref), calls=%async_computation | async-start | bytes 3342336 | tf_op jit(solution)/shard_map/all_to_all | solution.py:566
  10.8 0.0 copy-start
  10.8 0.0 copy-start.1
  10.8 2.9 %make_plan.1 = (bf16[2,64,640]{2,1,0:T(8,128)(2,1)}, bf16[64,640]{1,0:T(8,128)(2,1)}, s32[64]{0:T(128)}) custom-call(s32[10,1,32]{2,1,0:T(1,128)} %bitcast.14, s32[10,1,32]{2,1,0:T(1,128)} %bitcast.15, s32[10,1,32]{2,1,0:T(1,128)} %bitcast.16, bf16[10,64,640]{2,1,0:T(8,128)(2,1)} %act_ref.3, bf16[16,408,128]{2,1,0:T(8,128)(2,1)} %pack_weights.1.blob_ref), custom_call_target="tpu_custom_call" | custom-call | bytes 4194304 | tf_op jit(solution)/shard_map/make_plan/pallas_call | solution.py:167
  13.7 0.0 copy-start.3
  13.7 3.6 %collective-permute-start = (bf16[2,64,640]{2,1,0:T(8,128)(2,1)}, bf16[2,64,640]{2,1,0:T(8,128)(2,1)S(1)}, u32[]{:S(2)}, u32[]{:S(2)}) collective-permute-start(bf16[2,64,640]{2,1,0:T(8,128)(2,1)} %get-tuple-element.25), channel_id=1, source_target_pairs={{0,32},{16,48},{32,64},{48,80},{64,96},{80,112},{96,128},{112,144}... | collective-permute-start | bytes 491528 | tf_op jit(solution)/shard_map/ppermute | solution.py:27
  17.3 11.5 %collective-permute-done.arr_a_ref = bf16[2,64,640]{2,1,0:T(8,128)(2,1)S(1)} collective-permute-done((bf16[2,64,640]{2,1,0:T(8,128)(2,1)}, bf16[2,64,640]{2,1,0:T(8,128)(2,1)S(1)}, u32[]{:S(2)}, u32[]{:S(2)}) %collective-permute-start) | collective-permute-done | bytes 163872 | tf_op jit(solution)/shard_map/ppermute | solution.py:27
  28.8 0.9 pad_maximum_fusion
  29.8 0.0 collective-permute-start.1
  29.8 2.3 %collective-permute-done.1.arr_b_ref = bf16[2,64,640]{2,1,0:T(8,128)(2,1)S(1)} collective-permute-done((bf16[2,64,640]{2,1,0:T(8,128)(2,1)S(1)}, bf16[2,64,640]{2,1,0:T(8,128)(2,1)S(1)}, u32[]{:S(2)}, u32[]{:S(2)}) %collective-permute-start.1) | collective-permute-done | bytes 163872 | tf_op jit(solution)/shard_map/ppermute | solution.py:27
  32.0 0.0 copy-done
  32.0 0.0 copy-done.1
  32.0 0.0 copy-start.2
  32.0 0.7 copy-done.2
  32.7 2.5 %arrange_windows.1 = (bf16[7,64,640]{2,1,0:T(8,128)(2,1)S(1)}, f32[448,640]{1,0:T(8,128)S(1)}, bf16[448,640]{1,0:T(8,128)(2,1)S(1)}) custom-call(s32[64]{0:T(128)S(1)} %copy-done.2, bf16[10,64,640]{2,1,0:T(8,128)(2,1)S(1)} %copy-done, bf16[2,64,640]{2,1,0:T(8,128)(2,1)S(1)} %collective-permute-done.arr_a_ref, ...), custom_call_target="tpu_custom_call" | custom-call | bytes 8388608 | tf_op jit(solution)/shard_map/arrange_windows/pallas_call | solution.py:228
  35.2 0.0 copy-start.4
  35.2 1.0 copy-done.4
  36.2 0.0 copy-start.6
  36.2 0.8 copy-done.6
  37.0 0.0 all-to-all-done.g_ref
  37.0 6.7 %collective-permute-start.2 = (bf16[16,408,128]{2,1,0:T(8,128)(2,1)S(1)}, bf16[16,408,128]{2,1,0:T(8,128)(2,1)S(1)}, u32[]{:S(2)}, u32[]{:S(2)}) collective-permute-start(bf16[16,408,128]{2,1,0:T(8,128)(2,1)S(1)} %all-to-all-done.g_ref), channel_id=1, source_target_pairs={{0,16},{16,0},{32,48},{48,32},{64,80},{80,64},{96,112},{112,96},{1... | collective-permute-start | bytes 5013512 | tf_op jit(solution)/shard_map/ppermute | solution.py:32
  43.7 0.0 copy-done.3
  43.7 0.0 copy-start.5
  43.7 1.2 %copy-done.5 = f32[448,640]{1,0:T(8,128)S(1)} copy-done((f32[448,640]{1,0:T(8,128)S(1)}, f32[448,640]{1,0:T(8,128)}, u32[]{:S(2)}) %copy-start.5) | copy-done | bytes 1146904
  44.9 0.0 copy-start.7
  44.9 1.1 copy-done.7
  46.0 4.8 %first_half.1 = (bf16[448,640]{1,0:T(8,128)(2,1)S(1)}, f32[448,640]{1,0:T(8,128)S(1)}, f32[448,640]{1,0:T(8,128)S(1)}, bf16[16,104,128]{2,1,0:T(8,128)(2,1)S(1)}) custom-call(s32[64]{0:T(128)S(1)} %copy-done.3, f32[448,640]{1,0:T(8,128)S(1)} %copy-done.5, bf16[448,640]{1,0:T(8,128)(2,1)S(1)} %copy-done.7, bf16[16,408,128]{2,1,0:T(8,128)(2,1)S(1)} %all-to-all-done.g_ref), custom_call_target="tpu_custom_call" | custom-call | flops 1761607680 | bytes 8388608 | tf_op jit(solution)/shard_map/first_half/pallas_call | solution.py:455
  50.8 1.9 %collective-permute-start.3 = (bf16[16,104,128]{2,1,0:T(8,128)(2,1)S(1)}, bf16[16,104,128]{2,1,0:T(8,128)(2,1)S(1)}, u32[]{:S(2)}, u32[]{:S(2)}) collective-permute-start(bf16[16,104,128]{2,1,0:T(8,128)(2,1)S(1)} %get-tuple-element.39), channel_id=1, source_target_pairs={{0,16},{16,0},{32,48},{48,32},{64,80},{80,64},{96,112},{112,96},{1... | collective-permute-start | bytes 1277960 | tf_op jit(solution)/shard_map/ppermute | solution.py:32
  52.7 0.0 collective-permute-done.2.g_ref
  52.7 6.5 %second_half.1 = (bf16[7,64,640]{2,1,0:T(8,128)(2,1)}, bf16[10,64,640]{2,1,0:T(8,128)(2,1)}, bf16[2,64,640]{2,1,0:T(8,128)(2,1)S(1)}, bf16[64,640]{1,0:T(8,128)(2,1)S(1)}, f32[16,104,128]{2,1,0:T(8,128)S(1)}) custom-call(s32[64]{0:T(128)S(1)} %copy-done.3, bf16[7,64,640]{2,1,0:T(8,128)(2,1)S(1)} %get-tuple-element.30.xb, ...), custom_call_target="tpu_custom_call" | custom-call | flops 1761607680 | bytes 8388608 | tf_op jit(solution)/shard_map/second_half/pallas_call | solution.py:485
  59.2 0.0 collective-permute-done.3
  59.2 0.8 add_convert_fusion
  60.1 6.4 %all-to-all-start.1 = ((bf16[16,104,128]{2,1,0:T(8,128)(2,1)}), bf16[16,104,128]{2,1,0:T(8,128)(2,1)S(1)}, u32[]{:S(2)}, u32[]{:S(2)}) async-start(bf16[16,104,128]{2,1,0:T(8,128)(2,1)} %add_convert_fusion), calls=%async_computation.1 | async-start | bytes 851968 | tf_op jit(solution)/shard_map/all_to_all | solution.py:580
  66.4 0.5 collective-permute-start.4
  66.9 4.6 %collective-permute-done.4.back_c_ref = bf16[2,64,640]{2,1,0:T(8,128)(2,1)S(1)} collective-permute-done((bf16[2,64,640]{2,1,0:T(8,128)(2,1)S(1)}, bf16[2,64,640]{2,1,0:T(8,128)(2,1)S(1)}, u32[]{:S(2)}, u32[]{:S(2)}) %collective-permute-start.4) | collective-permute-done | bytes 163872 | tf_op jit(solution)/shard_map/ppermute | solution.py:27
  71.5 3.9 %collective-permute-start.5 = (bf16[2,64,640]{2,1,0:T(8,128)(2,1)S(1)}, bf16[2,64,640]{2,1,0:T(8,128)(2,1)S(1)}, u32[]{:S(2)}, u32[]{:S(2)}) collective-permute-start(bf16[2,64,640]{2,1,0:T(8,128)(2,1)S(1)} %pad_maximum_fusion.1), channel_id=1, source_target_pairs={{0,480},{16,496},{32,0},{48,16},{64,32},{80,48},{96,64},{112,80},{... | collective-permute-start | bytes 491528 | tf_op jit(solution)/shard_map/ppermute | solution.py:27
  75.4 0.6 all-to-all-done.1
  76.0 0.1 reduce_sum.12
  76.1 32.0 %all-gather = bf16[3328,128]{1,0:T(8,128)(2,1)S(1)} all-gather(bf16[104,128]{1,0:T(8,128)(2,1)S(1)} %reduce_sum.12), channel_id=2, replica_groups=mesh['dp'=32,'shard'=16] {'dp'}, dimensions={0}, use_global_device_ids=true | all-gather | bytes 878592 | tf_op jit(solution)/shard_map/all_gather | solution.py:583
  108.1 0.0 collective-permute-done.5.back_d_ref
  108.1 2.0 %finish.1 = (bf16[10,64,640]{2,1,0:T(8,128)(2,1)}, f32[40,640]{1,0:T(8,128)}) custom-call(s32[64]{0:T(128)S(1)} %copy-done.3, bf16[32,104,128]{2,1,0:T(8,128)(2,1)S(1)} %bitcast.10, bf16[2,64,640]{2,1,0:T(8,128)(2,1)S(1)} %collective-permute-done.4.back_c_ref, ...), custom_call_target="tpu_custom_call", output_to_operand_aliasing={{0}: (4, {})} | custom-call | tf_op jit(solution)/shard_map/finish/pallas_call | solution.py:544
  (3 shorter events, 0.0 us)
Async XLA Ops:
  3.2 33.9 %all-to-all-start = ((bf16[16,408,128]{2,1,0:T(8,128)(2,1)}), bf16[16,408,128]{2,1,0:T(8,128)(2,1)S(1)}, u32[]{:S(2)}, u32[]{:S(2)}) async-start(bf16[16,408,128]{2,1,0:T(8,128)(2,1)} %pack_weights.1.blob_ref), calls=%async_computation | async-start | bytes 3342336 | tf_op jit(solution)/shard_map/all_to_all | solution.py:566
  10.8 21.3 %copy-start = (bf16[10,64,640]{2,1,0:T(8,128)(2,1)S(1)}, bf16[10,64,640]{2,1,0:T(8,128)(2,1)}, u32[]{:S(2)}) copy-start(bf16[10,64,640]{2,1,0:T(8,128)(2,1)} %act_ref.3) | copy-start | bytes 2457604
  10.8 21.3 %copy-start.1 = (bf16[7,64,640]{2,1,0:T(8,128)(2,1)S(1)}, bf16[7,64,640]{2,1,0:T(8,128)(2,1)}, u32[]{:S(2)}) copy-start(bf16[7,64,640]{2,1,0:T(8,128)(2,1)} %cot_ref.1) | copy-start | bytes 1720324
  13.7 30.0 %copy-start.3 = (s32[64]{0:T(128)S(1)}, s32[64]{0:T(128)}, u32[]{:S(2)}) copy-start(s32[64]{0:T(128)} %get-tuple-element.24.plan_ref) | copy-start | bytes 772
  13.7 15.2 %collective-permute-start = (bf16[2,64,640]{2,1,0:T(8,128)(2,1)}, bf16[2,64,640]{2,1,0:T(8,128)(2,1)S(1)}, u32[]{:S(2)}, u32[]{:S(2)}) collective-permute-start(bf16[2,64,640]{2,1,0:T(8,128)(2,1)} %get-tuple-element.25), channel_id=1, source_target_pairs={{0,32},{16,48},{32,64},{48,80},{64,96},{80,112},{96,128},{112,144}... | collective-permute-start | bytes 491528 | tf_op jit(solution)/shard_map/ppermute | solution.py:27
  29.8 2.3 %collective-permute-start.1 = (bf16[2,64,640]{2,1,0:T(8,128)(2,1)S(1)}, bf16[2,64,640]{2,1,0:T(8,128)(2,1)S(1)}, u32[]{:S(2)}, u32[]{:S(2)}) collective-permute-start(bf16[2,64,640]{2,1,0:T(8,128)(2,1)S(1)} %pad_maximum_fusion), channel_id=1, source_target_pairs={{0,16},{16,32},{32,48},{48,64},{64,80},{80,96},{96,112},{112,128},... | collective-permute-start | bytes 491528 | tf_op jit(solution)/shard_map/ppermute | solution.py:27
  32.0 0.7 copy-start.2
  35.2 1.0 copy-start.4
  36.2 0.8 copy-start.6
  37.0 15.7 %collective-permute-start.2 = (bf16[16,408,128]{2,1,0:T(8,128)(2,1)S(1)}, bf16[16,408,128]{2,1,0:T(8,128)(2,1)S(1)}, u32[]{:S(2)}, u32[]{:S(2)}) collective-permute-start(bf16[16,408,128]{2,1,0:T(8,128)(2,1)S(1)} %all-to-all-done.g_ref), channel_id=1, source_target_pairs={{0,16},{16,0},{32,48},{48,32},{64,80},{80,64},{96,112},{112,96},{1... | collective-permute-start | bytes 5013512 | tf_op jit(solution)/shard_map/ppermute | solution.py:32
  43.7 1.3 %copy-start.5 = (f32[448,640]{1,0:T(8,128)S(1)}, f32[448,640]{1,0:T(8,128)}, u32[]{:S(2)}) copy-start(f32[448,640]{1,0:T(8,128)} %copy-done.4) | copy-start | bytes 3440644
  44.9 1.1 copy-start.7
  50.8 8.4 %collective-permute-start.3 = (bf16[16,104,128]{2,1,0:T(8,128)(2,1)S(1)}, bf16[16,104,128]{2,1,0:T(8,128)(2,1)S(1)}, u32[]{:S(2)}, u32[]{:S(2)}) collective-permute-start(bf16[16,104,128]{2,1,0:T(8,128)(2,1)S(1)} %get-tuple-element.39), channel_id=1, source_target_pairs={{0,16},{16,0},{32,48},{48,32},{64,80},{80,64},{96,112},{112,96},{1... | collective-permute-start | bytes 1277960 | tf_op jit(solution)/shard_map/ppermute | solution.py:32
  60.1 15.9 %all-to-all-start.1 = ((bf16[16,104,128]{2,1,0:T(8,128)(2,1)}), bf16[16,104,128]{2,1,0:T(8,128)(2,1)S(1)}, u32[]{:S(2)}, u32[]{:S(2)}) async-start(bf16[16,104,128]{2,1,0:T(8,128)(2,1)} %add_convert_fusion), calls=%async_computation.1 | async-start | bytes 851968 | tf_op jit(solution)/shard_map/all_to_all | solution.py:580
  66.4 5.1 %collective-permute-start.4 = (bf16[2,64,640]{2,1,0:T(8,128)(2,1)S(1)}, bf16[2,64,640]{2,1,0:T(8,128)(2,1)S(1)}, u32[]{:S(2)}, u32[]{:S(2)}) collective-permute-start(bf16[2,64,640]{2,1,0:T(8,128)(2,1)S(1)} %get-tuple-element.40), channel_id=1, source_target_pairs={{0,496},{16,0},{32,16},{48,32},{64,48},{80,64},{96,80},{112,96},{1... | collective-permute-start | bytes 491528 | tf_op jit(solution)/shard_map/ppermute | solution.py:27
  71.5 36.5 %collective-permute-start.5 = (bf16[2,64,640]{2,1,0:T(8,128)(2,1)S(1)}, bf16[2,64,640]{2,1,0:T(8,128)(2,1)S(1)}, u32[]{:S(2)}, u32[]{:S(2)}) collective-permute-start(bf16[2,64,640]{2,1,0:T(8,128)(2,1)S(1)} %pad_maximum_fusion.1), channel_id=1, source_target_pairs={{0,480},{16,496},{32,0},{48,16},{64,32},{80,48},{96,64},{112,80},{... | collective-permute-start | bytes 491528 | tf_op jit(solution)/shard_map/ppermute | solution.py:27

commit v5 on v4

--- a/solution.py
+++ b/solution.py
@@ -13,7 +13,6 @@
 HALF = 320
 PADH = 384
 LANES = 128
-KEPT = 7
 CODES, LENS, STAYS, LEAVES, PLAN = 0, 16, 32, 48, 64
 VMEM_LIMIT = 24 * 1024 * 1024
 PACK_VMEM_LIMIT = 60 * 1024 * 1024
@@ -181,7 +180,7 @@
 
 
 def arrange_kernel(
-    plan_ref, act_ref, arr_a_ref, arr_b_ref, cot_ref, x_ref, scaled_ref, ub_ref, cotb, win_sems, sem
+    plan_ref, act_ref, arr_a_ref, arr_b_ref, cot_ref, x_ref, inv_ref, ub_ref, cotb, win_sems, sem
 ):
     slots = act_ref.shape[0]
     kept, patches, ch = x_ref.shape
@@ -217,7 +216,7 @@
 
         x = x_ref[b].astype(f32)
         inv = lax.rsqrt(jnp.mean(x * x, axis=-1, keepdims=True) + EPS)
-        scaled_ref[b * patches : (b + 1) * patches, :] = x * inv
+        inv_ref[b * patches : (b + 1) * patches, :] = jnp.broadcast_to(inv, (patches, LANES))
 
 
 def arrange(plan, act, arr_a, arr_b, cot):
@@ -229,7 +228,7 @@
         arrange_kernel,
         out_shape=(
             jax.ShapeDtypeStruct(cot.shape, bf16),
-            jax.ShapeDtypeStruct((kept * patches, ch), f32),
+            jax.ShapeDtypeStruct((kept * patches, LANES), f32),
             jax.ShapeDtypeStruct((kept * patches, ch), bf16),
         ),
         in_specs=[smem] + [hbm] * 4,
@@ -336,18 +335,21 @@
 
 
 def first_half_kernel(
-    plan_ref, scaled, ub, g_ref, nrm, added, dn, gt,
+    plan_ref, xb, inv_ref, ub, g_ref, nrm, added, dn, gt,
     bias_row, gain_row, wqkv, wo, qkv, da, att, dproj,
 ):
-    tokens = scaled.shape[0]
-    patches = tokens // KEPT
+    kept, patches, ch = xb.shape
     n_shard = g_ref.shape[0]
     rows = g_ref.shape[1] // 10
     core = lax.rem(lax.axis_index("dp"), 2)
-    lens = [plan_ref[LENS + b] for b in range(KEPT)]
+    lens = [plan_ref[LENS + b] for b in range(kept)]
     unpack_weights(g_ref, wqkv, wo, bias_row, gain_row)
     bias = bias_of(bias_row, core == 0)
-    nrm[...] = (scaled[...] * gain_row[...]).astype(bf16)
+    gain = gain_row[...]
+    for b in range(kept):
+        at = slice(b * patches, (b + 1) * patches)
+        inv = jnp.concatenate([inv_ref[at, :]] * (ch // LANES), axis=1)
+        nrm[at, :] = (xb[b].astype(f32) * inv * gain).astype(bf16)
     qkv[...] = (dot(nrm[...], wqkv[...], 1, 0) + bias).astype(bf16)
     da[...] = dot(ub[...], wo[...], 1, 0).astype(bf16)
     attention(lens, patches, qkv, da, att, dproj)
@@ -359,7 +361,7 @@
 
 
 def second_half_kernel(
-    plan_ref, xb, nrm, ub, added, dn, g_ref,
+    plan_ref, xb, inv_ref, nrm, ub, added, dn, g_ref,
     out_ref, grad_ref, ret_c_ref, ret_d_ref, gt,
     outb, gbuf, zeros, bias_row, gain_row, wqkv, wo, qkv, da, att, dproj,
     zero_sems, win_sems, out_sem,
@@ -413,7 +415,7 @@
     for b in range(kept):
         at = slice(b * patches, (b + 1) * patches)
         x = xb[b].astype(f32)
-        inv = lax.rsqrt(jnp.mean(x * x, axis=-1, keepdims=True) + EPS)
+        inv = jnp.concatenate([inv_ref[at, :]] * (ch // LANES), axis=1)
         t = d_nrm[at].astype(bf16).astype(f32) * gain
         along = jnp.mean(t * x, axis=-1, keepdims=True)
         dx = t * inv - x * (inv * inv * inv * along)
@@ -447,8 +449,9 @@
     ]
 
 
-def first_half(plan, scaled, ub, own):
-    tokens, ch = scaled.shape
+def first_half(plan, x, inv, ub, own):
+    kept, patches, ch = x.shape
+    tokens = kept * patches
     share = (own.shape[0],) + SHARE
     smem = pl.BlockSpec(memory_space=pltpu.SMEM)
     vmem = pl.BlockSpec(memory_space=pltpu.VMEM)
@@ -460,7 +463,7 @@
             jax.ShapeDtypeStruct((tokens, ch), f32),
             jax.ShapeDtypeStruct(share, bf16),
         ),
-        in_specs=[smem, vmem, vmem, vmem],
+        in_specs=[smem, vmem, vmem, vmem, vmem],
         out_specs=(vmem,) * 4,
         scratch_shapes=[
             pltpu.VMEM((1, 6 * HALF), f32),
@@ -468,12 +471,12 @@
             *half_scratch(tokens, ch),
         ],
         compiler_params=pltpu.CompilerParams(vmem_limit_bytes=VMEM_LIMIT),
-        cost_estimate=half_cost(tokens, tokens // KEPT, ch),
+        cost_estimate=half_cost(tokens, patches, ch),
         name="first_half",
-    )(plan, scaled, ub, own)
-
-
-def second_half(plan, x, nrm, ub, added, dn, oth, slots):
+    )(plan, x, inv, ub, own)
+
+
+def second_half(plan, x, inv, nrm, ub, added, dn, oth, slots):
     kept, patches, ch = x.shape
     tokens = kept * patches
     share = (oth.shape[0],) + SHARE
@@ -491,7 +494,7 @@
             jax.ShapeDtypeStruct(window, bf16),
             jax.ShapeDtypeStruct(share, f32),
         ),
-        in_specs=[smem] + [vmem] * 6,
+        in_specs=[smem] + [vmem] * 7,
         out_specs=(hbm,) * 4 + (vmem,),
         scratch_shapes=[
             held, held,
@@ -506,7 +509,7 @@
         compiler_params=pltpu.CompilerParams(vmem_limit_bytes=VMEM_LIMIT),
         cost_estimate=half_cost(tokens, patches, ch),
         name="second_half",
-    )(plan, x, nrm, ub, added, dn, oth)
+    )(plan, x, inv, nrm, ub, added, dn, oth)
 
 
 def finish_kernel(
@@ -567,13 +570,13 @@
     par_a, par_b, plan = make_plan(tables, activations, blob)
     arr_a = permute_dp(par_a, 2)
     arr_b = permute_dp(jnp.stack([par_b, arr_a[1]]), 1)
-    x, scaled, ub = arrange(plan, activations, arr_a, arr_b, cotangent)
-    own, x, scaled, ub = lax.optimization_barrier((own, x, scaled, ub))
+    x, inv, ub = arrange(plan, activations, arr_a, arr_b, cotangent)
+    own, x, inv, ub = lax.optimization_barrier((own, x, inv, ub))
     oth = swap_cores(own)
-    nrm, added, dn, gt_out = first_half(plan, scaled, ub, own)
+    nrm, added, dn, gt_out = first_half(plan, x, inv, ub, own)
     gt_in = swap_cores(gt_out)
     out, grad, ret_c, ret_d, gt = second_half(
-        plan, x, nrm, ub, added, dn, oth, activations.shape[0]
+        plan, x, inv, nrm, ub, added, dn, oth, activations.shape[0]
     )
     back_c = permute_dp(ret_c, -1)
     share = (gt + gt_in.astype(f32)).astype(bf16)

time: 111 us -> 109 us (0.982)
  local copies, waits for them, and re-layouts: 4.83 us -> 2.55 us
  starting transfers between devices: 30.5 us -> 32.2 us
    unnamed x16 -> x12, local copies, waits for them, and re-layouts: 4.81 us -> 2.53 us
  transfers between devices with their start and end apart: 8 -> 8, of which waited for: 4 -> 3; matrix products, arithmetic and copies ran while one was open for 1% -> 1% of each run, Pallas kernels for 15% -> 15%
where the time goes in v5:
time: 109 us; the launch traced here: 108 us
  starting transfers between devices  32.2 us (30%)
  blocking collectives  32.1 us (29%)
  Pallas kernels  20.1 us (18%)
  waiting for transfers between devices  18.2 us (17%)
  local copies, waits for them, and re-layouts  2.55 us (2%)
  other arithmetic  1.85 us (2%)
    all_gather x1, blocking collectives, shards(): parts = lax.all_gather(summed, 'dp', axis=0)  32.1 us
    ppermute x4, waiting for transfers between devices, permute_dp(): return lax.ppermute(array, 'dp', [(i, (i + by) % n) for i in range(n)])  18.2 us
    ppermute x4, starting transfers between devices, permute_dp(): return lax.ppermute(array, 'dp', [(i, (i + by) % n) for i in range(n)])  9.02 us
    ppermute x2, starting transfers between devices, swap_cores(): return lax.ppermute(array, 'dp', [(i, i ^ 1) for i in range(n)])  8.98 us
    all_to_all x1, starting transfers between devices, shards(): own = lax.all_to_all(blob, 'shard', 0, 0)  7.6 us
    all_to_all x1, starting transfers between devices, shards(): chunks = lax.all_to_all(share, 'shard', 0, 0)  6.64 us
    pallas_call x1, Pallas kernels, second_half(): pl.pallas_call(second_half_kernel, out_shape=(jax.ShapeDtypeStruct(x.shap...  6.18 us
    pallas_call x1, Pallas kernels, first_half(): pl.pallas_call(first_half_kernel, out_shape=(jax.ShapeDtypeStruct((tokens...  4.8 us
  transfers between devices with their start and end apart: 8, of which 3 were waited for; matrix products, arithmetic and copies ran while one was open for 1% of the time, Pallas kernels for 15%

profile of v5, /device:TPU:1, one launch (start us, length us, event | category | flops | bytes accessed | tf_op | source)
XLA Modules:
  0.0 107.8 jit_solution(7207139767009067115)
XLA Ops:
  0.6 2.5 %pack_weights.1.blob_ref = bf16[16,408,128]{2,1,0:T(8,128)(2,1)} custom-call(bf16[40,1920]{1,0:T(8,128)(2,1)} %wqkv_ref.1, bf16[1,120]{1,0:T(2,128)(2,1)} %bitcast.17, bf16[1,40]{1,0:T(2,128)(2,1)} %bitcast.18, bf16[40,640]{1,0:T(8,128)(2,1)} %bitcast.13), custom_call_target="tpu_custom_call" | custom-call | tf_op jit(solution)/shard_map/pack_weights/pallas_call | solution.py:103
  3.1 7.6 %all-to-all-start = ((bf16[16,408,128]{2,1,0:T(8,128)(2,1)}), bf16[16,408,128]{2,1,0:T(8,128)(2,1)S(1)}, u32[]{:S(2)}, u32[]{:S(2)}) async-start(bf16[16,408,128]{2,1,0:T(8,128)(2,1)} %pack_weights.1.blob_ref), calls=%async_computation | async-start | bytes 3342336 | tf_op jit(solution)/shard_map/all_to_all | solution.py:569
  10.7 0.0 copy-start
  10.7 0.0 copy-start.1
  10.8 2.9 %make_plan.1 = (bf16[2,64,640]{2,1,0:T(8,128)(2,1)}, bf16[64,640]{1,0:T(8,128)(2,1)}, s32[64]{0:T(128)}) custom-call(s32[10,1,32]{2,1,0:T(1,128)} %bitcast.14, s32[10,1,32]{2,1,0:T(1,128)} %bitcast.15, s32[10,1,32]{2,1,0:T(1,128)} %bitcast.16, bf16[10,64,640]{2,1,0:T(8,128)(2,1)} %act_ref.3, bf16[16,408,128]{2,1,0:T(8,128)(2,1)} %pack_weights.1.blob_ref), custom_call_target="tpu_custom_call" | custom-call | bytes 4194304 | tf_op jit(solution)/shard_map/make_plan/pallas_call | solution.py:166
  13.7 0.0 copy-start.3
  13.7 3.5 %collective-permute-start = (bf16[2,64,640]{2,1,0:T(8,128)(2,1)}, bf16[2,64,640]{2,1,0:T(8,128)(2,1)S(1)}, u32[]{:S(2)}, u32[]{:S(2)}) collective-permute-start(bf16[2,64,640]{2,1,0:T(8,128)(2,1)} %get-tuple-element.25), channel_id=1, source_target_pairs={{0,32},{16,48},{32,64},{48,80},{64,96},{80,112},{96,128},{112,144}... | collective-permute-start | bytes 491528 | tf_op jit(solution)/shard_map/ppermute | solution.py:26
  17.3 11.5 %collective-permute-done.arr_a_ref = bf16[2,64,640]{2,1,0:T(8,128)(2,1)S(1)} collective-permute-done((bf16[2,64,640]{2,1,0:T(8,128)(2,1)}, bf16[2,64,640]{2,1,0:T(8,128)(2,1)S(1)}, u32[]{:S(2)}, u32[]{:S(2)}) %collective-permute-start) | collective-permute-done | bytes 163872 | tf_op jit(solution)/shard_map/ppermute | solution.py:26
  28.8 0.9 pad_maximum_fusion
  29.7 0.0 collective-permute-start.1
  29.8 2.3 %collective-permute-done.1.arr_b_ref = bf16[2,64,640]{2,1,0:T(8,128)(2,1)S(1)} collective-permute-done((bf16[2,64,640]{2,1,0:T(8,128)(2,1)S(1)}, bf16[2,64,640]{2,1,0:T(8,128)(2,1)S(1)}, u32[]{:S(2)}, u32[]{:S(2)}) %collective-permute-start.1) | collective-permute-done | bytes 163872 | tf_op jit(solution)/shard_map/ppermute | solution.py:26
  32.0 0.0 copy-done
  32.0 0.0 copy-done.1
  32.0 0.0 copy-start.2
  32.0 0.7 copy-done.2
  32.7 2.3 %arrange_windows.1 = (bf16[7,64,640]{2,1,0:T(8,128)(2,1)S(1)}, f32[448,128]{1,0:T(8,128)S(1)}, bf16[448,640]{1,0:T(8,128)(2,1)S(1)}) custom-call(s32[64]{0:T(128)S(1)} %copy-done.2, bf16[10,64,640]{2,1,0:T(8,128)(2,1)S(1)} %copy-done, bf16[2,64,640]{2,1,0:T(8,128)(2,1)S(1)} %collective-permute-done.arr_a_ref, ...), custom_call_target="tpu_custom_call" | custom-call | bytes 8388608 | tf_op jit(solution)/shard_map/arrange_windows/pallas_call | solution.py:227
  35.0 0.0 copy-start.4
  35.0 0.8 copy-done.4
  35.8 0.0 all-to-all-done.g_ref
  35.8 7.1 %collective-permute-start.2 = (bf16[16,408,128]{2,1,0:T(8,128)(2,1)S(1)}, bf16[16,408,128]{2,1,0:T(8,128)(2,1)S(1)}, u32[]{:S(2)}, u32[]{:S(2)}) collective-permute-start(bf16[16,408,128]{2,1,0:T(8,128)(2,1)S(1)} %all-to-all-done.g_ref), channel_id=1, source_target_pairs={{0,16},{16,0},{32,48},{48,32},{64,80},{80,64},{96,112},{112,96},{1... | collective-permute-start | bytes 5013512 | tf_op jit(solution)/shard_map/ppermute | solution.py:31
  42.9 0.0 copy-done.3
  42.9 0.0 copy-start.5
  42.9 1.1 copy-done.5
  44.0 4.8 %first_half.1 = (bf16[448,640]{1,0:T(8,128)(2,1)S(1)}, f32[448,640]{1,0:T(8,128)S(1)}, f32[448,640]{1,0:T(8,128)S(1)}, bf16[16,104,128]{2,1,0:T(8,128)(2,1)S(1)}) custom-call(s32[64]{0:T(128)S(1)} %copy-done.3, bf16[7,64,640]{2,1,0:T(8,128)(2,1)S(1)} %get-tuple-element.30.xb, f32[448,128]{1,0:T(8,128)S(1)} %get-tuple-element.31.inv_ref, ...), custom_call_target="tpu_custom_call" | custom-call | flops 1761607680 | bytes 8388608 | tf_op jit(solution)/shard_map/first_half/pallas_call | solution.py:458
  48.8 1.9 %collective-permute-start.3 = (bf16[16,104,128]{2,1,0:T(8,128)(2,1)S(1)}, bf16[16,104,128]{2,1,0:T(8,128)(2,1)S(1)}, u32[]{:S(2)}, u32[]{:S(2)}) collective-permute-start(bf16[16,104,128]{2,1,0:T(8,128)(2,1)S(1)} %get-tuple-element.39), channel_id=1, source_target_pairs={{0,16},{16,0},{32,48},{48,32},{64,80},{80,64},{96,112},{112,96},{1... | collective-permute-start | bytes 1277960 | tf_op jit(solution)/shard_map/ppermute | solution.py:31
  50.7 0.0 collective-permute-done.2.g_ref
  50.7 6.2 %second_half.1 = (bf16[7,64,640]{2,1,0:T(8,128)(2,1)}, bf16[10,64,640]{2,1,0:T(8,128)(2,1)}, bf16[2,64,640]{2,1,0:T(8,128)(2,1)S(1)}, bf16[64,640]{1,0:T(8,128)(2,1)S(1)}, f32[16,104,128]{2,1,0:T(8,128)S(1)}) custom-call(s32[64]{0:T(128)S(1)} %copy-done.3, bf16[7,64,640]{2,1,0:T(8,128)(2,1)S(1)} %get-tuple-element.30.xb, ...), custom_call_target="tpu_custom_call" | custom-call | flops 1761607680 | bytes 8388608 | tf_op jit(solution)/shard_map/second_half/pallas_call | solution.py:488
  56.9 0.0 collective-permute-done.3
  56.9 0.9 add_convert_fusion
  57.8 6.6 %all-to-all-start.1 = ((bf16[16,104,128]{2,1,0:T(8,128)(2,1)}), bf16[16,104,128]{2,1,0:T(8,128)(2,1)S(1)}, u32[]{:S(2)}, u32[]{:S(2)}) async-start(bf16[16,104,128]{2,1,0:T(8,128)(2,1)} %add_convert_fusion), calls=%async_computation.1 | async-start | bytes 851968 | tf_op jit(solution)/shard_map/all_to_all | solution.py:583
  64.4 0.7 collective-permute-start.4
  65.1 4.4 %collective-permute-done.4.back_c_ref = bf16[2,64,640]{2,1,0:T(8,128)(2,1)S(1)} collective-permute-done((bf16[2,64,640]{2,1,0:T(8,128)(2,1)S(1)}, bf16[2,64,640]{2,1,0:T(8,128)(2,1)S(1)}, u32[]{:S(2)}, u32[]{:S(2)}) %collective-permute-start.4) | collective-permute-done | bytes 163872 | tf_op jit(solution)/shard_map/ppermute | solution.py:26
  69.5 4.8 %collective-permute-start.5 = (bf16[2,64,640]{2,1,0:T(8,128)(2,1)S(1)}, bf16[2,64,640]{2,1,0:T(8,128)(2,1)S(1)}, u32[]{:S(2)}, u32[]{:S(2)}) collective-permute-start(bf16[2,64,640]{2,1,0:T(8,128)(2,1)S(1)} %pad_maximum_fusion.1), channel_id=1, source_target_pairs={{0,480},{16,496},{32,0},{48,16},{64,32},{80,48},{96,64},{112,80},{... | collective-permute-start | bytes 491528 | tf_op jit(solution)/shard_map/ppermute | solution.py:26
  74.3 0.0 all-to-all-done.1
  74.3 0.1 reduce_sum.12
  74.4 32.1 %all-gather = bf16[3328,128]{1,0:T(8,128)(2,1)S(1)} all-gather(bf16[104,128]{1,0:T(8,128)(2,1)S(1)} %reduce_sum.12), channel_id=2, replica_groups=mesh['dp'=32,'shard'=16] {'dp'}, dimensions={0}, use_global_device_ids=true | all-gather | bytes 878592 | tf_op jit(solution)/shard_map/all_gather | solution.py:586
  106.5 0.0 collective-permute-done.5.back_d_ref
  106.5 1.4 %finish.1 = (bf16[10,64,640]{2,1,0:T(8,128)(2,1)}, f32[40,640]{1,0:T(8,128)}) custom-call(s32[64]{0:T(128)S(1)} %copy-done.3, bf16[32,104,128]{2,1,0:T(8,128)(2,1)S(1)} %bitcast.10, bf16[2,64,640]{2,1,0:T(8,128)(2,1)S(1)} %collective-permute-done.4.back_c_ref, ...), custom_call_target="tpu_custom_call", output_to_operand_aliasing={{0}: (4, {})} | custom-call | tf_op jit(solution)/shard_map/finish/pallas_call | solution.py:547
  (3 shorter events, 0.0 us)
Async XLA Ops:
  3.1 32.7 %all-to-all-start = ((bf16[16,408,128]{2,1,0:T(8,128)(2,1)}), bf16[16,408,128]{2,1,0:T(8,128)(2,1)S(1)}, u32[]{:S(2)}, u32[]{:S(2)}) async-start(bf16[16,408,128]{2,1,0:T(8,128)(2,1)} %pack_weights.1.blob_ref), calls=%async_computation | async-start | bytes 3342336 | tf_op jit(solution)/shard_map/all_to_all | solution.py:569
  10.7 21.3 %copy-start = (bf16[10,64,640]{2,1,0:T(8,128)(2,1)S(1)}, bf16[10,64,640]{2,1,0:T(8,128)(2,1)}, u32[]{:S(2)}) copy-start(bf16[10,64,640]{2,1,0:T(8,128)(2,1)} %act_ref.3) | copy-start | bytes 2457604
  10.7 21.3 %copy-start.1 = (bf16[7,64,640]{2,1,0:T(8,128)(2,1)S(1)}, bf16[7,64,640]{2,1,0:T(8,128)(2,1)}, u32[]{:S(2)}) copy-start(bf16[7,64,640]{2,1,0:T(8,128)(2,1)} %cot_ref.1) | copy-start | bytes 1720324
  13.7 29.2 %copy-start.3 = (s32[64]{0:T(128)S(1)}, s32[64]{0:T(128)}, u32[]{:S(2)}) copy-start(s32[64]{0:T(128)} %get-tuple-element.24.plan_ref) | copy-start | bytes 772
  13.7 15.1 %collective-permute-start = (bf16[2,64,640]{2,1,0:T(8,128)(2,1)}, bf16[2,64,640]{2,1,0:T(8,128)(2,1)S(1)}, u32[]{:S(2)}, u32[]{:S(2)}) collective-permute-start(bf16[2,64,640]{2,1,0:T(8,128)(2,1)} %get-tuple-element.25), channel_id=1, source_target_pairs={{0,32},{16,48},{32,64},{48,80},{64,96},{80,112},{96,128},{112,144}... | collective-permute-start | bytes 491528 | tf_op jit(solution)/shard_map/ppermute | solution.py:26
  29.7 2.3 %collective-permute-start.1 = (bf16[2,64,640]{2,1,0:T(8,128)(2,1)S(1)}, bf16[2,64,640]{2,1,0:T(8,128)(2,1)S(1)}, u32[]{:S(2)}, u32[]{:S(2)}) collective-permute-start(bf16[2,64,640]{2,1,0:T(8,128)(2,1)S(1)} %pad_maximum_fusion), channel_id=1, source_target_pairs={{0,16},{16,32},{32,48},{48,64},{64,80},{80,96},{96,112},{112,128},... | collective-permute-start | bytes 491528 | tf_op jit(solution)/shard_map/ppermute | solution.py:26
  32.0 0.7 copy-start.2
  35.0 0.8 copy-start.4
  35.8 14.9 %collective-permute-start.2 = (bf16[16,408,128]{2,1,0:T(8,128)(2,1)S(1)}, bf16[16,408,128]{2,1,0:T(8,128)(2,1)S(1)}, u32[]{:S(2)}, u32[]{:S(2)}) collective-permute-start(bf16[16,408,128]{2,1,0:T(8,128)(2,1)S(1)} %all-to-all-done.g_ref), channel_id=1, source_target_pairs={{0,16},{16,0},{32,48},{48,32},{64,80},{80,64},{96,112},{112,96},{1... | collective-permute-start | bytes 5013512 | tf_op jit(solution)/shard_map/ppermute | solution.py:31
  42.9 1.1 copy-start.5
  48.8 8.1 %collective-permute-start.3 = (bf16[16,104,128]{2,1,0:T(8,128)(2,1)S(1)}, bf16[16,104,128]{2,1,0:T(8,128)(2,1)S(1)}, u32[]{:S(2)}, u32[]{:S(2)}) collective-permute-start(bf16[16,104,128]{2,1,0:T(8,128)(2,1)S(1)} %get-tuple-element.39), channel_id=1, source_target_pairs={{0,16},{16,0},{32,48},{48,32},{64,80},{80,64},{96,112},{112,96},{1... | collective-permute-start | bytes 1277960 | tf_op jit(solution)/shard_map/ppermute | solution.py:31
  57.8 16.6 %all-to-all-start.1 = ((bf16[16,104,128]{2,1,0:T(8,128)(2,1)}), bf16[16,104,128]{2,1,0:T(8,128)(2,1)S(1)}, u32[]{:S(2)}, u32[]{:S(2)}) async-start(bf16[16,104,128]{2,1,0:T(8,128)(2,1)} %add_convert_fusion), calls=%async_computation.1 | async-start | bytes 851968 | tf_op jit(solution)/shard_map/all_to_all | solution.py:583
  64.4 5.1 %collective-permute-start.4 = (bf16[2,64,640]{2,1,0:T(8,128)(2,1)S(1)}, bf16[2,64,640]{2,1,0:T(8,128)(2,1)S(1)}, u32[]{:S(2)}, u32[]{:S(2)}) collective-permute-start(bf16[2,64,640]{2,1,0:T(8,128)(2,1)S(1)} %get-tuple-element.40), channel_id=1, source_target_pairs={{0,496},{16,0},{32,16},{48,32},{64,48},{80,64},{96,80},{112,96},{1... | collective-permute-start | bytes 491528 | tf_op jit(solution)/shard_map/ppermute | solution.py:26
  69.5 37.0 %collective-permute-start.5 = (bf16[2,64,640]{2,1,0:T(8,128)(2,1)S(1)}, bf16[2,64,640]{2,1,0:T(8,128)(2,1)S(1)}, u32[]{:S(2)}, u32[]{:S(2)}) collective-permute-start(bf16[2,64,640]{2,1,0:T(8,128)(2,1)S(1)} %pad_maximum_fusion.1), channel_id=1, source_target_pairs={{0,480},{16,496},{32,0},{48,16},{64,32},{80,48},{96,64},{112,80},{... | collective-permute-start | bytes 491528 | tf_op jit(solution)/shard_map/ppermute | solution.py:26

commit v6 on v5

--- a/solution.py
+++ b/solution.py
@@ -362,7 +362,7 @@
 
 def second_half_kernel(
     plan_ref, xb, inv_ref, nrm, ub, added, dn, g_ref,
-    out_ref, grad_ref, ret_c_ref, ret_d_ref, gt,
+    out_ref, grad_ref, ret_1_ref, ret_2_ref, ret_3_ref, gt,
     outb, gbuf, zeros, bias_row, gain_row, wqkv, wo, qkv, da, att, dproj,
     zero_sems, win_sems, out_sem,
 ):
@@ -383,7 +383,7 @@
         def _(s=s):
             zero_copy(s).start()
 
-    returned = [ret_c_ref.at[0], ret_d_ref, ret_c_ref.at[1]]
+    returned = [ret_1_ref, ret_2_ref, ret_3_ref]
 
     def ready(b):
         @pl.when((code[b] >= 0) & (code[b] < slots))
@@ -490,12 +490,13 @@
         out_shape=(
             jax.ShapeDtypeStruct(x.shape, bf16),
             jax.ShapeDtypeStruct((slots,) + window, bf16),
-            jax.ShapeDtypeStruct((2,) + window, bf16),
+            jax.ShapeDtypeStruct(window, bf16),
+            jax.ShapeDtypeStruct(window, bf16),
             jax.ShapeDtypeStruct(window, bf16),
             jax.ShapeDtypeStruct(share, f32),
         ),
         in_specs=[smem] + [vmem] * 7,
-        out_specs=(hbm,) * 4 + (vmem,),
+        out_specs=(hbm,) * 5 + (vmem,),
         scratch_shapes=[
             held, held,
             pltpu.VMEM(window, bf16),
@@ -513,9 +514,9 @@
 
 
 def finish_kernel(
-    plan_ref, parts_ref, back_c_ref, back_d_ref, grad_in_ref, grad_ref, total_ref, sems
+    plan_ref, parts_ref, back_1_ref, back_2_ref, back_3_ref, grad_in_ref, grad_ref, total_ref, sems
 ):
-    back = [back_c_ref.at[0], back_d_ref.at[0], back_d_ref.at[1]]
+    back = [back_1_ref, back_2_ref, back_3_ref]
     copies = []
     for d in range(MOVES):
         s = plan_ref[LEAVES + d + 1]
@@ -540,7 +541,7 @@
             cp.wait()
 
 
-def finish(plan, parts, back_c, back_d, grad, rows):
+def finish(plan, parts, back, grad, rows):
     smem = pl.BlockSpec(memory_space=pltpu.SMEM)
     vmem = pl.BlockSpec(memory_space=pltpu.VMEM)
     hbm = pl.BlockSpec(memory_space=pl.ANY)
@@ -550,13 +551,13 @@
             jax.ShapeDtypeStruct(grad.shape, bf16),
             jax.ShapeDtypeStruct((rows, 2 * HALF), f32),
         ),
-        in_specs=[smem, vmem, vmem, vmem, hbm],
+        in_specs=[smem, vmem, vmem, vmem, vmem, hbm],
         out_specs=(hbm, vmem),
         scratch_shapes=[pltpu.SemaphoreType.DMA((MOVES,))],
-        input_output_aliases={4: 0},
+        input_output_aliases={5: 0},
         compiler_params=pltpu.CompilerParams(vmem_limit_bytes=VMEM_LIMIT),
         name="finish",
-    )(plan, parts, back_c, back_d, grad)
+    )(plan, parts, *back, grad)
 
 
 def shards(
@@ -575,16 +576,15 @@
     oth = swap_cores(own)
     nrm, added, dn, gt_out = first_half(plan, x, inv, ub, own)
     gt_in = swap_cores(gt_out)
-    out, grad, ret_c, ret_d, gt = second_half(
+    out, grad, *returned, gt = second_half(
         plan, x, inv, nrm, ub, added, dn, oth, activations.shape[0]
     )
-    back_c = permute_dp(ret_c, -1)
+    back = [permute_dp(r, -d) for d, r in enumerate(returned, 1)]
     share = (gt + gt_in.astype(f32)).astype(bf16)
     chunks = lax.all_to_all(share, "shard", 0, 0)
     summed = jnp.sum(chunks.astype(f32), axis=0).astype(bf16)
-    back_d = permute_dp(jnp.stack([ret_d, back_c[1]]), -2)
     parts = lax.all_gather(summed, "dp", axis=0)
-    grad_input, total = finish(plan, parts, back_c, back_d, grad, rows)
+    grad_input, total = finish(plan, parts, back, grad, rows)
     return (out, grad_input, total.T)
 
 

time: 109 us -> 109 us (level)
  waiting for transfers between devices: 18.2 us -> 14.7 us
  starting transfers between devices: 32.2 us -> 34.7 us
  blocking collectives: 32.1 us -> 33.9 us
    ppermute x4 -> x5, waiting for transfers between devices: 18.2 us -> 13.9 us  [permute_dp(): return lax.ppermute(array, 'dp', [(i, (i + by) % n) for i in range(n)])]
    ppermute x4 -> x5, starting transfers between devices: 9.02 us -> 11.2 us  [permute_dp(): return lax.ppermute(array, 'dp', [(i, (i + by) % n) for i in range(n)])]
    all_gather x1, blocking collectives: 32.1 us -> 33.9 us  [shards(): parts = lax.all_gather(summed, 'dp', axis=0)]
  transfers between devices with their start and end apart: 8 -> 9, of which waited for: 3 -> 3; matrix products, arithmetic and copies ran while one was open for 1% -> 1% of each run, Pallas kernels for 15% -> 15%
where the time goes in v6:
time: 109 us; the launch traced here: 108 us
  starting transfers between devices  34.7 us (32%)
  blocking collectives  33.9 us (31%)
  Pallas kernels  20 us (18%)
  waiting for transfers between devices  14.7 us (13%)
  local copies, waits for them, and re-layouts  2.54 us (2%)
  other arithmetic  1.82 us (2%)
    all_gather x1, blocking collectives, shards(): parts = lax.all_gather(summed, 'dp', axis=0)  33.9 us
    ppermute x5, waiting for transfers between devices, permute_dp(): return lax.ppermute(array, 'dp', [(i, (i + by) % n) for i in range(n)])  13.9 us
    ppermute x5, starting transfers between devices, permute_dp(): return lax.ppermute(array, 'dp', [(i, (i + by) % n) for i in range(n)])  11.2 us
    ppermute x2, starting transfers between devices, swap_cores(): return lax.ppermute(array, 'dp', [(i, i ^ 1) for i in range(n)])  8.61 us
    all_to_all x1, starting transfers between devices, shards(): own = lax.all_to_all(blob, 'shard', 0, 0)  7.6 us
    all_to_all x1, starting transfers between devices, shards(): chunks = lax.all_to_all(share, 'shard', 0, 0)  7.34 us
    pallas_call x1, Pallas kernels, second_half(): pl.pallas_call(second_half_kernel, out_shape=(jax.ShapeDtypeStruct(x.shap...  6.06 us
    pallas_call x1, Pallas kernels, first_half(): pl.pallas_call(first_half_kernel, out_shape=(jax.ShapeDtypeStruct((tokens...  4.84 us
  transfers between devices with their start and end apart: 9, of which 3 were waited for; matrix products, arithmetic and copies ran while one was open for 1% of the time, Pallas kernels for 15%

profile of v6, /device:TPU:1, one launch (start us, length us, event | category | flops | bytes accessed | tf_op | source)
XLA Modules:
  0.0 108.4 jit_solution(12504800487019999383)
XLA Ops:
  0.6 2.5 %pack_weights.1.blob_ref = bf16[16,408,128]{2,1,0:T(8,128)(2,1)} custom-call(bf16[40,1920]{1,0:T(8,128)(2,1)} %wqkv_ref.1, bf16[1,120]{1,0:T(2,128)(2,1)} %bitcast.15, bf16[1,40]{1,0:T(2,128)(2,1)} %bitcast.16, bf16[40,640]{1,0:T(8,128)(2,1)} %bitcast.11), custom_call_target="tpu_custom_call" | custom-call | tf_op jit(solution)/shard_map/pack_weights/pallas_call | solution.py:103
  3.1 7.6 %all-to-all-start = ((bf16[16,408,128]{2,1,0:T(8,128)(2,1)}), bf16[16,408,128]{2,1,0:T(8,128)(2,1)S(1)}, u32[]{:S(2)}, u32[]{:S(2)}) async-start(bf16[16,408,128]{2,1,0:T(8,128)(2,1)} %pack_weights.1.blob_ref), calls=%async_computation | async-start | bytes 3342336 | tf_op jit(solution)/shard_map/all_to_all | solution.py:570
  10.7 0.0 copy-start
  10.8 0.0 copy-start.1
  10.8 2.9 %make_plan.1 = (bf16[2,64,640]{2,1,0:T(8,128)(2,1)}, bf16[64,640]{1,0:T(8,128)(2,1)}, s32[64]{0:T(128)}) custom-call(s32[10,1,32]{2,1,0:T(1,128)} %bitcast.12, s32[10,1,32]{2,1,0:T(1,128)} %bitcast.13, s32[10,1,32]{2,1,0:T(1,128)} %bitcast.14, bf16[10,64,640]{2,1,0:T(8,128)(2,1)} %act_ref.3, bf16[16,408,128]{2,1,0:T(8,128)(2,1)} %pack_weights.1.blob_ref), custom_call_target="tpu_custom_call" | custom-call | bytes 4194304 | tf_op jit(solution)/shard_map/make_plan/pallas_call | solution.py:166
  13.7 0.0 copy-start.3
  13.7 3.5 %collective-permute-start = (bf16[2,64,640]{2,1,0:T(8,128)(2,1)}, bf16[2,64,640]{2,1,0:T(8,128)(2,1)S(1)}, u32[]{:S(2)}, u32[]{:S(2)}) collective-permute-start(bf16[2,64,640]{2,1,0:T(8,128)(2,1)} %get-tuple-element.26), channel_id=1, source_target_pairs={{0,32},{16,48},{32,64},{48,80},{64,96},{80,112},{96,128},{112,144}... | collective-permute-start | bytes 491528 | tf_op jit(solution)/shard_map/ppermute | solution.py:26
  17.3 11.6 %collective-permute-done.arr_a_ref = bf16[2,64,640]{2,1,0:T(8,128)(2,1)S(1)} collective-permute-done((bf16[2,64,640]{2,1,0:T(8,128)(2,1)}, bf16[2,64,640]{2,1,0:T(8,128)(2,1)S(1)}, u32[]{:S(2)}, u32[]{:S(2)}) %collective-permute-start) | collective-permute-done | bytes 163872 | tf_op jit(solution)/shard_map/ppermute | solution.py:26
  28.9 0.9 pad_maximum_fusion
  29.8 0.0 collective-permute-start.1
  29.8 2.3 %collective-permute-done.1.arr_b_ref = bf16[2,64,640]{2,1,0:T(8,128)(2,1)S(1)} collective-permute-done((bf16[2,64,640]{2,1,0:T(8,128)(2,1)S(1)}, bf16[2,64,640]{2,1,0:T(8,128)(2,1)S(1)}, u32[]{:S(2)}, u32[]{:S(2)}) %collective-permute-start.1) | collective-permute-done | bytes 163872 | tf_op jit(solution)/shard_map/ppermute | solution.py:26
  32.1 0.0 copy-done
  32.1 0.0 copy-done.1
  32.1 0.0 copy-start.2
  32.1 0.7 copy-done.2
  32.8 2.2 %arrange_windows.1 = (bf16[7,64,640]{2,1,0:T(8,128)(2,1)S(1)}, f32[448,128]{1,0:T(8,128)S(1)}, bf16[448,640]{1,0:T(8,128)(2,1)S(1)}) custom-call(s32[64]{0:T(128)S(1)} %copy-done.2, bf16[10,64,640]{2,1,0:T(8,128)(2,1)S(1)} %copy-done, bf16[2,64,640]{2,1,0:T(8,128)(2,1)S(1)} %collective-permute-done.arr_a_ref, ...), custom_call_target="tpu_custom_call" | custom-call | bytes 8388608 | tf_op jit(solution)/shard_map/arrange_windows/pallas_call | solution.py:227
  35.0 0.0 copy-start.4
  35.0 0.8 copy-done.4
  35.8 0.0 all-to-all-done.g_ref
  35.8 6.7 %collective-permute-start.2 = (bf16[16,408,128]{2,1,0:T(8,128)(2,1)S(1)}, bf16[16,408,128]{2,1,0:T(8,128)(2,1)S(1)}, u32[]{:S(2)}, u32[]{:S(2)}) collective-permute-start(bf16[16,408,128]{2,1,0:T(8,128)(2,1)S(1)} %all-to-all-done.g_ref), channel_id=1, source_target_pairs={{0,16},{16,0},{32,48},{48,32},{64,80},{80,64},{96,112},{112,96},{1... | collective-permute-start | bytes 5013512 | tf_op jit(solution)/shard_map/ppermute | solution.py:31
  42.5 0.0 copy-done.3
  42.5 0.0 copy-start.5
  42.5 1.1 copy-done.5
  43.6 4.8 %first_half.1 = (bf16[448,640]{1,0:T(8,128)(2,1)S(1)}, f32[448,640]{1,0:T(8,128)S(1)}, f32[448,640]{1,0:T(8,128)S(1)}, bf16[16,104,128]{2,1,0:T(8,128)(2,1)S(1)}) custom-call(s32[64]{0:T(128)S(1)} %copy-done.3, bf16[7,64,640]{2,1,0:T(8,128)(2,1)S(1)} %get-tuple-element.31.xb, f32[448,128]{1,0:T(8,128)S(1)} %get-tuple-element.32.inv_ref, ...), custom_call_target="tpu_custom_call" | custom-call | flops 1761607680 | bytes 8388608 | tf_op jit(solution)/shard_map/first_half/pallas_call | solution.py:458
  48.4 1.9 %collective-permute-start.3 = (bf16[16,104,128]{2,1,0:T(8,128)(2,1)S(1)}, bf16[16,104,128]{2,1,0:T(8,128)(2,1)S(1)}, u32[]{:S(2)}, u32[]{:S(2)}) collective-permute-start(bf16[16,104,128]{2,1,0:T(8,128)(2,1)S(1)} %get-tuple-element.40), channel_id=1, source_target_pairs={{0,16},{16,0},{32,48},{48,32},{64,80},{80,64},{96,112},{112,96},{1... | collective-permute-start | bytes 1277960 | tf_op jit(solution)/shard_map/ppermute | solution.py:31
  50.4 0.0 collective-permute-done.2.g_ref
  50.4 6.1 %second_half.1 = (bf16[7,64,640]{2,1,0:T(8,128)(2,1)}, bf16[10,64,640]{2,1,0:T(8,128)(2,1)}, bf16[64,640]{1,0:T(8,128)(2,1)S(1)}, bf16[64,640]{1,0:T(8,128)(2,1)...) custom-call(s32[64]{0:T(128)S(1)} %copy-done.3, bf16[7,64,640]{2,1,0:T(8,128)(2,1)S(1)} %get-tuple-element.31.xb, ...), custom_call_target="tpu_custom_call" | custom-call | flops 1761607680 | bytes 8388608 | tf_op jit(solution)/shard_map/second_half/pallas_call | solution.py:488
  56.5 0.0 collective-permute-done.3
  56.5 0.8 add_convert_fusion
  57.3 7.3 %all-to-all-start.1 = ((bf16[16,104,128]{2,1,0:T(8,128)(2,1)}), bf16[16,104,128]{2,1,0:T(8,128)(2,1)S(1)}, u32[]{:S(2)}, u32[]{:S(2)}) async-start(bf16[16,104,128]{2,1,0:T(8,128)(2,1)} %add_convert_fusion), calls=%async_computation.1 | async-start | bytes 851968 | tf_op jit(solution)/shard_map/all_to_all | solution.py:584
  64.7 0.9 collective-permute-start.4
  65.6 3.5 %collective-permute-start.5 = (bf16[64,640]{1,0:T(8,128)(2,1)S(1)}, bf16[64,640]{1,0:T(8,128)(2,1)S(1)}, u32[]{:S(2)}, u32[]{:S(2)}) collective-permute-start(bf16[64,640]{1,0:T(8,128)(2,1)S(1)} %get-tuple-element.42), channel_id=1, source_target_pairs={{0,480},{16,496},{32,0},{48,16},{64,32},{80,48},{96,64},{112,80},{... | collective-permute-start | bytes 245768 | tf_op jit(solution)/shard_map/ppermute | solution.py:26
  69.1 3.1 %collective-permute-start.6 = (bf16[64,640]{1,0:T(8,128)(2,1)S(1)}, bf16[64,640]{1,0:T(8,128)(2,1)S(1)}, u32[]{:S(2)}, u32[]{:S(2)}) collective-permute-start(bf16[64,640]{1,0:T(8,128)(2,1)S(1)} %get-tuple-element.43), channel_id=1, source_target_pairs={{0,464},{16,480},{32,496},{48,0},{64,16},{80,32},{96,48},{112,64},... | collective-permute-start | bytes 245768 | tf_op jit(solution)/shard_map/ppermute | solution.py:26
  72.3 0.8 all-to-all-done.1
  73.1 0.1 reduce_sum.12
  73.2 33.9 %all-gather = bf16[3328,128]{1,0:T(8,128)(2,1)S(1)} all-gather(bf16[104,128]{1,0:T(8,128)(2,1)S(1)} %reduce_sum.12), channel_id=2, replica_groups=mesh['dp'=32,'shard'=16] {'dp'}, dimensions={0}, use_global_device_ids=true | all-gather | bytes 878592 | tf_op jit(solution)/shard_map/all_gather | solution.py:586
  107.1 0.0 collective-permute-done.4.back_1_ref
  107.1 0.0 collective-permute-done.5.back_2_ref
  107.1 0.0 collective-permute-done.6.back_3_ref
  107.1 1.4 %finish.1 = (bf16[10,64,640]{2,1,0:T(8,128)(2,1)}, f32[40,640]{1,0:T(8,128)}) custom-call(s32[64]{0:T(128)S(1)} %copy-done.3, bf16[32,104,128]{2,1,0:T(8,128)(2,1)S(1)} %bitcast.9, bf16[64,640]{1,0:T(8,128)(2,1)S(1)} %collective-permute-done.4.back_1_ref, bf16[64,640]{1,0:T(8,128)(2,1)S(1)} %collective-permute-done.5.back_2_ref, ...), custom_call_target="tpu_custom_call", output_to_operand_aliasing={{0}: (5, {})} | custom-call | tf_op jit(solution)/shard_map/finish/pallas_call | solution.py:548
  (1 shorter events, 0.0 us)
Async XLA Ops:
  3.1 32.7 %all-to-all-start = ((bf16[16,408,128]{2,1,0:T(8,128)(2,1)}), bf16[16,408,128]{2,1,0:T(8,128)(2,1)S(1)}, u32[]{:S(2)}, u32[]{:S(2)}) async-start(bf16[16,408,128]{2,1,0:T(8,128)(2,1)} %pack_weights.1.blob_ref), calls=%async_computation | async-start | bytes 3342336 | tf_op jit(solution)/shard_map/all_to_all | solution.py:570
  10.7 21.4 %copy-start = (bf16[10,64,640]{2,1,0:T(8,128)(2,1)S(1)}, bf16[10,64,640]{2,1,0:T(8,128)(2,1)}, u32[]{:S(2)}) copy-start(bf16[10,64,640]{2,1,0:T(8,128)(2,1)} %act_ref.3) | copy-start | bytes 2457604
  10.8 21.4 %copy-start.1 = (bf16[7,64,640]{2,1,0:T(8,128)(2,1)S(1)}, bf16[7,64,640]{2,1,0:T(8,128)(2,1)}, u32[]{:S(2)}) copy-start(bf16[7,64,640]{2,1,0:T(8,128)(2,1)} %cot_ref.1) | copy-start | bytes 1720324
  13.7 28.8 %copy-start.3 = (s32[64]{0:T(128)S(1)}, s32[64]{0:T(128)}, u32[]{:S(2)}) copy-start(s32[64]{0:T(128)} %get-tuple-element.25.plan_ref) | copy-start | bytes 772
  13.7 15.2 %collective-permute-start = (bf16[2,64,640]{2,1,0:T(8,128)(2,1)}, bf16[2,64,640]{2,1,0:T(8,128)(2,1)S(1)}, u32[]{:S(2)}, u32[]{:S(2)}) collective-permute-start(bf16[2,64,640]{2,1,0:T(8,128)(2,1)} %get-tuple-element.26), channel_id=1, source_target_pairs={{0,32},{16,48},{32,64},{48,80},{64,96},{80,112},{96,128},{112,144}... | collective-permute-start | bytes 491528 | tf_op jit(solution)/shard_map/ppermute | solution.py:26
  29.8 2.3 %collective-permute-start.1 = (bf16[2,64,640]{2,1,0:T(8,128)(2,1)S(1)}, bf16[2,64,640]{2,1,0:T(8,128)(2,1)S(1)}, u32[]{:S(2)}, u32[]{:S(2)}) collective-permute-start(bf16[2,64,640]{2,1,0:T(8,128)(2,1)S(1)} %pad_maximum_fusion), channel_id=1, source_target_pairs={{0,16},{16,32},{32,48},{48,64},{64,80},{80,96},{96,112},{112,128},... | collective-permute-start | bytes 491528 | tf_op jit(solution)/shard_map/ppermute | solution.py:26
  32.1 0.7 copy-start.2
  35.0 0.8 copy-start.4
  35.8 14.6 %collective-permute-start.2 = (bf16[16,408,128]{2,1,0:T(8,128)(2,1)S(1)}, bf16[16,408,128]{2,1,0:T(8,128)(2,1)S(1)}, u32[]{:S(2)}, u32[]{:S(2)}) collective-permute-start(bf16[16,408,128]{2,1,0:T(8,128)(2,1)S(1)} %all-to-all-done.g_ref), channel_id=1, source_target_pairs={{0,16},{16,0},{32,48},{48,32},{64,80},{80,64},{96,112},{112,96},{1... | collective-permute-start | bytes 5013512 | tf_op jit(solution)/shard_map/ppermute | solution.py:31
  42.5 1.1 copy-start.5
  48.4 8.0 %collective-permute-start.3 = (bf16[16,104,128]{2,1,0:T(8,128)(2,1)S(1)}, bf16[16,104,128]{2,1,0:T(8,128)(2,1)S(1)}, u32[]{:S(2)}, u32[]{:S(2)}) collective-permute-start(bf16[16,104,128]{2,1,0:T(8,128)(2,1)S(1)} %get-tuple-element.40), channel_id=1, source_target_pairs={{0,16},{16,0},{32,48},{48,32},{64,80},{80,64},{96,112},{112,96},{1... | collective-permute-start | bytes 1277960 | tf_op jit(solution)/shard_map/ppermute | solution.py:31
  57.3 15.8 %all-to-all-start.1 = ((bf16[16,104,128]{2,1,0:T(8,128)(2,1)}), bf16[16,104,128]{2,1,0:T(8,128)(2,1)S(1)}, u32[]{:S(2)}, u32[]{:S(2)}) async-start(bf16[16,104,128]{2,1,0:T(8,128)(2,1)} %add_convert_fusion), calls=%async_computation.1 | async-start | bytes 851968 | tf_op jit(solution)/shard_map/all_to_all | solution.py:584
  64.7 42.4 %collective-permute-start.4 = (bf16[64,640]{1,0:T(8,128)(2,1)S(1)}, bf16[64,640]{1,0:T(8,128)(2,1)S(1)}, u32[]{:S(2)}, u32[]{:S(2)}) collective-permute-start(bf16[64,640]{1,0:T(8,128)(2,1)S(1)} %get-tuple-element.41), channel_id=1, source_target_pairs={{0,496},{16,0},{32,16},{48,32},{64,48},{80,64},{96,80},{112,96},{1... | collective-permute-start | bytes 245768 | tf_op jit(solution)/shard_map/ppermute | solution.py:26
  65.6 41.5 %collective-permute-start.5 = (bf16[64,640]{1,0:T(8,128)(2,1)S(1)}, bf16[64,640]{1,0:T(8,128)(2,1)S(1)}, u32[]{:S(2)}, u32[]{:S(2)}) collective-permute-start(bf16[64,640]{1,0:T(8,128)(2,1)S(1)} %get-tuple-element.42), channel_id=1, source_target_pairs={{0,480},{16,496},{32,0},{48,16},{64,32},{80,48},{96,64},{112,80},{... | collective-permute-start | bytes 245768 | tf_op jit(solution)/shard_map/ppermute | solution.py:26
  69.1 37.9 %collective-permute-start.6 = (bf16[64,640]{1,0:T(8,128)(2,1)S(1)}, bf16[64,640]{1,0:T(8,128)(2,1)S(1)}, u32[]{:S(2)}, u32[]{:S(2)}) collective-permute-start(bf16[64,640]{1,0:T(8,128)(2,1)S(1)} %get-tuple-element.43), channel_id=1, source_target_pairs={{0,464},{16,480},{32,496},{48,0},{64,16},{80,32},{96,48},{112,64},... | collective-permute-start | bytes 245768 | tf_op jit(solution)/shard_map/ppermute | solution.py:26
